TPU v7x, 256 devices: a whole 4x4x8 slice. The times are simulated.
256 devices in a mesh: tensor: 8 (over z_lo, y), grow: 4 (over x), gcol: 8 (over z_hi, core).
Axes of the slice: x: 4, y: 4, z: 8 (z_hi: 4, z_lo: 2; z = z_hi * 2 + z_lo), core: 2. Of those that a mesh axis runs over, the one named last changes fastest.
Arguments:
- hidden: bfloat16 [2048, 8192], P(None, 'grow'), may hold values from -6 to 6
- gain: float32 [8192], P('grow'), may hold values from 0.5 to 2
- gate_weight: bfloat16 [8192, 14336], P('grow', ('tensor', 'gcol')), may hold values from -0.0625 to 0.0625
- up_weight: bfloat16 [8192, 14336], P('grow', ('tensor', 'gcol')), may hold values from -0.0625 to 0.0625
Outputs:
- moments: float32 [14336, 8, 1792], P(('tensor', 'grow'), 'gcol')
All inputs are finite; a program needn't handle non-finite values.
Results may differ from a plain program's by a relative error of at most 0.0065.
Values may be sent and summed in bfloat16 or wider, within the bound.
No kernel may reach another device: no remote copies, remote signals or barrier semaphores. Data moves between devices by JAX's collectives and lax.ppermute only.
A program may use at most 128 MiB of HBM per device.

v0:
```python
import jax
import jax.numpy as jnp
from jax import lax
from jax.sharding import PartitionSpec as P

D = 8192


EPS = 1e-05


def shards(hidden, gain, gate_weight, up_weight):
    values = hidden.astype(jnp.float32)
    local_sums = jnp.sum(values * values, axis=1)
    total = lax.psum(local_sums, "grow")
    scale = lax.rsqrt(total / D + EPS)
    normed = (values * gain[None, :] * scale[:, None]).astype(jnp.bfloat16)
    width = gate_weight.shape[1]
    n_tensor = lax.axis_size("tensor")
    n_grow = lax.axis_size("grow")
    n_gcol = lax.axis_size("gcol")
    local_tok = normed.shape[0] // n_grow
    gate_part = jnp.dot(normed, gate_weight, preferred_element_type=jnp.float32)
    up_part = jnp.dot(normed, up_weight, preferred_element_type=jnp.float32)
    mixed = lax.psum_scatter(
        jnp.concatenate([gate_part, up_part], axis=1), "grow", scatter_dimension=0, tiled=True
    )
    keys = (jax.nn.silu(mixed[:, :width]) * mixed[:, width:]).astype(jnp.bfloat16)
    columns = lax.all_gather(
        keys.reshape(1, local_tok, width), ("tensor", "grow"), axis=0, tiled=True
    )
    columns = columns.reshape(n_tensor, n_grow, local_tok, width)
    row_width = width * n_gcol // n_grow
    token_count = local_tok * n_grow
    every = lax.all_gather(keys.reshape(local_tok, 1, width), ("grow", "gcol"), axis=1, tiled=True)
    every = every.reshape(local_tok, n_grow, n_gcol * width)
    row_keys = lax.dynamic_slice_in_dim(every, lax.axis_index("grow") * row_width, row_width, 2)
    tile = jnp.einsum("sra,trsj->atj", row_keys, columns, preferred_element_type=jnp.float32)
    tile = tile / token_count
    return tile.reshape(row_width, 1, n_tensor * width)


def solution(mesh):
    in_specs = (
        P(None, "grow"),
        P("grow"),
        P("grow", ("tensor", "gcol")),
        P("grow", ("tensor", "gcol")),
    )
    out_specs = P(("tensor", "grow"), "gcol", None)
    return jax.shard_map(shards, mesh=mesh, in_specs=in_specs, out_specs=out_specs, check_vma=False)
```

profile of v0, /device:TPU:1, one launch (start us, length us, event | category | flops | bytes accessed | tf_op | source)
XLA Modules:
  0.0 356.6 jit_solution(904383456335328473)
XLA Ops:
  6.5 0.0 copy-start
  6.5 0.0 copy-start.3
  6.5 0.0 reduce-scatter.2.cloned.1.call-start
  6.5 5.2 %fusion.2 = f32[2048]{0:T(1024)S(1)} fusion(bf16[2048,2048]{1,0:T(8,128)(2,1)} %param.4), kind=kLoop, calls=%fused_computation.4 | loop fusion | flops 12580864 | bytes 8396800 | tf_op jit(solution)/shard_map/reduce_sum | solution.py:14
  11.7 9.4 %psum.7 = f32[2048]{0:T(1024)S(1)} all-reduce(f32[2048]{0:T(1024)S(1)} %fusion.2), channel_id=1, replica_groups=mesh['tensor'=8,'grow'=4,'gcol'=8] {'grow'}, use_global_device_ids=true, to_apply=%region_1.0 | all-reduce | flops 2048 | bytes 16384 | tf_op jit(solution)/shard_map/psum | solution.py:15
  21.1 0.0 copy-done
  21.1 0.0 copy-done.3
  21.2 0.0 copy-start.1
  21.2 0.0 copy-start.2
  21.2 6.3 %fusion.5 = f32[2048,224]{0,1:T(8,128)S(1)} fusion(bf16[2048,224]{0,1:T(8,128)(2,1)S(1)} %copy-done, bf16[2048,2048]{1,0:T(8,128)(2,1)} %param.4, f32[2048]{0:T(1024)S(1)} %add_rsqrt_fusion, f32[2048]{0:T(1024)S(1)} %copy-done.3), kind=kOutput, calls=%fused_computation.9 | convolution fusion | flops 1895825408 | bytes 11157504 | tf_op jit(solution)/shard_map/dot_general | solution.py:24
  27.5 0.0 copy-done.1
  27.5 0.0 copy-done.2
  27.5 3.0 fusion.7
  30.5 2.2 pad_maximum_fusion
  32.8 0.0 reduce-scatter.2.cloned.1.call-update
  32.8 0.0 all-gather.7.cloned.1.call-start
  32.8 48.0 %reduce-scatter.2.cloned.1.call-done = f32[512,448]{0,1:T(8,128)} async-done(((f32[2048,448]{0,1:T(8,128)}), f32[512,448]{0,1:T(8,128)}) %reduce-scatter.2.cloned.1.call-update) | async-done | bytes 917520 | tf_op jit(solution)/shard_map/reduce_scatter | solution.py:25
  80.9 2.0 fusion.13
  82.9 0.0 all-gather.7.cloned.1.call-update
  82.9 0.2 all-gather.5.cloned.1.call-start
  83.1 0.5 all-gather.5.cloned.1.call-update
  83.6 148.5 %all-gather.7.cloned.1.call-done = bf16[16384,224]{0,1:T(8,128)(2,1)} async-done(((bf16[512,224]{0,1:T(8,128)(2,1)}), bf16[16384,224]{0,1:T(8,128)(2,1)}) %all-gather.7.cloned.1.call-update) | async-done | bytes 7340048 | tf_op jit(solution)/shard_map/all_gather | solution.py:29
  232.1 12.8 %reshape.20 = bf16[8,4,512,224]{2,1,0,3:T(4,128)(2,1)} reshape(bf16[16384,224]{0,1:T(8,128)(2,1)} %all-gather.7.cloned.1.call-done) | data formatting | bytes 14680064 | tf_op jit(solution)/shard_map/reshape | solution.py:32
  244.9 82.1 %all-gather.5.cloned.1.call-done = bf16[512,7168]{0,1:T(8,128)(2,1)} async-done(((bf16[512,224]{0,1:T(8,128)(2,1)}), bf16[512,7168]{0,1:T(8,128)(2,1)}) %all-gather.5.cloned.1.call-update) | async-done | bytes 7340048 | tf_op jit(solution)/shard_map/all_gather | solution.py:35
  327.0 14.3 %bitcast_multiply_fusion = f32[448,8,224]{0,2,1:T(8,128)} fusion(bf16[8,4,512,224]{2,1,0,3:T(4,128)(2,1)} %reshape.20, bf16[512,4,1792]{0,2,1:T(8,128)(2,1)} %bitcast.13, s32[]{:T(128)S(6)} %select_n.3), kind=kOutput, calls=%fused_computation.8 | convolution fusion | flops 3289137152 | bytes 12386308 | tf_op jit(solution)/shard_map/sra,trsj->atj/dot_general | solution.py:38
  341.4 8.7 %copy.6 = f32[448,1,1792]{2,1,0:T(1,128)} copy(f32[448,1,1792]{0,2,1:T(8,128)} %bitcast.12) | data formatting | bytes 6422528 | tf_op jit(solution)/shard_map/reshape | solution.py:40
  (1 shorter events, 0.0 us)
Async XLA Ops:
  6.5 14.6 %copy-start = (bf16[2048,224]{0,1:T(8,128)(2,1)S(1)}, bf16[2048,224]{0,1:T(8,128)(2,1)}, u32[]{:S(2)}) copy-start(bf16[2048,224]{0,1:T(8,128)(2,1)} %param.7) | copy-start | bytes 2752516
  6.5 14.6 %copy-start.3 = (f32[2048]{0:T(1024)S(1)}, f32[2048]{0:T(1024)}, u32[]{:S(2)}) copy-start(f32[2048]{0:T(1024)} %param.5) | copy-start | bytes 24580
  6.5 74.3 %reduce-scatter.2.cloned.1.call-start = ((), (), s32[]{:S(2)}) async-start(), calls=%async_computation.1 | async-start | bytes 4587520 | tf_op jit(solution)/shard_map/reduce_scatter | solution.py:25
  21.2 6.4 %copy-start.1 = (bf16[2048,2048]{1,0:T(8,128)(2,1)S(1)}, bf16[2048,2048]{1,0:T(8,128)(2,1)}, u32[]{:S(2)}) copy-start(bf16[2048,2048]{1,0:T(8,128)(2,1)} %param.4) | copy-start | bytes 25165828
  21.2 6.4 %copy-start.2 = (bf16[2048,224]{0,1:T(8,128)(2,1)S(1)}, bf16[2048,224]{0,1:T(8,128)(2,1)}, u32[]{:S(2)}) copy-start(bf16[2048,224]{0,1:T(8,128)(2,1)} %param.6) | copy-start | bytes 2752516
  32.8 199.3 %all-gather.7.cloned.1.call-start = ((), (), s32[]{:S(2)}) async-start(), calls=%async_computation.3 | async-start | bytes 7569408 | tf_op jit(solution)/shard_map/all_gather | solution.py:29
  82.9 244.2 %all-gather.5.cloned.1.call-start = ((), (), s32[]{:S(2)}) async-start(), calls=%async_computation.2 | async-start | bytes 7569408 | tf_op jit(solution)/shard_map/all_gather | solution.py:35
Sparse Core Ops, SparseCore 0:
  32.9 47.9 reduce-scatter.1
  83.0 149.0 all-gather.6
  234.7 92.3 all-gather.4
where the time goes:
time: 357 us
  waiting for transfers between devices  279 us (78%)
  matrix products  23.7 us (7%)
  local copies, waits for them, and re-layouts  21.6 us (6%)
  between operations  13.2 us (4%)
  blocking collectives  9.41 us (3%)
  other arithmetic  9.38 us (3%)
    all_gather x1, waiting for transfers between devices, shards(): lax.all_gather(keys.reshape(1, local_tok, width), ('tensor', 'grow'), axi...  148 us
    all_gather x1, waiting for transfers between devices, shards(): lax.all_gather(keys.reshape(local_tok, 1, width), ('grow', 'gcol'), axis=...  82.1 us
    reduce_scatter x1, waiting for transfers between devices, shards(): lax.psum_scatter(jnp.concatenate([gate_part, up_part], axis=1), 'grow', s...  48 us
    dot_general x1, matrix products, shards(): jnp.einsum('sra,trsj->atj', row_keys, columns, preferred_element_type=jnp...  14.3 us
    reshape x1, local copies, waits for them, and re-layouts, shards(): columns = columns.reshape(n_tensor, n_grow, local_tok, width)  12.8 us
    psum x1, blocking collectives, shards(): total = lax.psum(local_sums, 'grow')  9.41 us
    reshape x1, local copies, waits for them, and re-layouts, shards(): return tile.reshape(row_width, 1, n_tensor * width)  8.74 us
  transfers between devices with their start and end apart: 3, of which 3 were waited for; matrix products, arithmetic and copies ran while one was open for 4% of the time, Pallas kernels for 0%

commit v1 on v0

v1 whole, which is shorter than its diff:
```python
import jax
import jax.numpy as jnp
from jax import lax
from jax.experimental import pallas as pl
from jax.experimental.pallas import tpu as pltpu
from jax.sharding import Mesh, PartitionSpec as P

D = 8192
EPS = 1e-05
TINY = 1e-30
F32 = jnp.float32
BF16 = jnp.bfloat16
NT = (((1,), (1,)), ((), ()))
PAD = 16


def shift(value, axis, n, by):
    return lax.ppermute(value, axis, [(i, (i + by) % n) for i in range(n)])


def encode(v):
    s = v * v
    s = s * s
    return jnp.where(v < 0, -s, s).astype(BF16)


def decode(y):
    y = y.astype(F32)
    q = lax.rsqrt(jnp.maximum(jnp.abs(y), TINY))
    return (y * q) * (q * lax.rsqrt(q))


def sumsq_row(h):
    v = h.astype(F32)
    v = v * v
    lanes = v[:, 0:128]
    for i in range(1, v.shape[1] // 128):
        lanes = lanes + v[:, i * 128 : (i + 1) * 128]
    return jnp.sum(lanes.T, axis=0, keepdims=True)


def emit_send(part, squares, o_ref, at_token):
    rows = part.shape[0]
    r = lax.rsqrt(squares + TINY)
    tokens = slice(at_token, at_token + part.shape[1])
    o_ref[0:rows, tokens] = encode(part * r)
    hi = squares.astype(BF16).astype(F32)
    rest = squares - hi
    mid = rest.astype(BF16).astype(F32)
    lo = rest - mid
    at = lax.broadcasted_iota(jnp.int32, (PAD, squares.shape[1]), 0)
    tile = jnp.where(at == 0, hi, jnp.where(at == 1, mid, jnp.where(at == 2, lo, 0.0)))
    o_ref[rows : rows + PAD, tokens] = tile.astype(BF16)


def first_kernel(idx_ref, gain_ref, gw_ref, uw_ref, h_ref, w_ref, o_ref, gu_buf, h_buf, sem):
    width = gw_ref.shape[0]
    at = pl.ds(pl.multiple_of(idx_ref[0] * 512, 512), 512)
    loads = [
        pltpu.make_async_copy(gw_ref, gu_buf.at[0], sem.at[0]),
        pltpu.make_async_copy(uw_ref, gu_buf.at[1], sem.at[1]),
        pltpu.make_async_copy(h_ref.at[at, :], h_buf, sem.at[2]),
    ]
    for cp in loads:
        cp.start()
    loads[0].wait()
    loads[1].wait()
    g = gain_ref[...]
    for i in range(2):
        w_ref[i * width : (i + 1) * width, :] = (gu_buf[i].astype(F32) * g).astype(BF16)
    loads[2].wait()
    part = lax.dot_general(w_ref[...], h_buf[...], NT, preferred_element_type=F32)
    emit_send(part, sumsq_row(h_buf[...]), o_ref, 0)


def fetch(idx_ref, h_ref, h_buf, sem):
    copies = []
    for j in range(h_buf.shape[0]):
        at = pl.ds(pl.multiple_of(idx_ref[j] * 512, 512), 512)
        copies.append(pltpu.make_async_copy(h_ref.at[at, :], h_buf.at[j], sem.at[j]))
    for cp in copies:
        cp.start()
    for cp in copies:
        cp.wait()


def send_kernel(idx_ref, w_ref, h_ref, o_ref, p_ref, h_buf, sem):
    fetch(idx_ref, h_ref, h_buf, sem)
    for k, ref in enumerate((o_ref, p_ref)):
        part = lax.dot_general(w_ref[...], h_buf[k], NT, preferred_element_type=F32)
        emit_send(part, sumsq_row(h_buf[k]), ref, 0)


def own_kernel(idx_ref, w_ref, h_ref, o_ref, h_buf, sem):
    rows = w_ref.shape[0]
    fetch(idx_ref, h_ref, h_buf, sem)
    o_ref[0:rows, :] = lax.dot_general(w_ref[...], h_buf[0], NT, preferred_element_type=F32)
    o_ref[rows : rows + 8, :] = jnp.broadcast_to(sumsq_row(h_buf[0]), (8, o_ref.shape[1]))


def keys_kernel(own_ref, p_ref, q_ref, r_ref, k_ref):
    rows = own_ref.shape[0] - 8
    width = rows // 2
    total = own_ref[rows : rows + 1, :]
    norms = []
    for ref in (p_ref, q_ref, r_ref):
        s = ref[rows : rows + PAD, :].astype(F32)
        s = s[0:1, :] + (s[1:2, :] + s[2:3, :])
        norms.append(jnp.sqrt(s + TINY))
        total = total + s
    scale = lax.rsqrt(total / D + EPS)
    mixed = own_ref[0:rows, :]
    for ref, norm in zip((p_ref, q_ref, r_ref), norms):
        mixed = mixed + decode(ref[0:rows, :]) * norm
    mixed = mixed * scale
    gate, up = mixed[0:width, :], mixed[width:rows, :]
    k_ref[...] = (gate / (1.0 + jnp.exp(-gate)) * up).astype(BF16)


ORDER = (0, 1, 3, 2)
WIDTH_TILE = 256


def lanes(s, tokens):
    return pl.ds(pl.multiple_of(lax.rem(s, 4) * tokens, tokens), tokens)


def places(t, width):
    return pl.ds(pl.multiple_of(t * width, width), width)


def put_own(cols, ref, idx_ref, d, ks):
    width = cols.shape[0] // 8
    zl, y, x = idx_ref[0], idx_ref[1], idx_ref[2]
    for i, k in enumerate(ks):
        at = places(zl * 4 + lax.rem(y + ORDER[k], 4), width)
        cols[at, lanes(x + d, 512)] = ref[i * width : (i + 1) * width, :]


def put_far(cols, ref, idx_ref, d, ks):
    width = cols.shape[0] // 8
    zl, y, x = idx_ref[0], idx_ref[1], idx_ref[2]
    for i, k in enumerate(ks):
        at = places((1 - zl) * 4 + lax.rem(y + d, 4), width)
        cols[at, lanes(x + ORDER[k], 512)] = ref[i * width : (i + 1) * width, :]


def own_cols_kernel(idx_ref, own_ref, up_ref, down_ref, cols, a_ref, b_ref):
    half = a_ref.shape[0]
    a_ref[...] = down_ref[0:half, :]
    b_ref[...] = up_ref[half:, :]
    for d, ref in ((0, own_ref), (1, up_ref), (3, down_ref)):
        put_own(cols, ref, idx_ref, d, range(4))


def far_kernel(idx_ref, cols_in, far_ref, up_ref, down_ref, cols, a_ref, b_ref):
    half = a_ref.shape[0]
    a_ref[...] = down_ref[0:half, :]
    b_ref[...] = up_ref[half:, :]
    for d, ref in ((0, far_ref), (1, up_ref), (3, down_ref)):
        put_far(cols, ref, idx_ref, d, range(4))


def moment_kernel(idx_ref, cols_in, own_a, own_b, far_a, far_b, r0, r1, s0, s1, o_ref, cols, r_buf, o_buf, sem):
    width = cols.shape[0] // 8
    zh, c = idx_ref[3], idx_ref[4]
    for n, pair in enumerate(((r0, r1), (s0, s1))):
        core = lax.rem(c + n, 2)
        for j, ref in enumerate(pair):
            at = lanes(zh + 8 - j - 2 * core, 512)
            r_buf[places(core, width), at] = ref[0:width, :]
            r_buf[places(1 - core, width), at] = ref[width:, :]
    put_own(cols, own_a, idx_ref, 2, (0, 1))
    put_own(cols, own_b, idx_ref, 2, (2, 3))
    put_far(cols, far_a, idx_ref, 2, (0, 1))
    put_far(cols, far_b, idx_ref, 2, (2, 3))
    for n in range(cols.shape[0] // WIDTH_TILE):
        at = slice(n * WIDTH_TILE, (n + 1) * WIDTH_TILE)
        acc = lax.dot_general(r_buf[...], cols[at, :], NT, preferred_element_type=F32)
        o_buf[:, 0, at] = acc * (1.0 / 2048)
    cp = pltpu.make_async_copy(o_buf, o_ref, sem.at[0])
    cp.start()
    cp.wait()


SMEM = pl.BlockSpec(memory_space=pltpu.SMEM)
VMEM = pl.BlockSpec(memory_space=pltpu.VMEM)
HBM = pl.BlockSpec(memory_space=pltpu.HBM)
MIB = 1024 * 1024


def shards(hidden, gain, gate_weight, up_weight):
    zl, y, x, zh, c = (lax.axis_index(a).astype(jnp.int32) for a in ("zl", "y", "x", "zh", "c"))
    features = hidden.shape[1]
    width = gate_weight.shape[1]
    rows = 2 * width
    gw, uw = gate_weight.T, up_weight.T
    g2 = gain[None, :]
    flops = 2 * 512 * features * rows
    def call(kernel, in_specs, out_shape, out_specs, scratch, limit, cost, *ins):
        return pl.pallas_call(
            kernel,
            in_specs=in_specs,
            out_specs=out_specs,
            out_shape=out_shape,
            scratch_shapes=scratch,
            compiler_params=pltpu.CompilerParams(vmem_limit_bytes=limit),
            cost_estimate=pl.CostEstimate(flops=cost, bytes_accessed=2 * MIB, transcendentals=0),
        )(*ins)

    def at(*ds):
        return jnp.stack([lax.rem(x + d, 4) for d in ds])

    send_shape = jax.ShapeDtypeStruct((rows + PAD, 512), BF16)

    def h_scratch(n):
        return [pltpu.VMEM((n, 512, features), BF16), pltpu.SemaphoreType.DMA((n,))]

    w, block2 = call(
        first_kernel, [SMEM, VMEM, HBM, HBM, HBM],
        (jax.ShapeDtypeStruct((rows, features), BF16), send_shape), (VMEM, VMEM),
        [pltpu.VMEM((2, width, features), BF16), pltpu.VMEM((512, features), BF16), pltpu.SemaphoreType.DMA((3,))],
        57 * MIB, flops, at(2), g2, gw, uw, hidden,
    )
    got2 = shift(block2, "x", 4, 2)
    block1, block3 = call(
        send_kernel, [SMEM, VMEM, HBM], (send_shape, send_shape), (VMEM, VMEM),
        h_scratch(2), 53 * MIB, 2 * flops, at(1, 3), w, hidden,
    )
    got1 = shift(block1, "x", 4, 1)
    got3 = shift(block3, "x", 4, -1)
    own_part = call(
        own_kernel, [SMEM, VMEM, HBM], jax.ShapeDtypeStruct((rows + 8, 512), F32), VMEM,
        h_scratch(1), 53 * MIB, flops, at(0), w, hidden,
    )
    keys = call(
        keys_kernel, [VMEM] * 4, jax.ShapeDtypeStruct((width, 512), BF16), VMEM, [], 16 * MIB, flops, own_part, got1, got2, got3
    )

    def after(v, *others):
        return lax.optimization_barrier((v,) + others)[0]

    def join(*parts):
        return jnp.concatenate(parts, axis=0)

    def rows_to(j):
        return [
            ((i * 4 + k) * 2 + e, (k * 4 + (i + j + 2 * e) % 4) * 2 + e)
            for i in range(4) for k in range(4) for e in range(2)
        ]

    place = jnp.stack([zl, y, x, zh, c])
    columns = jax.ShapeDtypeStruct((8 * width, 2048), BF16)
    two = jax.ShapeDtypeStruct((rows, 512), BF16)

    partner = shift(keys, "zl", 2, 1)
    y1, y3 = shift(keys, "y", 4, -1), shift(keys, "y", 4, 1)
    both = join(keys, shift(keys, "c", 2, 1))
    r0 = lax.ppermute(both, ("x", "zh", "c"), rows_to(0))
    r1 = lax.ppermute(both, ("x", "zh", "c"), rows_to(1))
    x1, x3 = shift(partner, "x", 4, -1), shift(partner, "x", 4, 1)
    y2 = shift(after(keys, y1, y3), "y", 4, 2)
    x2 = shift(after(partner, x1, x3), "x", 4, 2)
    own = after(join(keys, y1, y3, y2), r0)
    own_x1, own_x3 = shift(own, "x", 4, -1), shift(own, "x", 4, 1)
    far = after(join(partner, x1, x3, x2), r1)
    far_y1, far_y3 = shift(far, "y", 4, -1), shift(far, "y", 4, 1)
    s0, s1 = shift(r0, "c", 2, 1), shift(r1, "c", 2, 1)
    cols, own_up, own_down = call(
        own_cols_kernel, [SMEM] + [VMEM] * 3, (columns, two, two), (VMEM,) * 3, [], 4 * MIB, flops // 4, place, own, own_x1, own_x3
    )
    own_x2a, own_x2b = shift(own_up, "x", 4, 1), shift(own_down, "x", 4, -1)
    cols, far_up, far_down = pl.pallas_call(
        far_kernel,
        in_specs=[SMEM] + [VMEM] * 4,
        out_specs=(VMEM,) * 3,
        out_shape=(columns, two, two),
        input_output_aliases={1: 0},
        compiler_params=pltpu.CompilerParams(vmem_limit_bytes=4 * MIB),
        cost_estimate=pl.CostEstimate(flops=flops // 4, bytes_accessed=2 * MIB, transcendentals=0),
    )(place, cols, far, far_y1, far_y3)
    far_y2a, far_y2b = shift(far_up, "y", 4, 1), shift(far_down, "y", 4, -1)
    return pl.pallas_call(
        moment_kernel,
        in_specs=[SMEM] + [VMEM] * 9,
        out_specs=(HBM, VMEM),
        out_shape=(jax.ShapeDtypeStruct((rows, 1, 8 * width), F32), columns),
        scratch_shapes=[
            pltpu.VMEM((rows, 2048), BF16),
            pltpu.VMEM((rows, 1, 8 * width), F32),
            pltpu.SemaphoreType.DMA((1,)),
        ],
        input_output_aliases={1: 1},
        compiler_params=pltpu.CompilerParams(vmem_limit_bytes=16 * MIB),
        cost_estimate=pl.CostEstimate(flops=4 * flops, bytes_accessed=4 * MIB, transcendentals=0),
    )(place, cols, own_x2a, own_x2b, far_y2a, far_y2b, r0, r1, s0, s1)[0]


def solution(mesh):
    fine = Mesh(mesh.devices.reshape(2, 4, 4, 4, 2), ("zl", "y", "x", "zh", "c"))
    cols = ("zl", "y", "zh", "c")
    in_specs = (P(None, "x"), P("x"), P("x", cols), P("x", cols))
    out_specs = P(("zl", "y", "x"), ("zh", "c"), None)
    return jax.shard_map(shards, mesh=fine, in_specs=in_specs, out_specs=out_specs, check_vma=False)
```

time: 357 us -> 121 us (0.34)
  waiting for transfers between devices: 279 us -> 37.6 us
  starting transfers between devices: 0.27 us -> 53.7 us
  Pallas kernels: 0 us -> 27.2 us
  matrix products: 23.7 us -> 0 us
  local copies, waits for them, and re-layouts: 21.6 us -> 0.08 us
  between operations: 13.2 us -> 0.34 us
  blocking collectives: 9.41 us -> 0 us
  other arithmetic: 9.38 us -> 0.23 us
    all_gather x2 -> x0, waiting for transfers between devices: 231 us -> none  [the longest x1 148 us: shards(): lax.all_gather(keys.reshape(1, local_tok, width), ('tensor', 'grow'), axi...]
    ppermute x0 -> x23, starting transfers between devices: none -> 53.7 us  [the longest x21 43.4 us: shift(): return lax.ppermute(value, axis, [(i, (i + by) % n) for i in range(n)])]
    reduce_scatter x1 -> x0, waiting for transfers between devices: 48 us -> none  [shards(): lax.psum_scatter(jnp.concatenate([gate_part, up_part], axis=1), 'grow', s...]
    ppermute x0 -> x23, waiting for transfers between devices: none -> 37.6 us  [the longest x21 37.6 us: shift(): return lax.ppermute(value, axis, [(i, (i + by) % n) for i in range(n)])]
    pallas_call x0 -> x7, Pallas kernels: none -> 27.2 us  [the longest x5 18.5 us: call(): pl.pallas_call(kernel, in_specs=in_specs, out_specs=out_specs, out_shape=...]
    dot_general x3 -> x0, matrix products: 23.7 us -> none  [the longest x1 14.3 us: shards(): jnp.einsum('sra,trsj->atj', row_keys, columns, preferred_element_type=jnp...]
    reshape x2 -> x0, local copies, waits for them, and re-layouts: 21.6 us -> none  [the longest x1 12.8 us: shards(): columns = columns.reshape(n_tensor, n_grow, local_tok, width)]
    psum x1 -> x0, blocking collectives: 9.41 us -> none  [shards(): total = lax.psum(local_sums, 'grow')]
  transfers between devices with their start and end apart: 3 -> 23, of which waited for: 3 -> 7; matrix products, arithmetic and copies ran while one was open for 4% -> 0% of each run, Pallas kernels for 0% -> 12%
where the time goes in v1:
time: 121 us; the launch traced here: 119 us
  starting transfers between devices  53.7 us (44%)
  waiting for transfers between devices  37.6 us (31%)
  Pallas kernels  27.2 us (22%)
    ppermute x21, starting transfers between devices, shift(): return lax.ppermute(value, axis, [(i, (i + by) % n) for i in range(n)])  43.4 us
    ppermute x21, waiting for transfers between devices, shift(): return lax.ppermute(value, axis, [(i, (i + by) % n) for i in range(n)])  37.6 us
    pallas_call x5, Pallas kernels, call(): pl.pallas_call(kernel, in_specs=in_specs, out_specs=out_specs, out_shape=...  18.5 us
    ppermute x1, starting transfers between devices, shards(): r0 = lax.ppermute(both, ('x', 'zh', 'c'), rows_to(0))  7.9 us
    pallas_call x1, Pallas kernels, shards(): pl.pallas_call(moment_kernel, in_specs=[SMEM] + [VMEM] * 9, out_specs=(HB...  7.27 us
  transfers between devices with their start and end apart: 23, of which 7 were waited for; matrix products, arithmetic and copies ran while one was open for 0% of the time, Pallas kernels for 12%

profile of v1, /device:TPU:1, one launch (start us, length us, event | category | flops | bytes accessed | tf_op | source)
XLA Modules:
  0.0 119.2 jit_solution(13300739010881471465)
XLA Ops:
  0.0 4.9 %shard_map.46 = (bf16[448,2048]{1,0:T(8,128)(2,1)}, bf16[464,512]{1,0:T(8,128)(2,1)}) custom-call(s32[1]{0:T(128)} %bitcast.6.idx_ref, f32[1,2048]{1,0:T(1,128)} %bitcast.14, bf16[224,2048]{1,0:T(8,128)(2,1)} %bitcast.12, bf16[224,2048]{1,0:T(8,128)(2,1)} %bitcast.13, bf16[2048,2048]{1,0:T(8,128)(2,1)} %h_ref.5), custom_call_target="tpu_custom_call" | custom-call | flops 939524096 | bytes 2097152 | tf_op jit(solution)/shard_map/pallas_call | solution.py:201
  4.9 3.7 %collective-permute-start.1 = (bf16[464,512]{1,0:T(8,128)(2,1)}, bf16[464,512]{1,0:T(8,128)(2,1)S(1)}, u32[]{:S(2)}, u32[]{:S(2)}) collective-permute-start(bf16[464,512]{1,0:T(8,128)(2,1)} %get-tuple-element.22), channel_id=1, source_target_pairs={{0,16},{8,24},{16,0},{24,8},{1,17},{9,25},{17,1},{25,9},{2,18},{10... | collective-permute-start | bytes 1425416 | tf_op jit(solution)/shard_map/ppermute | solution.py:18
  8.7 6.2 %shard_map.48 = (bf16[464,512]{1,0:T(8,128)(2,1)S(1)}, bf16[464,512]{1,0:T(8,128)(2,1)S(1)}) custom-call(s32[2]{0:T(128)S(1)} %pad_add_fusion.idx_ref, bf16[448,2048]{1,0:T(8,128)(2,1)} %get-tuple-element.20.w_ref, bf16[2048,2048]{1,0:T(8,128)(2,1)} %h_ref.5), custom_call_target="tpu_custom_call" | custom-call | flops 1879048192 | bytes 2097152 | tf_op jit(solution)/shard_map/pallas_call | solution.py:201
  14.9 0.4 collective-permute-start
  15.3 2.4 %collective-permute-start.2 = (bf16[464,512]{1,0:T(8,128)(2,1)S(1)}, bf16[464,512]{1,0:T(8,128)(2,1)S(1)}, u32[]{:S(2)}, u32[]{:S(2)}) collective-permute-start(bf16[464,512]{1,0:T(8,128)(2,1)S(1)} %get-tuple-element.23), channel_id=1, source_target_pairs={{0,24},{8,0},{16,8},{24,16},{1,25},{9,1},{17,9},{25,17},{2,26},{10... | collective-permute-start | bytes 1425416 | tf_op jit(solution)/shard_map/ppermute | solution.py:18
  17.6 4.5 %shard_map.47.own_ref = f32[456,512]{1,0:T(8,128)S(1)} custom-call(s32[1]{0:T(128)} %bitcast.5.idx_ref, bf16[448,2048]{1,0:T(8,128)(2,1)} %get-tuple-element.20.w_ref, bf16[2048,2048]{1,0:T(8,128)(2,1)} %h_ref.5), custom_call_target="tpu_custom_call" | custom-call | flops 939524096 | bytes 2097152 | tf_op jit(solution)/shard_map/pallas_call | solution.py:201
  22.1 7.8 %collective-permute-done.p_ref = bf16[464,512]{1,0:T(8,128)(2,1)S(1)} collective-permute-done((bf16[464,512]{1,0:T(8,128)(2,1)S(1)}, bf16[464,512]{1,0:T(8,128)(2,1)S(1)}, u32[]{:S(2)}, u32[]{:S(2)}) %collective-permute-start) | collective-permute-done | bytes 475168 | tf_op jit(solution)/shard_map/ppermute | solution.py:18
  29.9 1.1 shard_map.49
  31.1 1.3 %collective-permute-start.6 = (bf16[224,512]{1,0:T(8,128)(2,1)S(1)}, bf16[224,512]{1,0:T(8,128)(2,1)S(1)}, u32[]{:S(2)}, u32[]{:S(2)}) collective-permute-start(bf16[224,512]{1,0:T(8,128)(2,1)S(1)} %shard_map.49), channel_id=1, source_target_pairs={{0,1},{1,0},{2,3},{3,2},{4,5},{5,4},{6,7},{7,6},{8,9},{9,8},{10,11... | collective-permute-start | bytes 688136 | tf_op jit(solution)/shard_map/ppermute | solution.py:18
  32.4 1.7 %collective-permute-start.10 = (bf16[224,512]{1,0:T(8,128)(2,1)S(1)}, bf16[224,512]{1,0:T(8,128)(2,1)S(1)}, u32[]{:S(2)}, u32[]{:S(2)}) collective-permute-start(bf16[224,512]{1,0:T(8,128)(2,1)S(1)} %shard_map.49), channel_id=1, source_target_pairs={{0,128},{128,0},{1,129},{129,1},{2,130},{130,2},{3,131},{131,3},{4... | collective-permute-start | bytes 688136 | tf_op jit(solution)/shard_map/ppermute | solution.py:18
  34.0 1.3 %collective-permute-start.4 = (bf16[224,512]{1,0:T(8,128)(2,1)S(1)}, bf16[224,512]{1,0:T(8,128)(2,1)S(1)}, u32[]{:S(2)}, u32[]{:S(2)}) collective-permute-start(bf16[224,512]{1,0:T(8,128)(2,1)S(1)} %shard_map.49), channel_id=1, source_target_pairs={{0,32},{32,64},{64,96},{96,0},{1,33},{33,65},{65,97},{97,1},{2,34}... | collective-permute-start | bytes 688136 | tf_op jit(solution)/shard_map/ppermute | solution.py:18
  35.3 1.4 %collective-permute-start.3 = (bf16[224,512]{1,0:T(8,128)(2,1)S(1)}, bf16[224,512]{1,0:T(8,128)(2,1)S(1)}, u32[]{:S(2)}, u32[]{:S(2)}) collective-permute-start(bf16[224,512]{1,0:T(8,128)(2,1)S(1)} %shard_map.49), channel_id=1, source_target_pairs={{0,96},{32,0},{64,32},{96,64},{1,97},{33,1},{65,33},{97,65},{2,98}... | collective-permute-start | bytes 688136 | tf_op jit(solution)/shard_map/ppermute | solution.py:18
  36.8 7.9 %collective-permute-start.7 = (bf16[448,512]{1,0:T(8,128)(2,1)S(1)}, bf16[448,512]{1,0:T(8,128)(2,1)S(1)}, u32[]{:S(2)}, u32[]{:S(2)}) collective-permute-start(bf16[448,512]{1,0:T(8,128)(2,1)S(1)} %pad_maximum_fusion.2), channel_id=1, source_target_pairs={{0,0},{1,5},{2,8},{3,13},{4,16},{5,21},{6,24},{7,29},{8,2},{9,7},{... | collective-permute-start | bytes 1376264 | tf_op jit(solution)/shard_map/ppermute | solution.py:259
  44.7 0.4 collective-permute-start.12
  45.1 2.4 %collective-permute-start.11 = (bf16[224,512]{1,0:T(8,128)(2,1)S(1)}, bf16[224,512]{1,0:T(8,128)(2,1)S(1)}, u32[]{:S(2)}, u32[]{:S(2)}) collective-permute-start(bf16[224,512]{1,0:T(8,128)(2,1)S(1)} %collective-permute-done.10), channel_id=1, source_target_pairs={{0,24},{8,0},{16,8},{24,16},{1,25},{9,1},{17,9},{25,17},{2,26},{10... | collective-permute-start | bytes 688136 | tf_op jit(solution)/shard_map/ppermute | solution.py:18
  47.5 1.6 %collective-permute-start.5 = (bf16[224,512]{1,0:T(8,128)(2,1)S(1)}, bf16[224,512]{1,0:T(8,128)(2,1)S(1)}, u32[]{:S(2)}, u32[]{:S(2)}) collective-permute-start(bf16[224,512]{1,0:T(8,128)(2,1)S(1)} %shard_map.49), channel_id=1, source_target_pairs={{0,64},{32,96},{64,0},{96,32},{1,65},{33,97},{65,1},{97,33},{2,66}... | collective-permute-start | bytes 688136 | tf_op jit(solution)/shard_map/ppermute | solution.py:18
  49.1 2.4 %collective-permute-start.14 = (bf16[448,512]{1,0:T(8,128)(2,1)S(1)}, bf16[448,512]{1,0:T(8,128)(2,1)}, u32[]{:S(2)}, u32[]{:S(2)}) collective-permute-start(bf16[448,512]{1,0:T(8,128)(2,1)S(1)} %pad_maximum_fusion.2), channel_id=1, source_target_pairs={{0,2},{1,7},{2,10},{3,15},{4,18},{5,23},{6,26},{7,31},{8,4},{9,1},... | collective-permute-start | bytes 1376264 | tf_op jit(solution)/shard_map/ppermute | solution.py:260
  51.5 4.1 %collective-permute-done.12 = bf16[224,512]{1,0:T(8,128)(2,1)S(1)} collective-permute-done((bf16[224,512]{1,0:T(8,128)(2,1)S(1)}, bf16[224,512]{1,0:T(8,128)(2,1)S(1)}, u32[]{:S(2)}, u32[]{:S(2)}) %collective-permute-start.12) | collective-permute-done | bytes 229408 | tf_op jit(solution)/shard_map/ppermute | solution.py:18
  55.7 9.8 %collective-permute-start.9 = (bf16[896,512]{1,0:T(8,128)(2,1)S(1)}, bf16[896,512]{1,0:T(8,128)(2,1)}, u32[]{:S(2)}, u32[]{:S(2)}) collective-permute-start(bf16[896,512]{1,0:T(8,128)(2,1)S(1)} %pad_maximum_fusion.own_ref), channel_id=1, source_target_pairs={{0,8},{8,16},{16,24},{24,0},{1,9},{9,17},{17,25},{25,1},{2,10},{10... | collective-permute-start | bytes 2752520 | tf_op jit(solution)/shard_map/ppermute | solution.py:18
  65.7 2.8 %collective-permute-start.15 = (bf16[896,512]{1,0:T(8,128)(2,1)S(1)}, bf16[896,512]{1,0:T(8,128)(2,1)}, u32[]{:S(2)}, u32[]{:S(2)}) collective-permute-start(bf16[896,512]{1,0:T(8,128)(2,1)S(1)} %pad_maximum_fusion.1.far_ref), channel_id=1, source_target_pairs={{0,96},{32,0},{64,32},{96,64},{1,97},{33,1},{65,33},{97,65},{2,98}... | collective-permute-start | bytes 2752520 | tf_op jit(solution)/shard_map/ppermute | solution.py:18
  68.6 3.5 %collective-permute-start.22 = (bf16[448,512]{1,0:T(8,128)(2,1)}, bf16[448,512]{1,0:T(8,128)(2,1)}, u32[]{:S(2)}, u32[]{:S(2)}) collective-permute-start(bf16[448,512]{1,0:T(8,128)(2,1)} %collective-permute-done.14.r1), channel_id=1, source_target_pairs={{0,1},{1,0},{2,3},{3,2},{4,5},{5,4},{6,7},{7,6},{8,9},{9,8},{10,11... | collective-permute-start | bytes 1376264 | tf_op jit(solution)/shard_map/ppermute | solution.py:18
  72.2 13.6 %collective-permute-done.9.down_ref = bf16[896,512]{1,0:T(8,128)(2,1)} collective-permute-done((bf16[896,512]{1,0:T(8,128)(2,1)S(1)}, bf16[896,512]{1,0:T(8,128)(2,1)}, u32[]{:S(2)}, u32[]{:S(2)}) %collective-permute-start.9) | collective-permute-done | bytes 917536 | tf_op jit(solution)/shard_map/ppermute | solution.py:18
  85.8 0.6 collective-permute-start.21
  86.3 2.6 %collective-permute-done.8.up_ref = bf16[896,512]{1,0:T(8,128)(2,1)} collective-permute-done((bf16[896,512]{1,0:T(8,128)(2,1)S(1)}, bf16[896,512]{1,0:T(8,128)(2,1)}, u32[]{:S(2)}, u32[]{:S(2)}) %collective-permute-start.8) | collective-permute-done | bytes 917536 | tf_op jit(solution)/shard_map/ppermute | solution.py:18
  88.9 1.7 %shard_map.50 = (bf16[1792,2048]{1,0:T(8,128)(2,1)S(1)}, bf16[448,512]{1,0:T(8,128)(2,1)S(1)}, bf16[448,512]{1,0:T(8,128)(2,1)S(1)}) custom-call(s32[5]{0:T(128)S(1)} %stack.38.idx_ref, bf16[896,512]{1,0:T(8,128)(2,1)S(1)} %pad_maximum_fusion.own_ref, bf16[896,512]{1,0:T(8,128)(2,1)} %collective-permute-done.8.up_ref, ...), custom_call_target="tpu_custom_call" | custom-call | flops 234881024 | bytes 2097152 | tf_op jit(solution)/shard_map/pallas_call | solution.py:201
  90.7 1.5 %shard_map.51 = (bf16[1792,2048]{1,0:T(8,128)(2,1)S(1)}, bf16[448,512]{1,0:T(8,128)(2,1)S(1)}, bf16[448,512]{1,0:T(8,128)(2,1)S(1)}) custom-call(s32[5]{0:T(128)S(1)} %stack.38.idx_ref, bf16[1792,2048]{1,0:T(8,128)(2,1)S(1)} %get-tuple-element.26.cols_in, bf16[896,512]{1,0:T(8,128)(2,1)S(1)} %pad_maximum_fusion.1.far_ref, ...), custom_call_target="tpu_custom_call", output_to_operand_aliasing={{0}: (1, {})} | custom-call | flops 234881024 | bytes 2097152 | tf_op jit(solution)/shard_map/pallas_call | solution.py:273
  92.2 2.7 %collective-permute-start.20 = (bf16[448,512]{1,0:T(8,128)(2,1)S(1)}, bf16[448,512]{1,0:T(8,128)(2,1)S(1)}, u32[]{:S(2)}, u32[]{:S(2)}) collective-permute-start(bf16[448,512]{1,0:T(8,128)(2,1)S(1)} %get-tuple-element.33), channel_id=1, source_target_pairs={{0,96},{32,0},{64,32},{96,64},{1,97},{33,1},{65,33},{97,65},{2,98}... | collective-permute-start | bytes 1376264 | tf_op jit(solution)/shard_map/ppermute | solution.py:18
  94.9 7.3 %collective-permute-start.17 = (bf16[448,512]{1,0:T(8,128)(2,1)S(1)}, bf16[448,512]{1,0:T(8,128)(2,1)S(1)}, u32[]{:S(2)}, u32[]{:S(2)}) collective-permute-start(bf16[448,512]{1,0:T(8,128)(2,1)S(1)} %get-tuple-element.30), channel_id=1, source_target_pairs={{0,8},{8,16},{16,24},{24,0},{1,9},{9,17},{17,25},{25,1},{2,10},{10... | collective-permute-start | bytes 1376264 | tf_op jit(solution)/shard_map/ppermute | solution.py:18
  102.2 2.7 %collective-permute-done.19.far_a = bf16[448,512]{1,0:T(8,128)(2,1)S(1)} collective-permute-done((bf16[448,512]{1,0:T(8,128)(2,1)S(1)}, bf16[448,512]{1,0:T(8,128)(2,1)S(1)}, u32[]{:S(2)}, u32[]{:S(2)}) %collective-permute-start.19) | collective-permute-done | bytes 458784 | tf_op jit(solution)/shard_map/ppermute | solution.py:18
  104.9 4.9 %collective-permute-done.17.own_a = bf16[448,512]{1,0:T(8,128)(2,1)S(1)} collective-permute-done((bf16[448,512]{1,0:T(8,128)(2,1)S(1)}, bf16[448,512]{1,0:T(8,128)(2,1)S(1)}, u32[]{:S(2)}, u32[]{:S(2)}) %collective-permute-start.17) | collective-permute-done | bytes 458784 | tf_op jit(solution)/shard_map/ppermute | solution.py:18
  109.8 1.9 %collective-permute-done.18.own_b = bf16[448,512]{1,0:T(8,128)(2,1)S(1)} collective-permute-done((bf16[448,512]{1,0:T(8,128)(2,1)S(1)}, bf16[448,512]{1,0:T(8,128)(2,1)S(1)}, u32[]{:S(2)}, u32[]{:S(2)}) %collective-permute-start.18) | collective-permute-done | bytes 458784 | tf_op jit(solution)/shard_map/ppermute | solution.py:18
  111.8 7.3 %shard_map.52 = (f32[448,1,1792]{2,1,0:T(1,128)}, bf16[1792,2048]{1,0:T(8,128)(2,1)S(1)}) custom-call(s32[5]{0:T(128)S(1)} %stack.38.idx_ref, bf16[1792,2048]{1,0:T(8,128)(2,1)S(1)} %get-tuple-element.29.cols_in, bf16[448,512]{1,0:T(8,128)(2,1)S(1)} %collective-permute-done.17.own_a, ...), custom_call_target="tpu_custom_call", output_to_operand_aliasing={{1}: (1, {})} | custom-call | flops 3758096384 | bytes 4194304 | tf_op jit(solution)/shard_map/pallas_call | solution.py:283
  (26 shorter events, 0.5 us)
Async XLA Ops:
  4.9 17.2 %collective-permute-start.1 = (bf16[464,512]{1,0:T(8,128)(2,1)}, bf16[464,512]{1,0:T(8,128)(2,1)S(1)}, u32[]{:S(2)}, u32[]{:S(2)}) collective-permute-start(bf16[464,512]{1,0:T(8,128)(2,1)} %get-tuple-element.22), channel_id=1, source_target_pairs={{0,16},{8,24},{16,0},{24,8},{1,17},{9,25},{17,1},{25,9},{2,18},{10... | collective-permute-start | bytes 1425416 | tf_op jit(solution)/shard_map/ppermute | solution.py:18
  14.9 15.0 %collective-permute-start = (bf16[464,512]{1,0:T(8,128)(2,1)S(1)}, bf16[464,512]{1,0:T(8,128)(2,1)S(1)}, u32[]{:S(2)}, u32[]{:S(2)}) collective-permute-start(bf16[464,512]{1,0:T(8,128)(2,1)S(1)} %get-tuple-element.21), channel_id=1, source_target_pairs={{0,8},{8,16},{16,24},{24,0},{1,9},{9,17},{17,25},{25,1},{2,10},{10... | collective-permute-start | bytes 1425416 | tf_op jit(solution)/shard_map/ppermute | solution.py:18
  15.3 14.7 %collective-permute-start.2 = (bf16[464,512]{1,0:T(8,128)(2,1)S(1)}, bf16[464,512]{1,0:T(8,128)(2,1)S(1)}, u32[]{:S(2)}, u32[]{:S(2)}) collective-permute-start(bf16[464,512]{1,0:T(8,128)(2,1)S(1)} %get-tuple-element.23), channel_id=1, source_target_pairs={{0,24},{8,0},{16,8},{24,16},{1,25},{9,1},{17,9},{25,17},{2,26},{10... | collective-permute-start | bytes 1425416 | tf_op jit(solution)/shard_map/ppermute | solution.py:18
  31.1 5.7 %collective-permute-start.6 = (bf16[224,512]{1,0:T(8,128)(2,1)S(1)}, bf16[224,512]{1,0:T(8,128)(2,1)S(1)}, u32[]{:S(2)}, u32[]{:S(2)}) collective-permute-start(bf16[224,512]{1,0:T(8,128)(2,1)S(1)} %shard_map.49), channel_id=1, source_target_pairs={{0,1},{1,0},{2,3},{3,2},{4,5},{5,4},{6,7},{7,6},{8,9},{9,8},{10,11... | collective-permute-start | bytes 688136 | tf_op jit(solution)/shard_map/ppermute | solution.py:18
  32.4 12.4 %collective-permute-start.10 = (bf16[224,512]{1,0:T(8,128)(2,1)S(1)}, bf16[224,512]{1,0:T(8,128)(2,1)S(1)}, u32[]{:S(2)}, u32[]{:S(2)}) collective-permute-start(bf16[224,512]{1,0:T(8,128)(2,1)S(1)} %shard_map.49), channel_id=1, source_target_pairs={{0,128},{128,0},{1,129},{129,1},{2,130},{130,2},{3,131},{131,3},{4... | collective-permute-start | bytes 688136 | tf_op jit(solution)/shard_map/ppermute | solution.py:18
  34.0 13.5 %collective-permute-start.4 = (bf16[224,512]{1,0:T(8,128)(2,1)S(1)}, bf16[224,512]{1,0:T(8,128)(2,1)S(1)}, u32[]{:S(2)}, u32[]{:S(2)}) collective-permute-start(bf16[224,512]{1,0:T(8,128)(2,1)S(1)} %shard_map.49), channel_id=1, source_target_pairs={{0,32},{32,64},{64,96},{96,0},{1,33},{33,65},{65,97},{97,1},{2,34}... | collective-permute-start | bytes 688136 | tf_op jit(solution)/shard_map/ppermute | solution.py:18
  35.3 12.2 %collective-permute-start.3 = (bf16[224,512]{1,0:T(8,128)(2,1)S(1)}, bf16[224,512]{1,0:T(8,128)(2,1)S(1)}, u32[]{:S(2)}, u32[]{:S(2)}) collective-permute-start(bf16[224,512]{1,0:T(8,128)(2,1)S(1)} %shard_map.49), channel_id=1, source_target_pairs={{0,96},{32,0},{64,32},{96,64},{1,97},{33,1},{65,33},{97,65},{2,98}... | collective-permute-start | bytes 688136 | tf_op jit(solution)/shard_map/ppermute | solution.py:18
  36.8 18.9 %collective-permute-start.7 = (bf16[448,512]{1,0:T(8,128)(2,1)S(1)}, bf16[448,512]{1,0:T(8,128)(2,1)S(1)}, u32[]{:S(2)}, u32[]{:S(2)}) collective-permute-start(bf16[448,512]{1,0:T(8,128)(2,1)S(1)} %pad_maximum_fusion.2), channel_id=1, source_target_pairs={{0,0},{1,5},{2,8},{3,13},{4,16},{5,21},{6,24},{7,29},{8,2},{9,7},{... | collective-permute-start | bytes 1376264 | tf_op jit(solution)/shard_map/ppermute | solution.py:259
  44.7 10.9 %collective-permute-start.12 = (bf16[224,512]{1,0:T(8,128)(2,1)S(1)}, bf16[224,512]{1,0:T(8,128)(2,1)S(1)}, u32[]{:S(2)}, u32[]{:S(2)}) collective-permute-start(bf16[224,512]{1,0:T(8,128)(2,1)S(1)} %collective-permute-done.10), channel_id=1, source_target_pairs={{0,8},{8,16},{16,24},{24,0},{1,9},{9,17},{17,25},{25,1},{2,10},{10... | collective-permute-start | bytes 688136 | tf_op jit(solution)/shard_map/ppermute | solution.py:18
  45.1 10.5 %collective-permute-start.11 = (bf16[224,512]{1,0:T(8,128)(2,1)S(1)}, bf16[224,512]{1,0:T(8,128)(2,1)S(1)}, u32[]{:S(2)}, u32[]{:S(2)}) collective-permute-start(bf16[224,512]{1,0:T(8,128)(2,1)S(1)} %collective-permute-done.10), channel_id=1, source_target_pairs={{0,24},{8,0},{16,8},{24,16},{1,25},{9,1},{17,9},{25,17},{2,26},{10... | collective-permute-start | bytes 688136 | tf_op jit(solution)/shard_map/ppermute | solution.py:18
  47.5 8.2 %collective-permute-start.5 = (bf16[224,512]{1,0:T(8,128)(2,1)S(1)}, bf16[224,512]{1,0:T(8,128)(2,1)S(1)}, u32[]{:S(2)}, u32[]{:S(2)}) collective-permute-start(bf16[224,512]{1,0:T(8,128)(2,1)S(1)} %shard_map.49), channel_id=1, source_target_pairs={{0,64},{32,96},{64,0},{96,32},{1,65},{33,97},{65,1},{97,33},{2,66}... | collective-permute-start | bytes 688136 | tf_op jit(solution)/shard_map/ppermute | solution.py:18
  49.1 16.5 %collective-permute-start.14 = (bf16[448,512]{1,0:T(8,128)(2,1)S(1)}, bf16[448,512]{1,0:T(8,128)(2,1)}, u32[]{:S(2)}, u32[]{:S(2)}) collective-permute-start(bf16[448,512]{1,0:T(8,128)(2,1)S(1)} %pad_maximum_fusion.2), channel_id=1, source_target_pairs={{0,2},{1,7},{2,10},{3,15},{4,18},{5,23},{6,26},{7,31},{8,4},{9,1},... | collective-permute-start | bytes 1376264 | tf_op jit(solution)/shard_map/ppermute | solution.py:260
  55.6 9.9 %collective-permute-start.13 = (bf16[224,512]{1,0:T(8,128)(2,1)S(1)}, bf16[224,512]{1,0:T(8,128)(2,1)S(1)}, u32[]{:S(2)}, u32[]{:S(2)}) collective-permute-start(bf16[224,512]{1,0:T(8,128)(2,1)S(1)} %collective-permute-done.10), channel_id=1, source_target_pairs={{0,16},{8,24},{16,0},{24,8},{1,17},{9,25},{17,1},{25,9},{2,18},{10... | collective-permute-start | bytes 688136 | tf_op jit(solution)/shard_map/ppermute | solution.py:18
  55.7 30.0 %collective-permute-start.9 = (bf16[896,512]{1,0:T(8,128)(2,1)S(1)}, bf16[896,512]{1,0:T(8,128)(2,1)}, u32[]{:S(2)}, u32[]{:S(2)}) collective-permute-start(bf16[896,512]{1,0:T(8,128)(2,1)S(1)} %pad_maximum_fusion.own_ref), channel_id=1, source_target_pairs={{0,8},{8,16},{16,24},{24,0},{1,9},{9,17},{17,25},{25,1},{2,10},{10... | collective-permute-start | bytes 2752520 | tf_op jit(solution)/shard_map/ppermute | solution.py:18
  65.6 23.3 %collective-permute-start.8 = (bf16[896,512]{1,0:T(8,128)(2,1)S(1)}, bf16[896,512]{1,0:T(8,128)(2,1)}, u32[]{:S(2)}, u32[]{:S(2)}) collective-permute-start(bf16[896,512]{1,0:T(8,128)(2,1)S(1)} %pad_maximum_fusion.own_ref), channel_id=1, source_target_pairs={{0,24},{8,0},{16,8},{24,16},{1,25},{9,1},{17,9},{25,17},{2,26},{10... | collective-permute-start | bytes 2752520 | tf_op jit(solution)/shard_map/ppermute | solution.py:18
  65.6 25.0 %collective-permute-start.16 = (bf16[896,512]{1,0:T(8,128)(2,1)S(1)}, bf16[896,512]{1,0:T(8,128)(2,1)S(1)}, u32[]{:S(2)}, u32[]{:S(2)}) collective-permute-start(bf16[896,512]{1,0:T(8,128)(2,1)S(1)} %pad_maximum_fusion.1.far_ref), channel_id=1, source_target_pairs={{0,32},{32,64},{64,96},{96,0},{1,33},{33,65},{65,97},{97,1},{2,34}... | collective-permute-start | bytes 2752520 | tf_op jit(solution)/shard_map/ppermute | solution.py:18
  65.7 24.9 %collective-permute-start.15 = (bf16[896,512]{1,0:T(8,128)(2,1)S(1)}, bf16[896,512]{1,0:T(8,128)(2,1)}, u32[]{:S(2)}, u32[]{:S(2)}) collective-permute-start(bf16[896,512]{1,0:T(8,128)(2,1)S(1)} %pad_maximum_fusion.1.far_ref), channel_id=1, source_target_pairs={{0,96},{32,0},{64,32},{96,64},{1,97},{33,1},{65,33},{97,65},{2,98}... | collective-permute-start | bytes 2752520 | tf_op jit(solution)/shard_map/ppermute | solution.py:18
  68.6 33.7 %collective-permute-start.22 = (bf16[448,512]{1,0:T(8,128)(2,1)}, bf16[448,512]{1,0:T(8,128)(2,1)}, u32[]{:S(2)}, u32[]{:S(2)}) collective-permute-start(bf16[448,512]{1,0:T(8,128)(2,1)} %collective-permute-done.14.r1), channel_id=1, source_target_pairs={{0,1},{1,0},{2,3},{3,2},{4,5},{5,4},{6,7},{7,6},{8,9},{9,8},{10,11... | collective-permute-start | bytes 1376264 | tf_op jit(solution)/shard_map/ppermute | solution.py:18
  85.8 16.4 %collective-permute-start.21 = (bf16[448,512]{1,0:T(8,128)(2,1)S(1)}, bf16[448,512]{1,0:T(8,128)(2,1)S(1)}, u32[]{:S(2)}, u32[]{:S(2)}) collective-permute-start(bf16[448,512]{1,0:T(8,128)(2,1)S(1)} %collective-permute-done.7.r0), channel_id=1, source_target_pairs={{0,1},{1,0},{2,3},{3,2},{4,5},{5,4},{6,7},{7,6},{8,9},{9,8},{10,11... | collective-permute-start | bytes 1376264 | tf_op jit(solution)/shard_map/ppermute | solution.py:18
  92.1 12.8 %collective-permute-start.19 = (bf16[448,512]{1,0:T(8,128)(2,1)S(1)}, bf16[448,512]{1,0:T(8,128)(2,1)S(1)}, u32[]{:S(2)}, u32[]{:S(2)}) collective-permute-start(bf16[448,512]{1,0:T(8,128)(2,1)S(1)} %get-tuple-element.32), channel_id=1, source_target_pairs={{0,32},{32,64},{64,96},{96,0},{1,33},{33,65},{65,97},{97,1},{2,34}... | collective-permute-start | bytes 1376264 | tf_op jit(solution)/shard_map/ppermute | solution.py:18
  92.2 12.7 %collective-permute-start.20 = (bf16[448,512]{1,0:T(8,128)(2,1)S(1)}, bf16[448,512]{1,0:T(8,128)(2,1)S(1)}, u32[]{:S(2)}, u32[]{:S(2)}) collective-permute-start(bf16[448,512]{1,0:T(8,128)(2,1)S(1)} %get-tuple-element.33), channel_id=1, source_target_pairs={{0,96},{32,0},{64,32},{96,64},{1,97},{33,1},{65,33},{97,65},{2,98}... | collective-permute-start | bytes 1376264 | tf_op jit(solution)/shard_map/ppermute | solution.py:18
  94.9 15.0 %collective-permute-start.17 = (bf16[448,512]{1,0:T(8,128)(2,1)S(1)}, bf16[448,512]{1,0:T(8,128)(2,1)S(1)}, u32[]{:S(2)}, u32[]{:S(2)}) collective-permute-start(bf16[448,512]{1,0:T(8,128)(2,1)S(1)} %get-tuple-element.30), channel_id=1, source_target_pairs={{0,8},{8,16},{16,24},{24,0},{1,9},{9,17},{17,25},{25,1},{2,10},{10... | collective-permute-start | bytes 1376264 | tf_op jit(solution)/shard_map/ppermute | solution.py:18
  102.2 9.6 %collective-permute-start.18 = (bf16[448,512]{1,0:T(8,128)(2,1)S(1)}, bf16[448,512]{1,0:T(8,128)(2,1)S(1)}, u32[]{:S(2)}, u32[]{:S(2)}) collective-permute-start(bf16[448,512]{1,0:T(8,128)(2,1)S(1)} %get-tuple-element.31), channel_id=1, source_target_pairs={{0,24},{8,0},{16,8},{24,16},{1,25},{9,1},{17,9},{25,17},{2,26},{10... | collective-permute-start | bytes 1376264 | tf_op jit(solution)/shard_map/ppermute | solution.py:18

commit v2 on v1

--- a/solution.py
+++ b/solution.py
@@ -118,7 +118,6 @@
 
 
 ORDER = (0, 1, 3, 2)
-WIDTH_TILE = 256
 
 
 def lanes(s, tokens):
@@ -129,58 +128,129 @@
     return pl.ds(pl.multiple_of(t * width, width), width)
 
 
-def put_own(cols, ref, idx_ref, d, ks):
-    width = cols.shape[0] // 8
-    zl, y, x = idx_ref[0], idx_ref[1], idx_ref[2]
-    for i, k in enumerate(ks):
-        at = places(zl * 4 + lax.rem(y + ORDER[k], 4), width)
-        cols[at, lanes(x + d, 512)] = ref[i * width : (i + 1) * width, :]
-
-
-def put_far(cols, ref, idx_ref, d, ks):
-    width = cols.shape[0] // 8
-    zl, y, x = idx_ref[0], idx_ref[1], idx_ref[2]
-    for i, k in enumerate(ks):
-        at = places((1 - zl) * 4 + lax.rem(y + d, 4), width)
-        cols[at, lanes(x + ORDER[k], 512)] = ref[i * width : (i + 1) * width, :]
-
-
-def own_cols_kernel(idx_ref, own_ref, up_ref, down_ref, cols, a_ref, b_ref):
-    half = a_ref.shape[0]
-    a_ref[...] = down_ref[0:half, :]
-    b_ref[...] = up_ref[half:, :]
-    for d, ref in ((0, own_ref), (1, up_ref), (3, down_ref)):
-        put_own(cols, ref, idx_ref, d, range(4))
-
-
-def far_kernel(idx_ref, cols_in, far_ref, up_ref, down_ref, cols, a_ref, b_ref):
-    half = a_ref.shape[0]
-    a_ref[...] = down_ref[0:half, :]
-    b_ref[...] = up_ref[half:, :]
-    for d, ref in ((0, far_ref), (1, up_ref), (3, down_ref)):
-        put_far(cols, ref, idx_ref, d, range(4))
-
-
-def moment_kernel(idx_ref, cols_in, own_a, own_b, far_a, far_b, r0, r1, s0, s1, o_ref, cols, r_buf, o_buf, sem):
-    width = cols.shape[0] // 8
-    zh, c = idx_ref[3], idx_ref[4]
-    for n, pair in enumerate(((r0, r1), (s0, s1))):
-        core = lax.rem(c + n, 2)
-        for j, ref in enumerate(pair):
-            at = lanes(zh + 8 - j - 2 * core, 512)
-            r_buf[places(core, width), at] = ref[0:width, :]
-            r_buf[places(1 - core, width), at] = ref[width:, :]
-    put_own(cols, own_a, idx_ref, 2, (0, 1))
-    put_own(cols, own_b, idx_ref, 2, (2, 3))
-    put_far(cols, far_a, idx_ref, 2, (0, 1))
-    put_far(cols, far_b, idx_ref, 2, (2, 3))
-    for n in range(cols.shape[0] // WIDTH_TILE):
-        at = slice(n * WIDTH_TILE, (n + 1) * WIDTH_TILE)
-        acc = lax.dot_general(r_buf[...], cols[at, :], NT, preferred_element_type=F32)
-        o_buf[:, 0, at] = acc * (1.0 / 2048)
-    cp = pltpu.make_async_copy(o_buf, o_ref, sem.at[0])
-    cp.start()
-    cp.wait()
+def put(cols, ref, idx_ref, role, d, offsets, which, step=2):
+    width = cols.shape[0] // 4
+    y, x = idx_ref[1], idx_ref[2]
+    for i, off in enumerate(offsets):
+        row, lane = y + off + role * (d - off), x + d + role * (off - d)
+        at = (step * i + which) * width
+        cols[places(lax.rem(row, 4), width), lanes(lane, 512)] = ref[at : at + width, :]
+
+
+def base_kernel(idx_ref, k_ref, k_other, p_ref, p_other, b_ref):
+    width = k_ref.shape[0]
+    for core, (first, second) in enumerate(((k_ref, k_other), (p_ref, p_other))):
+
+        @pl.when(idx_ref[4] == core)
+        def _():
+            b_ref[0:width, :] = first[...]
+            b_ref[width:, :] = second[...]
+
+
+def pack_kernel(*refs):
+    size = refs[0].shape[0]
+    for i, ref in enumerate(refs[:4]):
+        refs[4][i * size : (i + 1) * size, :] = ref[...]
+
+
+def clear(cols, idx_ref, role):
+    width = cols.shape[0] // 4
+    y, x = idx_ref[1], idx_ref[2]
+
+    @pl.when(role == 0)
+    def _():
+        cols[:, lanes(x + 2, 512)] = jnp.zeros((4 * width, 512), BF16)
+
+    @pl.when(role == 1)
+    def _():
+        cols[places(lax.rem(y + 2, 4), width), :] = jnp.zeros((width, cols.shape[1]), BF16)
+
+
+def mine_kernel(idx_ref, q_ref, up_ref, down_ref, near, far, cols, a_keep, a_give, b_keep, b_give, give):
+    width = cols.shape[0] // 4
+    for ref, first, k_ref, g_ref in ((down_ref, 0, a_keep, a_give), (up_ref, 4, b_keep, b_give)):
+        for i in range(2):
+            at = (first + 2 * i) * width
+            k_ref[i * width : (i + 1) * width, :] = ref[at : at + width, :]
+            g_ref[i * width : (i + 1) * width, :] = ref[at + width : at + 2 * width, :]
+    clear(cols, idx_ref, idx_ref[4])
+    for n, (d, ref) in enumerate(((0, q_ref), (1, up_ref), (3, down_ref))):
+        put(cols, ref, idx_ref, idx_ref[4], d, ORDER, 0)
+        for i in range(4):
+            to, at = (4 * n + i) * width, (2 * i + 1) * width
+            give[to : to + width, :] = ref[at : at + width, :]
+    give[12 * width : 14 * width, :] = near[...]
+    give[14 * width :, :] = far[...]
+
+
+def row_kernel(idx_ref, k_ref, k_other, near, far, got, out_ref, out2_ref, own_ref, buf):
+    width = k_ref.shape[0]
+    x, zh, c = idx_ref[2], idx_ref[3], idx_ref[4]
+    before, behind = lax.rem(zh + 3 + 2 * c, 4), lax.rem(zh + 5 - 2 * c, 4)
+    buf[zh, 0:width] = k_ref[...]
+    buf[zh, width:] = k_other[...]
+    buf[before] = near[...]
+    buf[behind, 0:width] = got[width : 2 * width, :]
+    buf[behind, width:] = got[0:width, :]
+    buf[lax.rem(zh + 2, 4), 0:width] = far[...]
+    buf[lax.rem(zh + 2, 4), width:] = got[2 * width :, :]
+    out_ref[...] = buf[lax.rem(x + 5 - 2 * c, 4)]
+    out2_ref[...] = buf[lax.rem(x + 2, 4), 0:width]
+    own_ref[...] = buf[x]
+
+
+def early_kernel(idx_ref, mine, got, row_own, near, far, r_buf, acc_mine, acc_theirs, theirs):
+    width = mine.shape[0] // 4
+    x, c = idx_ref[2], idx_ref[4]
+    this, that = places(c, width), places(1 - c, width)
+    before, behind = lanes(x + 3 + 2 * c, 512), lanes(x + 5 - 2 * c, 512)
+    r_buf[this, lanes(x, 512)] = row_own[0:width, :]
+    r_buf[that, lanes(x, 512)] = row_own[width:, :]
+    r_buf[this, before] = near[0:width, :]
+    r_buf[that, before] = near[width:, :]
+    r_buf[that, behind] = got[12 * width : 13 * width, :]
+    r_buf[this, behind] = got[13 * width : 14 * width, :]
+    r_buf[this, lanes(x + 2, 512)] = far[...]
+    r_buf[that, lanes(x + 2, 512)] = got[14 * width :, :]
+    clear(theirs, idx_ref, 1 - c)
+    for n, d in enumerate((0, 1, 3)):
+        put(theirs, got.at[4 * n * width : 4 * (n + 1) * width], idx_ref, 1 - c, d, ORDER, 0, 1)
+    acc_mine[...] = lax.dot_general(r_buf[...], mine[...], NT, preferred_element_type=F32)
+    acc_theirs[...] = lax.dot_general(r_buf[...], theirs[...], NT, preferred_element_type=F32)
+
+
+def moment_kernel(idx_ref, r_ref, acc_mine, acc_theirs, d_a, d_b, e_a, e_b, o_ref, tall, wide, o_buf, sem):
+    width = wide.shape[0]
+    zl, y, x, c = idx_ref[0], idx_ref[1], idx_ref[2], idx_ref[4]
+    unit = 1.0 / r_ref.shape[1]
+    copies = []
+    for n, (acc, role, a, b) in enumerate(((acc_mine, c, d_a, d_b), (acc_theirs, 1 - c, e_a, e_b))):
+        shards = [ref[i * width : (i + 1) * width, :] for ref in (a, b) for i in range(2)]
+
+        @pl.when(role == 0)
+        def _():
+            for off, v in zip(ORDER, shards):
+                tall[places(lax.rem(y + off, 4), width), :] = v
+            more = lax.dot_general(r_ref[:, lanes(x + 2, 512)], tall[...], NT, preferred_element_type=F32)
+            o_buf[n, :, 0, :] = (acc[...] + more) * unit
+
+        @pl.when(role == 1)
+        def _():
+            for off, v in zip(ORDER, shards):
+                wide[:, lanes(x + off, 512)] = v
+            more = lax.dot_general(r_ref[...], wide[...], NT, preferred_element_type=F32)
+            o_buf[n, :, 0, :] = acc[...] * unit
+            for k in range(4):
+
+                @pl.when(lax.rem(y + 2, 4) == k)
+                def _():
+                    o_buf[n, :, 0, k * width : (k + 1) * width] = more * unit
+
+        at = places(zl + role * (1 - 2 * zl), 4 * width)
+        copies.append(pltpu.make_async_copy(o_buf.at[n], o_ref.at[:, :, at], sem.at[n]))
+        copies[n].start()
+    for cp in copies:
+        cp.wait()
 
 
 SMEM = pl.BlockSpec(memory_space=pltpu.SMEM)
@@ -243,57 +313,69 @@
     def join(*parts):
         return jnp.concatenate(parts, axis=0)
 
-    def rows_to(j):
-        return [
-            ((i * 4 + k) * 2 + e, (k * 4 + (i + j + 2 * e) % 4) * 2 + e)
-            for i in range(4) for k in range(4) for e in range(2)
-        ]
-
     place = jnp.stack([zl, y, x, zh, c])
-    columns = jax.ShapeDtypeStruct((8 * width, 2048), BF16)
-    two = jax.ShapeDtypeStruct((rows, 512), BF16)
-
+
+    def local(kernel, ins, shapes, scratch=(), indexed=True):
+        single = not isinstance(shapes, tuple)
+        return call(
+            kernel, ([SMEM] if indexed else []) + [VMEM] * len(ins), shapes, VMEM if single else (VMEM,) * len(shapes),
+            list(scratch), 12 * MIB, flops // 4, *(((place,) if indexed else ()) + tuple(ins)),
+        )
+
+    def block(n):
+        return jax.ShapeDtypeStruct((n * width, 512), BF16)
+
+    def cross(v, d, swapped, flip=0):
+        pairs = []
+        for i in range(4):
+            for j in range(4):
+                for e in range(2):
+                    ni, nj = ((i + d) % 4, j) if (e == 0) != swapped else (i, (j + d) % 4)
+                    pairs.append(((i * 4 + j) * 2 + e, (ni * 4 + nj) * 2 + (e ^ flip)))
+        return lax.ppermute(v, ("y", "x", "c"), pairs)
+
+    def apart(v, axis):
+        return lax.ppermute(v, (axis, "c"), [(i * 2 + e, (i + 1 - 2 * e) % 4 * 2 + e) for i in range(4) for e in range(2)])
+
+    def swap(v):
+        return shift(v, "c", 2, 1)
+
+    cols = jax.ShapeDtypeStruct((4 * width, 2048), BF16)
     partner = shift(keys, "zl", 2, 1)
-    y1, y3 = shift(keys, "y", 4, -1), shift(keys, "y", 4, 1)
-    both = join(keys, shift(keys, "c", 2, 1))
-    r0 = lax.ppermute(both, ("x", "zh", "c"), rows_to(0))
-    r1 = lax.ppermute(both, ("x", "zh", "c"), rows_to(1))
-    x1, x3 = shift(partner, "x", 4, -1), shift(partner, "x", 4, 1)
-    y2 = shift(after(keys, y1, y3), "y", 4, 2)
-    x2 = shift(after(partner, x1, x3), "x", 4, 2)
-    own = after(join(keys, y1, y3, y2), r0)
-    own_x1, own_x3 = shift(own, "x", 4, -1), shift(own, "x", 4, 1)
-    far = after(join(partner, x1, x3, x2), r1)
-    far_y1, far_y3 = shift(far, "y", 4, -1), shift(far, "y", 4, 1)
-    s0, s1 = shift(r0, "c", 2, 1), shift(r1, "c", 2, 1)
-    cols, own_up, own_down = call(
-        own_cols_kernel, [SMEM] + [VMEM] * 3, (columns, two, two), (VMEM,) * 3, [], 4 * MIB, flops // 4, place, own, own_x1, own_x3
-    )
-    own_x2a, own_x2b = shift(own_up, "x", 4, 1), shift(own_down, "x", 4, -1)
-    cols, far_up, far_down = pl.pallas_call(
-        far_kernel,
-        in_specs=[SMEM] + [VMEM] * 4,
-        out_specs=(VMEM,) * 3,
-        out_shape=(columns, two, two),
-        input_output_aliases={1: 0},
-        compiler_params=pltpu.CompilerParams(vmem_limit_bytes=4 * MIB),
-        cost_estimate=pl.CostEstimate(flops=flops // 4, bytes_accessed=2 * MIB, transcendentals=0),
-    )(place, cols, far, far_y1, far_y3)
-    far_y2a, far_y2b = shift(far_up, "y", 4, 1), shift(far_down, "y", 4, -1)
-    return pl.pallas_call(
-        moment_kernel,
-        in_specs=[SMEM] + [VMEM] * 9,
-        out_specs=(HBM, VMEM),
-        out_shape=(jax.ShapeDtypeStruct((rows, 1, 8 * width), F32), columns),
-        scratch_shapes=[
-            pltpu.VMEM((rows, 2048), BF16),
-            pltpu.VMEM((rows, 1, 8 * width), F32),
-            pltpu.SemaphoreType.DMA((1,)),
+    other = swap(keys)
+    base = local(base_kernel, (keys, other, partner, swap(partner)), block(2))
+    near = apart(join(keys, other), "zh")
+    p1, p3, p2 = cross(base, -1, False), cross(base, 1, False), cross(base, 2, False)
+    far = apart(near[0:width], "zh")
+    q = local(pack_kernel, (base, p1, p3, after(p2, near)), block(8), indexed=False)
+    q1, q3 = cross(q, -1, True), cross(q, 1, True)
+    row_out, row_out2, row_own = local(
+        row_kernel, (keys, other, near, far, swap(join(near, far))), (block(2), block(1), block(2)),
+        [pltpu.VMEM((4, rows, 512), BF16)],
+    )
+    row_near, row_far = apart(row_out, "x"), shift(row_out2, "x", 4, 2)
+    mine, a_keep, a_give, b_keep, b_give, give = local(
+        mine_kernel, (q, q1, q3, row_near, row_far), (cols,) + (block(2),) * 4 + (block(15),)
+    )
+    d_a, d_b = cross(a_keep, 1, True), cross(b_keep, -1, True)
+    e_a, e_b = cross(a_give, 1, True, 1), cross(b_give, -1, True, 1)
+    got = swap(give)
+    sums = jax.ShapeDtypeStruct((rows, 4 * width), F32)
+    row_keys, acc_mine, acc_theirs = local(
+        early_kernel, (mine, got, row_own, row_near, row_far),
+        (jax.ShapeDtypeStruct((rows, 2048), BF16), sums, sums), [pltpu.VMEM((4 * width, 2048), BF16)],
+    )
+    ins = (row_keys, acc_mine, acc_theirs, d_a, d_b, e_a, e_b)
+    return call(
+        moment_kernel, [SMEM] + [VMEM] * len(ins), jax.ShapeDtypeStruct((rows, 1, 8 * width), F32), HBM,
+        [
+            pltpu.VMEM((4 * width, 512), BF16),
+            pltpu.VMEM((width, 2048), BF16),
+            pltpu.VMEM((2, rows, 1, 4 * width), F32),
+            pltpu.SemaphoreType.DMA((2,)),
         ],
-        input_output_aliases={1: 1},
-        compiler_params=pltpu.CompilerParams(vmem_limit_bytes=16 * MIB),
-        cost_estimate=pl.CostEstimate(flops=4 * flops, bytes_accessed=4 * MIB, transcendentals=0),
-    )(place, cols, own_x2a, own_x2b, far_y2a, far_y2b, r0, r1, s0, s1)[0]
+        16 * MIB, flops, place, *ins,
+    )
 
 
 def solution(mesh):

time: 121 us -> 117 us (0.967)
  starting transfers between devices: 53.7 us -> 43.2 us
  waiting for transfers between devices: 37.6 us -> 41.5 us
  Pallas kernels: 27.2 us -> 29.2 us
    ppermute x21 -> x9, starting transfers between devices: 43.4 us -> 19.8 us  [shift(): return lax.ppermute(value, axis, [(i, (i + by) % n) for i in range(n)])]
    ppermute x2 -> x12, waiting for transfers between devices: 0.01 us -> 20.7 us  [the longest x3 13.1 us: apart(): lax.ppermute(v, (axis, 'c'), [(i * 2 + e, (i + 1 - 2 * e) % 4 * 2 + e) fo...]
    ppermute x21 -> x9, waiting for transfers between devices: 37.6 us -> 20.8 us  [shift(): return lax.ppermute(value, axis, [(i, (i + by) % n) for i in range(n)])]
    ppermute x2 -> x12, starting transfers between devices: 10.3 us -> 23.4 us  [the longest x9 14.5 us: cross(): return lax.ppermute(v, ('y', 'x', 'c'), pairs)]
    pallas_call x5 -> x10, Pallas kernels: 18.5 us -> 29.2 us  [call(): pl.pallas_call(kernel, in_specs=in_specs, out_specs=out_specs, out_shape=...]
    pallas_call x2 -> x0, Pallas kernels: 8.72 us -> none  [the longest x1 7.27 us: shards(): pl.pallas_call(moment_kernel, in_specs=[SMEM] + [VMEM] * 9, out_specs=(HB...]
  transfers between devices with their start and end apart: 23 -> 21, of which waited for: 7 -> 11; matrix products, arithmetic and copies ran while one was open for 0% -> 0% of each run, Pallas kernels for 12% -> 15%
where the time goes in v2:
time: 117 us; the launch traced here: 114 us
  starting transfers between devices  43.2 us (37%)
  waiting for transfers between devices  41.5 us (35%)
  Pallas kernels  29.2 us (25%)
    pallas_call x10, Pallas kernels, call(): pl.pallas_call(kernel, in_specs=in_specs, out_specs=out_specs, out_shape=...  29.2 us
    ppermute x9, waiting for transfers between devices, shift(): return lax.ppermute(value, axis, [(i, (i + by) % n) for i in range(n)])  20.8 us
    ppermute x9, starting transfers between devices, shift(): return lax.ppermute(value, axis, [(i, (i + by) % n) for i in range(n)])  19.8 us
    ppermute x9, starting transfers between devices, cross(): return lax.ppermute(v, ('y', 'x', 'c'), pairs)  14.5 us
    ppermute x3, waiting for transfers between devices, apart(): lax.ppermute(v, (axis, 'c'), [(i * 2 + e, (i + 1 - 2 * e) % 4 * 2 + e) fo...  13.1 us
    ppermute x3, starting transfers between devices, apart(): lax.ppermute(v, (axis, 'c'), [(i * 2 + e, (i + 1 - 2 * e) % 4 * 2 + e) fo...  8.98 us
    ppermute x9, waiting for transfers between devices, cross(): return lax.ppermute(v, ('y', 'x', 'c'), pairs)  7.59 us
  transfers between devices with their start and end apart: 21, of which 11 were waited for; matrix products, arithmetic and copies ran while one was open for 0% of the time, Pallas kernels for 15%

profile of v2, /device:TPU:1, one launch (start us, length us, event | category | flops | bytes accessed | tf_op | source)
XLA Modules:
  0.0 114.4 jit_solution(18374956865243494999)
XLA Ops:
  0.0 4.9 %shard_map.46 = (bf16[448,2048]{1,0:T(8,128)(2,1)}, bf16[464,512]{1,0:T(8,128)(2,1)}) custom-call(s32[1]{0:T(128)} %bitcast.6.idx_ref, f32[1,2048]{1,0:T(1,128)} %bitcast.14, bf16[224,2048]{1,0:T(8,128)(2,1)} %bitcast.12, bf16[224,2048]{1,0:T(8,128)(2,1)} %bitcast.13, bf16[2048,2048]{1,0:T(8,128)(2,1)} %h_ref.5), custom_call_target="tpu_custom_call" | custom-call | flops 939524096 | bytes 2097152 | tf_op jit(solution)/shard_map/pallas_call | solution.py:271
  4.9 3.7 %collective-permute-start.1 = (bf16[464,512]{1,0:T(8,128)(2,1)}, bf16[464,512]{1,0:T(8,128)(2,1)S(1)}, u32[]{:S(2)}, u32[]{:S(2)}) collective-permute-start(bf16[464,512]{1,0:T(8,128)(2,1)} %get-tuple-element.24), channel_id=1, source_target_pairs={{0,16},{8,24},{16,0},{24,8},{1,17},{9,25},{17,1},{25,9},{2,18},{10... | collective-permute-start | bytes 1425416 | tf_op jit(solution)/shard_map/ppermute | solution.py:18
  8.7 6.2 %shard_map.48 = (bf16[464,512]{1,0:T(8,128)(2,1)S(1)}, bf16[464,512]{1,0:T(8,128)(2,1)S(1)}) custom-call(s32[2]{0:T(128)S(1)} %pad_add_fusion.idx_ref, bf16[448,2048]{1,0:T(8,128)(2,1)} %get-tuple-element.22.w_ref, bf16[2048,2048]{1,0:T(8,128)(2,1)} %h_ref.5), custom_call_target="tpu_custom_call" | custom-call | flops 1879048192 | bytes 2097152 | tf_op jit(solution)/shard_map/pallas_call | solution.py:271
  15.3 2.4 %collective-permute-start.2 = (bf16[464,512]{1,0:T(8,128)(2,1)S(1)}, bf16[464,512]{1,0:T(8,128)(2,1)S(1)}, u32[]{:S(2)}, u32[]{:S(2)}) collective-permute-start(bf16[464,512]{1,0:T(8,128)(2,1)S(1)} %get-tuple-element.25), channel_id=1, source_target_pairs={{0,24},{8,0},{16,8},{24,16},{1,25},{9,1},{17,9},{25,17},{2,26},{10... | collective-permute-start | bytes 1425416 | tf_op jit(solution)/shard_map/ppermute | solution.py:18
  17.6 4.5 %shard_map.47.own_ref = f32[456,512]{1,0:T(8,128)S(1)} custom-call(s32[1]{0:T(128)} %bitcast.5.idx_ref, bf16[448,2048]{1,0:T(8,128)(2,1)} %get-tuple-element.22.w_ref, bf16[2048,2048]{1,0:T(8,128)(2,1)} %h_ref.5), custom_call_target="tpu_custom_call" | custom-call | flops 939524096 | bytes 2097152 | tf_op jit(solution)/shard_map/pallas_call | solution.py:271
  22.1 7.8 %collective-permute-done.p_ref = bf16[464,512]{1,0:T(8,128)(2,1)S(1)} collective-permute-done((bf16[464,512]{1,0:T(8,128)(2,1)S(1)}, bf16[464,512]{1,0:T(8,128)(2,1)S(1)}, u32[]{:S(2)}, u32[]{:S(2)}) %collective-permute-start) | collective-permute-done | bytes 475168 | tf_op jit(solution)/shard_map/ppermute | solution.py:18
  31.1 1.9 %collective-permute-start.4 = (bf16[224,512]{1,0:T(8,128)(2,1)S(1)}, bf16[224,512]{1,0:T(8,128)(2,1)S(1)}, u32[]{:S(2)}, u32[]{:S(2)}) collective-permute-start(bf16[224,512]{1,0:T(8,128)(2,1)S(1)} %shard_map.49.k_ref), channel_id=1, source_target_pairs={{0,128},{128,0},{1,129},{129,1},{2,130},{130,2},{3,131},{131,3},{4... | collective-permute-start | bytes 688136 | tf_op jit(solution)/shard_map/ppermute | solution.py:18
  33.0 1.3 %collective-permute-start.3 = (bf16[224,512]{1,0:T(8,128)(2,1)S(1)}, bf16[224,512]{1,0:T(8,128)(2,1)S(1)}, u32[]{:S(2)}, u32[]{:S(2)}) collective-permute-start(bf16[224,512]{1,0:T(8,128)(2,1)S(1)} %shard_map.49.k_ref), channel_id=1, source_target_pairs={{0,1},{1,0},{2,3},{3,2},{4,5},{5,4},{6,7},{7,6},{8,9},{9,8},{10,11... | collective-permute-start | bytes 688136 | tf_op jit(solution)/shard_map/ppermute | solution.py:18
  34.3 3.5 %collective-permute-done.4.p_ref = bf16[224,512]{1,0:T(8,128)(2,1)S(1)} collective-permute-done((bf16[224,512]{1,0:T(8,128)(2,1)S(1)}, bf16[224,512]{1,0:T(8,128)(2,1)S(1)}, u32[]{:S(2)}, u32[]{:S(2)}) %collective-permute-start.4) | collective-permute-done | bytes 229408 | tf_op jit(solution)/shard_map/ppermute | solution.py:18
  37.7 1.8 %collective-permute-start.5 = (bf16[224,512]{1,0:T(8,128)(2,1)S(1)}, bf16[224,512]{1,0:T(8,128)(2,1)S(1)}, u32[]{:S(2)}, u32[]{:S(2)}) collective-permute-start(bf16[224,512]{1,0:T(8,128)(2,1)S(1)} %collective-permute-done.4.p_ref), channel_id=1, source_target_pairs={{0,1},{1,0},{2,3},{3,2},{4,5},{5,4},{6,7},{7,6},{8,9},{9,8},{10,11... | collective-permute-start | bytes 688136 | tf_op jit(solution)/shard_map/ppermute | solution.py:18
  39.6 5.9 %collective-permute-start.9 = (bf16[448,512]{1,0:T(8,128)(2,1)S(1)}, bf16[448,512]{1,0:T(8,128)(2,1)S(1)}, u32[]{:S(2)}, u32[]{:S(2)}) collective-permute-start(bf16[448,512]{1,0:T(8,128)(2,1)S(1)} %pad_maximum_fusion.1), channel_id=1, source_target_pairs={{0,2},{1,7},{2,4},{3,1},{4,6},{5,3},{6,0},{7,5},{8,10},{9,15},{10,... | collective-permute-start | bytes 1376264 | tf_op jit(solution)/shard_map/ppermute | solution.py:338
  46.1 3.3 %collective-permute-start.8 = (bf16[448,512]{1,0:T(8,128)(2,1)S(1)}, bf16[448,512]{1,0:T(8,128)(2,1)S(1)}, u32[]{:S(2)}, u32[]{:S(2)}) collective-permute-start(bf16[448,512]{1,0:T(8,128)(2,1)S(1)} %shard_map.50.refs_0_), channel_id=1, source_target_pairs={{0,64},{1,17},{8,72},{9,25},{16,80},{17,1},{24,88},{25,9},{32,96},... | collective-permute-start | bytes 1376264 | tf_op jit(solution)/shard_map/ppermute | solution.py:335
  49.5 2.7 %collective-permute-start.6 = (bf16[448,512]{1,0:T(8,128)(2,1)S(1)}, bf16[448,512]{1,0:T(8,128)(2,1)S(1)}, u32[]{:S(2)}, u32[]{:S(2)}) collective-permute-start(bf16[448,512]{1,0:T(8,128)(2,1)S(1)} %shard_map.50.refs_0_), channel_id=1, source_target_pairs={{0,96},{1,25},{8,104},{9,1},{16,112},{17,9},{24,120},{25,17},{32,0... | collective-permute-start | bytes 1376264 | tf_op jit(solution)/shard_map/ppermute | solution.py:335
  52.1 3.8 %collective-permute-done.9.near = bf16[448,512]{1,0:T(8,128)(2,1)S(1)} collective-permute-done((bf16[448,512]{1,0:T(8,128)(2,1)S(1)}, bf16[448,512]{1,0:T(8,128)(2,1)S(1)}, u32[]{:S(2)}, u32[]{:S(2)}) %collective-permute-start.9) | collective-permute-done | bytes 458784 | tf_op jit(solution)/shard_map/ppermute | solution.py:338
  55.9 4.3 %collective-permute-done.7.refs_2_ = bf16[448,512]{1,0:T(8,128)(2,1)S(1)} collective-permute-done((bf16[448,512]{1,0:T(8,128)(2,1)S(1)}, bf16[448,512]{1,0:T(8,128)(2,1)S(1)}, u32[]{:S(2)}, u32[]{:S(2)}) %collective-permute-start.7) | collective-permute-done | bytes 458784 | tf_op jit(solution)/shard_map/ppermute | solution.py:335
  60.4 1.4 %collective-permute-start.11 = (bf16[1792,512]{1,0:T(8,128)(2,1)S(1)}, bf16[1792,512]{1,0:T(8,128)(2,1)S(1)}, u32[]{:S(2)}, u32[]{:S(2)}) collective-permute-start(bf16[1792,512]{1,0:T(8,128)(2,1)S(1)} %shard_map.51.q_ref), channel_id=1, source_target_pairs={{0,8},{1,33},{8,16},{9,41},{16,24},{17,49},{24,0},{25,57},{32,40},... | collective-permute-start | bytes 5505032 | tf_op jit(solution)/shard_map/ppermute | solution.py:335
  61.7 1.5 %collective-permute-start.10 = (bf16[1792,512]{1,0:T(8,128)(2,1)S(1)}, bf16[1792,512]{1,0:T(8,128)(2,1)S(1)}, u32[]{:S(2)}, u32[]{:S(2)}) collective-permute-start(bf16[1792,512]{1,0:T(8,128)(2,1)S(1)} %shard_map.51.q_ref), channel_id=1, source_target_pairs={{0,24},{1,97},{8,0},{9,105},{16,8},{17,113},{24,16},{25,121},{32,5... | collective-permute-start | bytes 5505032 | tf_op jit(solution)/shard_map/ppermute | solution.py:335
  63.3 1.5 %collective-permute-start.12 = (bf16[224,512]{1,0:T(8,128)(2,1)S(1)}, bf16[224,512]{1,0:T(8,128)(2,1)S(1)}, u32[]{:S(2)}, u32[]{:S(2)}) collective-permute-start(bf16[224,512]{1,0:T(8,128)(2,1)S(1)} %slice.4), channel_id=1, source_target_pairs={{0,2},{1,7},{2,4},{3,1},{4,6},{5,3},{6,0},{7,5},{8,10},{9,15},{10,... | collective-permute-start | bytes 688136 | tf_op jit(solution)/shard_map/ppermute | solution.py:338
  64.8 7.1 %collective-permute-done.12.far = bf16[224,512]{1,0:T(8,128)(2,1)S(1)} collective-permute-done((bf16[224,512]{1,0:T(8,128)(2,1)S(1)}, bf16[224,512]{1,0:T(8,128)(2,1)S(1)}, u32[]{:S(2)}, u32[]{:S(2)}) %collective-permute-start.12) | collective-permute-done | bytes 229408 | tf_op jit(solution)/shard_map/ppermute | solution.py:338
  72.9 1.8 %collective-permute-done.13.got = bf16[672,512]{1,0:T(8,128)(2,1)S(1)} collective-permute-done((bf16[672,512]{1,0:T(8,128)(2,1)S(1)}, bf16[672,512]{1,0:T(8,128)(2,1)S(1)}, u32[]{:S(2)}, u32[]{:S(2)}) %collective-permute-start.13) | collective-permute-done | bytes 688160 | tf_op jit(solution)/shard_map/ppermute | solution.py:18
  75.4 1.5 %collective-permute-start.14 = (bf16[448,512]{1,0:T(8,128)(2,1)S(1)}, bf16[448,512]{1,0:T(8,128)(2,1)S(1)}, u32[]{:S(2)}, u32[]{:S(2)}) collective-permute-start(bf16[448,512]{1,0:T(8,128)(2,1)S(1)} %get-tuple-element.27), channel_id=1, source_target_pairs={{0,8},{1,25},{8,16},{9,1},{16,24},{17,9},{24,0},{25,17},{2,10},{3,... | collective-permute-start | bytes 1376264 | tf_op jit(solution)/shard_map/ppermute | solution.py:338
  77.0 1.3 %collective-permute-start.15 = (bf16[224,512]{1,0:T(8,128)(2,1)S(1)}, bf16[224,512]{1,0:T(8,128)(2,1)S(1)}, u32[]{:S(2)}, u32[]{:S(2)}) collective-permute-start(bf16[224,512]{1,0:T(8,128)(2,1)S(1)} %get-tuple-element.28), channel_id=1, source_target_pairs={{0,16},{8,24},{16,0},{24,8},{1,17},{9,25},{17,1},{25,9},{2,18},{10... | collective-permute-start | bytes 688136 | tf_op jit(solution)/shard_map/ppermute | solution.py:18
  78.3 7.6 %collective-permute-done.15.far = bf16[224,512]{1,0:T(8,128)(2,1)S(1)} collective-permute-done((bf16[224,512]{1,0:T(8,128)(2,1)S(1)}, bf16[224,512]{1,0:T(8,128)(2,1)S(1)}, u32[]{:S(2)}, u32[]{:S(2)}) %collective-permute-start.15) | collective-permute-done | bytes 229408 | tf_op jit(solution)/shard_map/ppermute | solution.py:18
  85.9 2.3 %collective-permute-done.14.near = bf16[448,512]{1,0:T(8,128)(2,1)S(1)} collective-permute-done((bf16[448,512]{1,0:T(8,128)(2,1)S(1)}, bf16[448,512]{1,0:T(8,128)(2,1)S(1)}, u32[]{:S(2)}, u32[]{:S(2)}) %collective-permute-start.14) | collective-permute-done | bytes 458784 | tf_op jit(solution)/shard_map/ppermute | solution.py:338
  88.1 1.2 %shard_map.53 = (bf16[896,2048]{1,0:T(8,128)(2,1)S(1)}, bf16[448,512]{1,0:T(8,128)(2,1)S(1)}, bf16[448,512]{1,0:T(8,128)(2,1)S(1)}, bf16[448,512]{1,0:T(8,128)(2...) custom-call(s32[5]{0:T(128)S(1)} %stack.38.idx_ref, bf16[1792,512]{1,0:T(8,128)(2,1)S(1)} %shard_map.51.q_ref, ...), custom_call_target="tpu_custom_call" | custom-call | flops 234881024 | bytes 2097152 | tf_op jit(solution)/shard_map/pallas_call | solution.py:271
  89.3 6.1 %collective-permute-start.16 = (bf16[3360,512]{1,0:T(8,128)(2,1)S(1)}, bf16[3360,512]{1,0:T(8,128)(2,1)S(1)}, u32[]{:S(2)}, u32[]{:S(2)}) collective-permute-start(bf16[3360,512]{1,0:T(8,128)(2,1)S(1)} %get-tuple-element.30), channel_id=1, source_target_pairs={{0,1},{1,0},{2,3},{3,2},{4,5},{5,4},{6,7},{7,6},{8,9},{9,8},{10,11... | collective-permute-start | bytes 10321928 | tf_op jit(solution)/shard_map/ppermute | solution.py:18
  96.5 1.6 %collective-permute-start.18 = (bf16[448,512]{1,0:T(8,128)(2,1)S(1)}, bf16[448,512]{1,0:T(8,128)(2,1)S(1)}, u32[]{:S(2)}, u32[]{:S(2)}) collective-permute-start(bf16[448,512]{1,0:T(8,128)(2,1)S(1)} %get-tuple-element.36), channel_id=1, source_target_pairs={{0,24},{1,97},{8,0},{9,105},{16,8},{17,113},{24,16},{25,121},{32,5... | collective-permute-start | bytes 1376264 | tf_op jit(solution)/shard_map/ppermute | solution.py:335
  98.1 1.6 %collective-permute-start.19 = (bf16[448,512]{1,0:T(8,128)(2,1)S(1)}, bf16[448,512]{1,0:T(8,128)(2,1)S(1)}, u32[]{:S(2)}, u32[]{:S(2)}) collective-permute-start(bf16[448,512]{1,0:T(8,128)(2,1)S(1)} %get-tuple-element.37), channel_id=1, source_target_pairs={{0,9},{1,32},{8,17},{9,40},{16,25},{17,48},{24,1},{25,56},{32,41},... | collective-permute-start | bytes 1376264 | tf_op jit(solution)/shard_map/ppermute | solution.py:335
  99.7 1.3 %collective-permute-start.20 = (bf16[448,512]{1,0:T(8,128)(2,1)S(1)}, bf16[448,512]{1,0:T(8,128)(2,1)S(1)}, u32[]{:S(2)}, u32[]{:S(2)}) collective-permute-start(bf16[448,512]{1,0:T(8,128)(2,1)S(1)} %get-tuple-element.38), channel_id=1, source_target_pairs={{0,25},{1,96},{8,1},{9,104},{16,9},{17,112},{24,17},{25,120},{32,5... | collective-permute-start | bytes 1376264 | tf_op jit(solution)/shard_map/ppermute | solution.py:335
  101.2 5.1 %shard_map.54 = (bf16[448,2048]{1,0:T(8,128)(2,1)S(1)}, f32[448,896]{1,0:T(8,128)S(1)}, f32[448,896]{1,0:T(8,128)S(1)}) custom-call(s32[5]{0:T(128)S(1)} %stack.38.idx_ref, bf16[896,2048]{1,0:T(8,128)(2,1)S(1)} %get-tuple-element.29.mine, bf16[3360,512]{1,0:T(8,128)(2,1)S(1)} %collective-permute-done.16.got, bf16[448,512]{1,0:T(8,128)(2,1)S(1)} %get-tuple-element.31.row_own, ...), custom_call_target="tpu_custom_call" | custom-call | flops 234881024 | bytes 2097152 | tf_op jit(solution)/shard_map/pallas_call | solution.py:271
  106.3 3.1 %collective-permute-done.19.e_a = bf16[448,512]{1,0:T(8,128)(2,1)S(1)} collective-permute-done((bf16[448,512]{1,0:T(8,128)(2,1)S(1)}, bf16[448,512]{1,0:T(8,128)(2,1)S(1)}, u32[]{:S(2)}, u32[]{:S(2)}) %collective-permute-start.19) | collective-permute-done | bytes 458784 | tf_op jit(solution)/shard_map/ppermute | solution.py:335
  109.5 4.7 %shard_map.55 = f32[448,1,1792]{2,1,0:T(1,128)} custom-call(s32[5]{0:T(128)S(1)} %stack.38.idx_ref, bf16[448,2048]{1,0:T(8,128)(2,1)S(1)} %get-tuple-element.32.r_ref, f32[448,896]{1,0:T(8,128)S(1)} %get-tuple-element.33.acc_mine, f32[448,896]{1,0:T(8,128)S(1)} %get-tuple-element.34.acc_theirs, bf16[448,512]{1,0:T(8,128)(2,1)S(1)} %collective-permute-done.17.d_a, ...), custom_call_target="tpu_custom_call" | custom-call | flops 939524096 | bytes 2097152 | tf_op jit(solution)/shard_map/pallas_call | solution.py:271
  (25 shorter events, 5.6 us)
Async XLA Ops:
  4.9 17.2 %collective-permute-start.1 = (bf16[464,512]{1,0:T(8,128)(2,1)}, bf16[464,512]{1,0:T(8,128)(2,1)S(1)}, u32[]{:S(2)}, u32[]{:S(2)}) collective-permute-start(bf16[464,512]{1,0:T(8,128)(2,1)} %get-tuple-element.24), channel_id=1, source_target_pairs={{0,16},{8,24},{16,0},{24,8},{1,17},{9,25},{17,1},{25,9},{2,18},{10... | collective-permute-start | bytes 1425416 | tf_op jit(solution)/shard_map/ppermute | solution.py:18
  14.9 15.0 %collective-permute-start = (bf16[464,512]{1,0:T(8,128)(2,1)S(1)}, bf16[464,512]{1,0:T(8,128)(2,1)S(1)}, u32[]{:S(2)}, u32[]{:S(2)}) collective-permute-start(bf16[464,512]{1,0:T(8,128)(2,1)S(1)} %get-tuple-element.23), channel_id=1, source_target_pairs={{0,8},{8,16},{16,24},{24,0},{1,9},{9,17},{17,25},{25,1},{2,10},{10... | collective-permute-start | bytes 1425416 | tf_op jit(solution)/shard_map/ppermute | solution.py:18
  15.3 14.7 %collective-permute-start.2 = (bf16[464,512]{1,0:T(8,128)(2,1)S(1)}, bf16[464,512]{1,0:T(8,128)(2,1)S(1)}, u32[]{:S(2)}, u32[]{:S(2)}) collective-permute-start(bf16[464,512]{1,0:T(8,128)(2,1)S(1)} %get-tuple-element.25), channel_id=1, source_target_pairs={{0,24},{8,0},{16,8},{24,16},{1,25},{9,1},{17,9},{25,17},{2,26},{10... | collective-permute-start | bytes 1425416 | tf_op jit(solution)/shard_map/ppermute | solution.py:18
  31.1 6.7 %collective-permute-start.4 = (bf16[224,512]{1,0:T(8,128)(2,1)S(1)}, bf16[224,512]{1,0:T(8,128)(2,1)S(1)}, u32[]{:S(2)}, u32[]{:S(2)}) collective-permute-start(bf16[224,512]{1,0:T(8,128)(2,1)S(1)} %shard_map.49.k_ref), channel_id=1, source_target_pairs={{0,128},{128,0},{1,129},{129,1},{2,130},{130,2},{3,131},{131,3},{4... | collective-permute-start | bytes 688136 | tf_op jit(solution)/shard_map/ppermute | solution.py:18
  33.0 6.6 %collective-permute-start.3 = (bf16[224,512]{1,0:T(8,128)(2,1)S(1)}, bf16[224,512]{1,0:T(8,128)(2,1)S(1)}, u32[]{:S(2)}, u32[]{:S(2)}) collective-permute-start(bf16[224,512]{1,0:T(8,128)(2,1)S(1)} %shard_map.49.k_ref), channel_id=1, source_target_pairs={{0,1},{1,0},{2,3},{3,2},{4,5},{5,4},{6,7},{7,6},{8,9},{9,8},{10,11... | collective-permute-start | bytes 688136 | tf_op jit(solution)/shard_map/ppermute | solution.py:18
  37.7 7.8 %collective-permute-start.5 = (bf16[224,512]{1,0:T(8,128)(2,1)S(1)}, bf16[224,512]{1,0:T(8,128)(2,1)S(1)}, u32[]{:S(2)}, u32[]{:S(2)}) collective-permute-start(bf16[224,512]{1,0:T(8,128)(2,1)S(1)} %collective-permute-done.4.p_ref), channel_id=1, source_target_pairs={{0,1},{1,0},{2,3},{3,2},{4,5},{5,4},{6,7},{7,6},{8,9},{9,8},{10,11... | collective-permute-start | bytes 688136 | tf_op jit(solution)/shard_map/ppermute | solution.py:18
  39.6 16.3 %collective-permute-start.9 = (bf16[448,512]{1,0:T(8,128)(2,1)S(1)}, bf16[448,512]{1,0:T(8,128)(2,1)S(1)}, u32[]{:S(2)}, u32[]{:S(2)}) collective-permute-start(bf16[448,512]{1,0:T(8,128)(2,1)S(1)} %pad_maximum_fusion.1), channel_id=1, source_target_pairs={{0,2},{1,7},{2,4},{3,1},{4,6},{5,3},{6,0},{7,5},{8,10},{9,15},{10,... | collective-permute-start | bytes 1376264 | tf_op jit(solution)/shard_map/ppermute | solution.py:338
  46.1 9.7 %collective-permute-start.8 = (bf16[448,512]{1,0:T(8,128)(2,1)S(1)}, bf16[448,512]{1,0:T(8,128)(2,1)S(1)}, u32[]{:S(2)}, u32[]{:S(2)}) collective-permute-start(bf16[448,512]{1,0:T(8,128)(2,1)S(1)} %shard_map.50.refs_0_), channel_id=1, source_target_pairs={{0,64},{1,17},{8,72},{9,25},{16,80},{17,1},{24,88},{25,9},{32,96},... | collective-permute-start | bytes 1376264 | tf_op jit(solution)/shard_map/ppermute | solution.py:335
  49.5 10.8 %collective-permute-start.7 = (bf16[448,512]{1,0:T(8,128)(2,1)S(1)}, bf16[448,512]{1,0:T(8,128)(2,1)S(1)}, u32[]{:S(2)}, u32[]{:S(2)}) collective-permute-start(bf16[448,512]{1,0:T(8,128)(2,1)S(1)} %shard_map.50.refs_0_), channel_id=1, source_target_pairs={{0,32},{1,9},{8,40},{9,17},{16,48},{17,25},{24,56},{25,1},{32,64},... | collective-permute-start | bytes 1376264 | tf_op jit(solution)/shard_map/ppermute | solution.py:335
  49.5 10.8 %collective-permute-start.6 = (bf16[448,512]{1,0:T(8,128)(2,1)S(1)}, bf16[448,512]{1,0:T(8,128)(2,1)S(1)}, u32[]{:S(2)}, u32[]{:S(2)}) collective-permute-start(bf16[448,512]{1,0:T(8,128)(2,1)S(1)} %shard_map.50.refs_0_), channel_id=1, source_target_pairs={{0,96},{1,25},{8,104},{9,1},{16,112},{17,9},{24,120},{25,17},{32,0... | collective-permute-start | bytes 1376264 | tf_op jit(solution)/shard_map/ppermute | solution.py:335
  60.4 27.8 %collective-permute-start.11 = (bf16[1792,512]{1,0:T(8,128)(2,1)S(1)}, bf16[1792,512]{1,0:T(8,128)(2,1)S(1)}, u32[]{:S(2)}, u32[]{:S(2)}) collective-permute-start(bf16[1792,512]{1,0:T(8,128)(2,1)S(1)} %shard_map.51.q_ref), channel_id=1, source_target_pairs={{0,8},{1,33},{8,16},{9,41},{16,24},{17,49},{24,0},{25,57},{32,40},... | collective-permute-start | bytes 5505032 | tf_op jit(solution)/shard_map/ppermute | solution.py:335
  61.7 26.4 %collective-permute-start.10 = (bf16[1792,512]{1,0:T(8,128)(2,1)S(1)}, bf16[1792,512]{1,0:T(8,128)(2,1)S(1)}, u32[]{:S(2)}, u32[]{:S(2)}) collective-permute-start(bf16[1792,512]{1,0:T(8,128)(2,1)S(1)} %shard_map.51.q_ref), channel_id=1, source_target_pairs={{0,24},{1,97},{8,0},{9,105},{16,8},{17,113},{24,16},{25,121},{32,5... | collective-permute-start | bytes 5505032 | tf_op jit(solution)/shard_map/ppermute | solution.py:335
  63.3 8.6 %collective-permute-start.12 = (bf16[224,512]{1,0:T(8,128)(2,1)S(1)}, bf16[224,512]{1,0:T(8,128)(2,1)S(1)}, u32[]{:S(2)}, u32[]{:S(2)}) collective-permute-start(bf16[224,512]{1,0:T(8,128)(2,1)S(1)} %slice.4), channel_id=1, source_target_pairs={{0,2},{1,7},{2,4},{3,1},{4,6},{5,3},{6,0},{7,5},{8,10},{9,15},{10,... | collective-permute-start | bytes 688136 | tf_op jit(solution)/shard_map/ppermute | solution.py:338
  71.9 2.8 %collective-permute-start.13 = (bf16[672,512]{1,0:T(8,128)(2,1)S(1)}, bf16[672,512]{1,0:T(8,128)(2,1)S(1)}, u32[]{:S(2)}, u32[]{:S(2)}) collective-permute-start(bf16[672,512]{1,0:T(8,128)(2,1)S(1)} %pad_maximum_fusion), channel_id=1, source_target_pairs={{0,1},{1,0},{2,3},{3,2},{4,5},{5,4},{6,7},{7,6},{8,9},{9,8},{10,11... | collective-permute-start | bytes 2064392 | tf_op jit(solution)/shard_map/ppermute | solution.py:18
  75.4 12.7 %collective-permute-start.14 = (bf16[448,512]{1,0:T(8,128)(2,1)S(1)}, bf16[448,512]{1,0:T(8,128)(2,1)S(1)}, u32[]{:S(2)}, u32[]{:S(2)}) collective-permute-start(bf16[448,512]{1,0:T(8,128)(2,1)S(1)} %get-tuple-element.27), channel_id=1, source_target_pairs={{0,8},{1,25},{8,16},{9,1},{16,24},{17,9},{24,0},{25,17},{2,10},{3,... | collective-permute-start | bytes 1376264 | tf_op jit(solution)/shard_map/ppermute | solution.py:338
  77.0 8.9 %collective-permute-start.15 = (bf16[224,512]{1,0:T(8,128)(2,1)S(1)}, bf16[224,512]{1,0:T(8,128)(2,1)S(1)}, u32[]{:S(2)}, u32[]{:S(2)}) collective-permute-start(bf16[224,512]{1,0:T(8,128)(2,1)S(1)} %get-tuple-element.28), channel_id=1, source_target_pairs={{0,16},{8,24},{16,0},{24,8},{1,17},{9,25},{17,1},{25,9},{2,18},{10... | collective-permute-start | bytes 688136 | tf_op jit(solution)/shard_map/ppermute | solution.py:18
  89.3 11.8 %collective-permute-start.16 = (bf16[3360,512]{1,0:T(8,128)(2,1)S(1)}, bf16[3360,512]{1,0:T(8,128)(2,1)S(1)}, u32[]{:S(2)}, u32[]{:S(2)}) collective-permute-start(bf16[3360,512]{1,0:T(8,128)(2,1)S(1)} %get-tuple-element.30), channel_id=1, source_target_pairs={{0,1},{1,0},{2,3},{3,2},{4,5},{5,4},{6,7},{7,6},{8,9},{9,8},{10,11... | collective-permute-start | bytes 10321928 | tf_op jit(solution)/shard_map/ppermute | solution.py:18
  95.4 10.9 %collective-permute-start.17 = (bf16[448,512]{1,0:T(8,128)(2,1)S(1)}, bf16[448,512]{1,0:T(8,128)(2,1)S(1)}, u32[]{:S(2)}, u32[]{:S(2)}) collective-permute-start(bf16[448,512]{1,0:T(8,128)(2,1)S(1)} %get-tuple-element.35), channel_id=1, source_target_pairs={{0,8},{1,33},{8,16},{9,41},{16,24},{17,49},{24,0},{25,57},{32,40},... | collective-permute-start | bytes 1376264 | tf_op jit(solution)/shard_map/ppermute | solution.py:335
  96.5 9.8 %collective-permute-start.18 = (bf16[448,512]{1,0:T(8,128)(2,1)S(1)}, bf16[448,512]{1,0:T(8,128)(2,1)S(1)}, u32[]{:S(2)}, u32[]{:S(2)}) collective-permute-start(bf16[448,512]{1,0:T(8,128)(2,1)S(1)} %get-tuple-element.36), channel_id=1, source_target_pairs={{0,24},{1,97},{8,0},{9,105},{16,8},{17,113},{24,16},{25,121},{32,5... | collective-permute-start | bytes 1376264 | tf_op jit(solution)/shard_map/ppermute | solution.py:335
  98.1 11.3 %collective-permute-start.19 = (bf16[448,512]{1,0:T(8,128)(2,1)S(1)}, bf16[448,512]{1,0:T(8,128)(2,1)S(1)}, u32[]{:S(2)}, u32[]{:S(2)}) collective-permute-start(bf16[448,512]{1,0:T(8,128)(2,1)S(1)} %get-tuple-element.37), channel_id=1, source_target_pairs={{0,9},{1,32},{8,17},{9,40},{16,25},{17,48},{24,1},{25,56},{32,41},... | collective-permute-start | bytes 1376264 | tf_op jit(solution)/shard_map/ppermute | solution.py:335
  99.7 9.8 %collective-permute-start.20 = (bf16[448,512]{1,0:T(8,128)(2,1)S(1)}, bf16[448,512]{1,0:T(8,128)(2,1)S(1)}, u32[]{:S(2)}, u32[]{:S(2)}) collective-permute-start(bf16[448,512]{1,0:T(8,128)(2,1)S(1)} %get-tuple-element.38), channel_id=1, source_target_pairs={{0,25},{1,96},{8,1},{9,104},{16,9},{17,112},{24,17},{25,120},{32,5... | collective-permute-start | bytes 1376264 | tf_op jit(solution)/shard_map/ppermute | solution.py:335

commit v3 on v2

--- a/solution.py
+++ b/solution.py
@@ -147,10 +147,12 @@
             b_ref[width:, :] = second[...]
 
 
-def pack_kernel(*refs):
-    size = refs[0].shape[0]
-    for i, ref in enumerate(refs[:4]):
-        refs[4][i * size : (i + 1) * size, :] = ref[...]
+def pack_kernel(base, p1_ref, p3_ref, p2_ref, q_ref, keep, give):
+    size = p1_ref.shape[0]
+    for i, ref in enumerate((base, p1_ref, p3_ref, p2_ref)):
+        q_ref[i * size : (i + 1) * size, :] = ref[...]
+    keep[...] = p2_ref[0 : size // 2, :]
+    give[...] = p2_ref[size // 2 :, :]
 
 
 def clear(cols, idx_ref, role):
@@ -166,21 +168,30 @@
         cols[places(lax.rem(y + 2, 4), width), :] = jnp.zeros((width, cols.shape[1]), BF16)
 
 
+REST = ORDER[1:]
+
+
 def mine_kernel(idx_ref, q_ref, up_ref, down_ref, near, far, cols, a_keep, a_give, b_keep, b_give, give):
     width = cols.shape[0] // 4
-    for ref, first, k_ref, g_ref in ((down_ref, 0, a_keep, a_give), (up_ref, 4, b_keep, b_give)):
-        for i in range(2):
-            at = (first + 2 * i) * width
-            k_ref[i * width : (i + 1) * width, :] = ref[at : at + width, :]
-            g_ref[i * width : (i + 1) * width, :] = ref[at + width : at + 2 * width, :]
+
+    def shard(ref, i):
+        return ref[i * width : (i + 1) * width, :]
+
+    a_keep[0:width, :] = shard(down_ref, 2)
+    a_keep[width:, :] = shard(down_ref, 6)
+    a_give[...] = shard(down_ref, 3)
+    b_keep[...] = shard(up_ref, 4)
+    b_give[0:width, :] = shard(up_ref, 5)
+    b_give[width:, :] = shard(up_ref, 7)
     clear(cols, idx_ref, idx_ref[4])
-    for n, (d, ref) in enumerate(((0, q_ref), (1, up_ref), (3, down_ref))):
+    to = 0
+    for d, ref in ((0, q_ref), (1, up_ref), (3, down_ref)):
         put(cols, ref, idx_ref, idx_ref[4], d, ORDER, 0)
         for i in range(4):
-            to, at = (4 * n + i) * width, (2 * i + 1) * width
-            give[to : to + width, :] = ref[at : at + width, :]
-    give[12 * width : 14 * width, :] = near[...]
-    give[14 * width :, :] = far[...]
+            give[to : to + width, :] = shard(ref, 2 * i + 1)
+            to += width
+    give[to : to + 2 * width, :] = near[...]
+    give[to + 2 * width :, :] = far[...]
 
 
 def row_kernel(idx_ref, k_ref, k_other, near, far, got, out_ref, out2_ref, own_ref, buf):
@@ -199,7 +210,7 @@
     own_ref[...] = buf[x]
 
 
-def early_kernel(idx_ref, mine, got, row_own, near, far, r_buf, acc_mine, acc_theirs, theirs):
+def early_kernel(idx_ref, mine_in, got, z_keep, z_give, row_own, near, far, r_buf, acc_mine, acc_theirs, mine, theirs):
     width = mine.shape[0] // 4
     x, c = idx_ref[2], idx_ref[4]
     this, that = places(c, width), places(1 - c, width)
@@ -215,6 +226,8 @@
     clear(theirs, idx_ref, 1 - c)
     for n, d in enumerate((0, 1, 3)):
         put(theirs, got.at[4 * n * width : 4 * (n + 1) * width], idx_ref, 1 - c, d, ORDER, 0, 1)
+    put(theirs, z_keep, idx_ref, 1 - c, 2, (0,), 0, 1)
+    put(mine, z_give, idx_ref, c, 2, (0,), 0, 1)
     acc_mine[...] = lax.dot_general(r_buf[...], mine[...], NT, preferred_element_type=F32)
     acc_theirs[...] = lax.dot_general(r_buf[...], theirs[...], NT, preferred_element_type=F32)
 
@@ -224,19 +237,22 @@
     zl, y, x, c = idx_ref[0], idx_ref[1], idx_ref[2], idx_ref[4]
     unit = 1.0 / r_ref.shape[1]
     copies = []
+    where = (((0, 0), (1, 0), (0, 1)), ((0, 0), (1, 0), (1, 1)))
     for n, (acc, role, a, b) in enumerate(((acc_mine, c, d_a, d_b), (acc_theirs, 1 - c, e_a, e_b))):
-        shards = [ref[i * width : (i + 1) * width, :] for ref in (a, b) for i in range(2)]
+        shards = [(a, b)[ref][i * width : (i + 1) * width, :] for ref, i in where[n]]
 
         @pl.when(role == 0)
         def _():
-            for off, v in zip(ORDER, shards):
+            tall[places(y, width), :] = jnp.zeros((width, 512), BF16)
+            for off, v in zip(REST, shards):
                 tall[places(lax.rem(y + off, 4), width), :] = v
             more = lax.dot_general(r_ref[:, lanes(x + 2, 512)], tall[...], NT, preferred_element_type=F32)
             o_buf[n, :, 0, :] = (acc[...] + more) * unit
 
         @pl.when(role == 1)
         def _():
-            for off, v in zip(ORDER, shards):
+            wide[:, lanes(x, 512)] = jnp.zeros((width, 512), BF16)
+            for off, v in zip(REST, shards):
                 wide[:, lanes(x + off, 512)] = v
             more = lax.dot_general(r_ref[...], wide[...], NT, preferred_element_type=F32)
             o_buf[n, :, 0, :] = acc[...] * unit
@@ -244,7 +260,8 @@
 
                 @pl.when(lax.rem(y + 2, 4) == k)
                 def _():
-                    o_buf[n, :, 0, k * width : (k + 1) * width] = more * unit
+                    part = slice(k * width, (k + 1) * width)
+                    o_buf[n, :, 0, part] = (acc[:, part] + more) * unit
 
         at = places(zl + role * (1 - 2 * zl), 4 * width)
         copies.append(pltpu.make_async_copy(o_buf.at[n], o_ref.at[:, :, at], sem.at[n]))
@@ -344,10 +361,12 @@
     partner = shift(keys, "zl", 2, 1)
     other = swap(keys)
     base = local(base_kernel, (keys, other, partner, swap(partner)), block(2))
-    near = apart(join(keys, other), "zh")
+    near = apart(after(join(keys, other), base), "zh")
     p1, p3, p2 = cross(base, -1, False), cross(base, 1, False), cross(base, 2, False)
     far = apart(near[0:width], "zh")
-    q = local(pack_kernel, (base, p1, p3, after(p2, near)), block(8), indexed=False)
+    q, z_keep, z_give = local(pack_kernel, (base, p1, p3, p2), (block(8), block(1), block(1)), indexed=False)
+    z_keep = shift(z_keep, "zl", 2, 1)
+    z_give = lax.ppermute(z_give, ("zl", "c"), [(0, 3), (1, 2), (2, 1), (3, 0)])
     q1, q3 = cross(q, -1, True), cross(q, 1, True)
     row_out, row_out2, row_own = local(
         row_kernel, (keys, other, near, far, swap(join(near, far))), (block(2), block(1), block(2)),
@@ -355,16 +374,23 @@
     )
     row_near, row_far = apart(row_out, "x"), shift(row_out2, "x", 4, 2)
     mine, a_keep, a_give, b_keep, b_give, give = local(
-        mine_kernel, (q, q1, q3, row_near, row_far), (cols,) + (block(2),) * 4 + (block(15),)
+        mine_kernel, (q, q1, after(q3, z_keep, z_give), row_near, row_far),
+        (cols, block(2), block(1), block(1), block(2), block(15)),
     )
     d_a, d_b = cross(a_keep, 1, True), cross(b_keep, -1, True)
     e_a, e_b = cross(a_give, 1, True, 1), cross(b_give, -1, True, 1)
     got = swap(give)
     sums = jax.ShapeDtypeStruct((rows, 4 * width), F32)
-    row_keys, acc_mine, acc_theirs = local(
-        early_kernel, (mine, got, row_own, row_near, row_far),
-        (jax.ShapeDtypeStruct((rows, 2048), BF16), sums, sums), [pltpu.VMEM((4 * width, 2048), BF16)],
-    )
+    row_keys, acc_mine, acc_theirs, _ = pl.pallas_call(
+        early_kernel,
+        in_specs=[SMEM] + [VMEM] * 7,
+        out_specs=(VMEM,) * 4,
+        out_shape=(jax.ShapeDtypeStruct((rows, 2048), BF16), sums, sums, cols),
+        scratch_shapes=[pltpu.VMEM((4 * width, 2048), BF16)],
+        input_output_aliases={1: 3},
+        compiler_params=pltpu.CompilerParams(vmem_limit_bytes=12 * MIB),
+        cost_estimate=pl.CostEstimate(flops=flops // 4, bytes_accessed=2 * MIB, transcendentals=0),
+    )(place, mine, got, z_keep, z_give, row_own, row_near, row_far)
     ins = (row_keys, acc_mine, acc_theirs, d_a, d_b, e_a, e_b)
     return call(
         moment_kernel, [SMEM] + [VMEM] * len(ins), jax.ShapeDtypeStruct((rows, 1, 8 * width), F32), HBM,

time: 117 us -> 111 us (0.949); the launches traced: 114 us -> 110 us
  waiting for transfers between devices: 41.5 us -> 33.7 us
  starting transfers between devices: 43.2 us -> 47.4 us
    pallas_call x10 -> x9, Pallas kernels: 29.2 us -> 23.7 us  [call(): pl.pallas_call(kernel, in_specs=in_specs, out_specs=out_specs, out_shape=...]
    pallas_call x0 -> x1, Pallas kernels: none -> 5.16 us  [shards(): pl.pallas_call(early_kernel, in_specs=[SMEM] + [VMEM] * 7, out_specs=(VME...]
    ppermute x9, waiting for transfers between devices: 7.59 us -> 3.11 us  [cross(): return lax.ppermute(v, ('y', 'x', 'c'), pairs)]
    ppermute x3, waiting for transfers between devices: 13.1 us -> 8.62 us  [apart(): lax.ppermute(v, (axis, 'c'), [(i * 2 + e, (i + 1 - 2 * e) % 4 * 2 + e) fo...]
    ppermute x3, starting transfers between devices: 8.98 us -> 12.3 us  [apart(): lax.ppermute(v, (axis, 'c'), [(i * 2 + e, (i + 1 - 2 * e) % 4 * 2 + e) fo...]
    ppermute x9, starting transfers between devices: 14.5 us -> 12.3 us  [cross(): return lax.ppermute(v, ('y', 'x', 'c'), pairs)]
    ppermute x0 -> x1, waiting for transfers between devices: none -> 1.74 us  [shards(): z_give = lax.ppermute(z_give, ('zl', 'c'), [(0, 3), (1, 2), (2, 1), (3, 0)])]
    ppermute x0 -> x1, starting transfers between devices: none -> 1.71 us  [shards(): z_give = lax.ppermute(z_give, ('zl', 'c'), [(0, 3), (1, 2), (2, 1), (3, 0)])]
  transfers between devices with their start and end apart: 21 -> 23, of which waited for: 11 -> 11; matrix products, arithmetic and copies ran while one was open for 0% -> 0% of each run, Pallas kernels for 15% -> 15%
where the time goes in v3:
time: 111 us; the launch traced here: 110 us
  starting transfers between devices  47.4 us (43%)
  waiting for transfers between devices  33.7 us (30%)
  Pallas kernels  28.9 us (26%)
    pallas_call x9, Pallas kernels, call(): pl.pallas_call(kernel, in_specs=in_specs, out_specs=out_specs, out_shape=...  23.7 us
    ppermute x10, starting transfers between devices, shift(): return lax.ppermute(value, axis, [(i, (i + by) % n) for i in range(n)])  21.1 us
    ppermute x10, waiting for transfers between devices, shift(): return lax.ppermute(value, axis, [(i, (i + by) % n) for i in range(n)])  20.2 us
    ppermute x3, starting transfers between devices, apart(): lax.ppermute(v, (axis, 'c'), [(i * 2 + e, (i + 1 - 2 * e) % 4 * 2 + e) fo...  12.3 us
    ppermute x9, starting transfers between devices, cross(): return lax.ppermute(v, ('y', 'x', 'c'), pairs)  12.3 us
    ppermute x3, waiting for transfers between devices, apart(): lax.ppermute(v, (axis, 'c'), [(i * 2 + e, (i + 1 - 2 * e) % 4 * 2 + e) fo...  8.62 us
    pallas_call x1, Pallas kernels, shards(): pl.pallas_call(early_kernel, in_specs=[SMEM] + [VMEM] * 7, out_specs=(VME...  5.16 us
    ppermute x9, waiting for transfers between devices, cross(): return lax.ppermute(v, ('y', 'x', 'c'), pairs)  3.11 us
  transfers between devices with their start and end apart: 23, of which 11 were waited for; matrix products, arithmetic and copies ran while one was open for 0% of the time, Pallas kernels for 15%

profile of v3, /device:TPU:1, one launch (start us, length us, event | category | flops | bytes accessed | tf_op | source)
XLA Modules:
  0.0 110.5 jit_solution(3921275033414030968)
XLA Ops:
  0.0 4.9 %shard_map.46 = (bf16[448,2048]{1,0:T(8,128)(2,1)}, bf16[464,512]{1,0:T(8,128)(2,1)}) custom-call(s32[1]{0:T(128)} %bitcast.6.idx_ref, f32[1,2048]{1,0:T(1,128)} %bitcast.14, bf16[224,2048]{1,0:T(8,128)(2,1)} %bitcast.12, bf16[224,2048]{1,0:T(8,128)(2,1)} %bitcast.13, bf16[2048,2048]{1,0:T(8,128)(2,1)} %h_ref.5), custom_call_target="tpu_custom_call" | custom-call | flops 939524096 | bytes 2097152 | tf_op jit(solution)/shard_map/pallas_call | solution.py:288
  4.9 3.7 %collective-permute-start.1 = (bf16[464,512]{1,0:T(8,128)(2,1)}, bf16[464,512]{1,0:T(8,128)(2,1)S(1)}, u32[]{:S(2)}, u32[]{:S(2)}) collective-permute-start(bf16[464,512]{1,0:T(8,128)(2,1)} %get-tuple-element.28), channel_id=1, source_target_pairs={{0,16},{8,24},{16,0},{24,8},{1,17},{9,25},{17,1},{25,9},{2,18},{10... | collective-permute-start | bytes 1425416 | tf_op jit(solution)/shard_map/ppermute | solution.py:18
  8.7 6.2 %shard_map.48 = (bf16[464,512]{1,0:T(8,128)(2,1)S(1)}, bf16[464,512]{1,0:T(8,128)(2,1)S(1)}) custom-call(s32[2]{0:T(128)S(1)} %pad_add_fusion.idx_ref, bf16[448,2048]{1,0:T(8,128)(2,1)} %get-tuple-element.26.w_ref, bf16[2048,2048]{1,0:T(8,128)(2,1)} %h_ref.5), custom_call_target="tpu_custom_call" | custom-call | flops 1879048192 | bytes 2097152 | tf_op jit(solution)/shard_map/pallas_call | solution.py:288
  15.3 2.4 %collective-permute-start.2 = (bf16[464,512]{1,0:T(8,128)(2,1)S(1)}, bf16[464,512]{1,0:T(8,128)(2,1)S(1)}, u32[]{:S(2)}, u32[]{:S(2)}) collective-permute-start(bf16[464,512]{1,0:T(8,128)(2,1)S(1)} %get-tuple-element.29), channel_id=1, source_target_pairs={{0,24},{8,0},{16,8},{24,16},{1,25},{9,1},{17,9},{25,17},{2,26},{10... | collective-permute-start | bytes 1425416 | tf_op jit(solution)/shard_map/ppermute | solution.py:18
  17.6 4.5 %shard_map.47.own_ref = f32[456,512]{1,0:T(8,128)S(1)} custom-call(s32[1]{0:T(128)} %bitcast.5.idx_ref, bf16[448,2048]{1,0:T(8,128)(2,1)} %get-tuple-element.26.w_ref, bf16[2048,2048]{1,0:T(8,128)(2,1)} %h_ref.5), custom_call_target="tpu_custom_call" | custom-call | flops 939524096 | bytes 2097152 | tf_op jit(solution)/shard_map/pallas_call | solution.py:288
  22.1 7.8 %collective-permute-done.p_ref = bf16[464,512]{1,0:T(8,128)(2,1)S(1)} collective-permute-done((bf16[464,512]{1,0:T(8,128)(2,1)S(1)}, bf16[464,512]{1,0:T(8,128)(2,1)S(1)}, u32[]{:S(2)}, u32[]{:S(2)}) %collective-permute-start) | collective-permute-done | bytes 475168 | tf_op jit(solution)/shard_map/ppermute | solution.py:18
  29.9 1.1 %shard_map.49.k_ref = bf16[224,512]{1,0:T(8,128)(2,1)S(1)} custom-call(f32[456,512]{1,0:T(8,128)S(1)} %shard_map.47.own_ref, bf16[464,512]{1,0:T(8,128)(2,1)S(1)} %collective-permute-done.p_ref, bf16[464,512]{1,0:T(8,128)(2,1)S(1)} %collective-permute-done.1.q_ref, bf16[464,512]{1,0:T(8,128)(2,1)S(1)} %collective-permute-done.2.r_ref), custom_call_target="tpu_custom_call" | custom-call | flops 939524096 | bytes 2097152 | tf_op jit(solution)/shard_map/pallas_call | solution.py:288
  31.1 1.9 %collective-permute-start.4 = (bf16[224,512]{1,0:T(8,128)(2,1)S(1)}, bf16[224,512]{1,0:T(8,128)(2,1)S(1)}, u32[]{:S(2)}, u32[]{:S(2)}) collective-permute-start(bf16[224,512]{1,0:T(8,128)(2,1)S(1)} %shard_map.49.k_ref), channel_id=1, source_target_pairs={{0,128},{128,0},{1,129},{129,1},{2,130},{130,2},{3,131},{131,3},{4... | collective-permute-start | bytes 688136 | tf_op jit(solution)/shard_map/ppermute | solution.py:18
  33.0 1.3 %collective-permute-start.3 = (bf16[224,512]{1,0:T(8,128)(2,1)S(1)}, bf16[224,512]{1,0:T(8,128)(2,1)S(1)}, u32[]{:S(2)}, u32[]{:S(2)}) collective-permute-start(bf16[224,512]{1,0:T(8,128)(2,1)S(1)} %shard_map.49.k_ref), channel_id=1, source_target_pairs={{0,1},{1,0},{2,3},{3,2},{4,5},{5,4},{6,7},{7,6},{8,9},{9,8},{10,11... | collective-permute-start | bytes 688136 | tf_op jit(solution)/shard_map/ppermute | solution.py:18
  34.3 3.5 %collective-permute-done.4.p_ref = bf16[224,512]{1,0:T(8,128)(2,1)S(1)} collective-permute-done((bf16[224,512]{1,0:T(8,128)(2,1)S(1)}, bf16[224,512]{1,0:T(8,128)(2,1)S(1)}, u32[]{:S(2)}, u32[]{:S(2)}) %collective-permute-start.4) | collective-permute-done | bytes 229408 | tf_op jit(solution)/shard_map/ppermute | solution.py:18
  37.7 1.8 %collective-permute-start.5 = (bf16[224,512]{1,0:T(8,128)(2,1)S(1)}, bf16[224,512]{1,0:T(8,128)(2,1)S(1)}, u32[]{:S(2)}, u32[]{:S(2)}) collective-permute-start(bf16[224,512]{1,0:T(8,128)(2,1)S(1)} %collective-permute-done.4.p_ref), channel_id=1, source_target_pairs={{0,1},{1,0},{2,3},{3,2},{4,5},{5,4},{6,7},{7,6},{8,9},{9,8},{10,11... | collective-permute-start | bytes 688136 | tf_op jit(solution)/shard_map/ppermute | solution.py:18
  41.2 3.3 %collective-permute-start.8 = (bf16[448,512]{1,0:T(8,128)(2,1)S(1)}, bf16[448,512]{1,0:T(8,128)(2,1)S(1)}, u32[]{:S(2)}, u32[]{:S(2)}) collective-permute-start(bf16[448,512]{1,0:T(8,128)(2,1)S(1)} %shard_map.50.base), channel_id=1, source_target_pairs={{0,64},{1,17},{8,72},{9,25},{16,80},{17,1},{24,88},{25,9},{32,96},... | collective-permute-start | bytes 1376264 | tf_op jit(solution)/shard_map/ppermute | solution.py:352
  44.5 2.7 %collective-permute-start.6 = (bf16[448,512]{1,0:T(8,128)(2,1)S(1)}, bf16[448,512]{1,0:T(8,128)(2,1)S(1)}, u32[]{:S(2)}, u32[]{:S(2)}) collective-permute-start(bf16[448,512]{1,0:T(8,128)(2,1)S(1)} %shard_map.50.base), channel_id=1, source_target_pairs={{0,96},{1,25},{8,104},{9,1},{16,112},{17,9},{24,120},{25,17},{32,0... | collective-permute-start | bytes 1376264 | tf_op jit(solution)/shard_map/ppermute | solution.py:352
  47.2 5.9 %collective-permute-start.13 = (bf16[448,512]{1,0:T(8,128)(2,1)S(1)}, bf16[448,512]{1,0:T(8,128)(2,1)S(1)}, u32[]{:S(2)}, u32[]{:S(2)}) collective-permute-start(bf16[448,512]{1,0:T(8,128)(2,1)S(1)} %pad_maximum_fusion.1), channel_id=1, source_target_pairs={{0,2},{1,7},{2,4},{3,1},{4,6},{5,3},{6,0},{7,5},{8,10},{9,15},{10,... | collective-permute-start | bytes 1376264 | tf_op jit(solution)/shard_map/ppermute | solution.py:355
  53.2 2.4 %collective-permute-done.7.p3_ref = bf16[448,512]{1,0:T(8,128)(2,1)S(1)} collective-permute-done((bf16[448,512]{1,0:T(8,128)(2,1)S(1)}, bf16[448,512]{1,0:T(8,128)(2,1)S(1)}, u32[]{:S(2)}, u32[]{:S(2)}) %collective-permute-start.7) | collective-permute-done | bytes 458784 | tf_op jit(solution)/shard_map/ppermute | solution.py:352
  55.8 1.4 %collective-permute-start.10 = (bf16[1792,512]{1,0:T(8,128)(2,1)S(1)}, bf16[1792,512]{1,0:T(8,128)(2,1)S(1)}, u32[]{:S(2)}, u32[]{:S(2)}) collective-permute-start(bf16[1792,512]{1,0:T(8,128)(2,1)S(1)} %get-tuple-element.30.q_ref), channel_id=1, source_target_pairs={{0,8},{1,33},{8,16},{9,41},{16,24},{17,49},{24,0},{25,57},{32,40},... | collective-permute-start | bytes 5505032 | tf_op jit(solution)/shard_map/ppermute | solution.py:352
  57.1 1.5 %collective-permute-start.9 = (bf16[1792,512]{1,0:T(8,128)(2,1)S(1)}, bf16[1792,512]{1,0:T(8,128)(2,1)S(1)}, u32[]{:S(2)}, u32[]{:S(2)}) collective-permute-start(bf16[1792,512]{1,0:T(8,128)(2,1)S(1)} %get-tuple-element.30.q_ref), channel_id=1, source_target_pairs={{0,24},{1,97},{8,0},{9,105},{16,8},{17,113},{24,16},{25,121},{32,5... | collective-permute-start | bytes 5505032 | tf_op jit(solution)/shard_map/ppermute | solution.py:352
  58.6 4.9 %collective-permute-done.13.near = bf16[448,512]{1,0:T(8,128)(2,1)S(1)} collective-permute-done((bf16[448,512]{1,0:T(8,128)(2,1)S(1)}, bf16[448,512]{1,0:T(8,128)(2,1)S(1)}, u32[]{:S(2)}, u32[]{:S(2)}) %collective-permute-start.13) | collective-permute-done | bytes 458784 | tf_op jit(solution)/shard_map/ppermute | solution.py:355
  63.5 4.1 %collective-permute-start.14 = (bf16[224,512]{1,0:T(8,128)(2,1)S(1)}, bf16[224,512]{1,0:T(8,128)(2,1)S(1)}, u32[]{:S(2)}, u32[]{:S(2)}) collective-permute-start(bf16[224,512]{1,0:T(8,128)(2,1)S(1)} %slice.4), channel_id=1, source_target_pairs={{0,2},{1,7},{2,4},{3,1},{4,6},{5,3},{6,0},{7,5},{8,10},{9,15},{10,... | collective-permute-start | bytes 688136 | tf_op jit(solution)/shard_map/ppermute | solution.py:355
  67.6 3.8 %collective-permute-done.14.far = bf16[224,512]{1,0:T(8,128)(2,1)S(1)} collective-permute-done((bf16[224,512]{1,0:T(8,128)(2,1)S(1)}, bf16[224,512]{1,0:T(8,128)(2,1)S(1)}, u32[]{:S(2)}, u32[]{:S(2)}) %collective-permute-start.14) | collective-permute-done | bytes 229408 | tf_op jit(solution)/shard_map/ppermute | solution.py:355
  71.4 2.2 %collective-permute-start.15 = (bf16[672,512]{1,0:T(8,128)(2,1)S(1)}, bf16[672,512]{1,0:T(8,128)(2,1)S(1)}, u32[]{:S(2)}, u32[]{:S(2)}) collective-permute-start(bf16[672,512]{1,0:T(8,128)(2,1)S(1)} %pad_maximum_fusion), channel_id=1, source_target_pairs={{0,1},{1,0},{2,3},{3,2},{4,5},{5,4},{6,7},{7,6},{8,9},{9,8},{10,11... | collective-permute-start | bytes 2064392 | tf_op jit(solution)/shard_map/ppermute | solution.py:18
  73.6 3.0 %collective-permute-start.11 = (bf16[224,512]{1,0:T(8,128)(2,1)S(1)}, bf16[224,512]{1,0:T(8,128)(2,1)S(1)}, u32[]{:S(2)}, u32[]{:S(2)}) collective-permute-start(bf16[224,512]{1,0:T(8,128)(2,1)S(1)} %get-tuple-element.31), channel_id=1, source_target_pairs={{0,128},{128,0},{1,129},{129,1},{2,130},{130,2},{3,131},{131,3},{4... | collective-permute-start | bytes 688136 | tf_op jit(solution)/shard_map/ppermute | solution.py:18
  77.3 2.3 %collective-permute-start.16 = (bf16[448,512]{1,0:T(8,128)(2,1)S(1)}, bf16[448,512]{1,0:T(8,128)(2,1)S(1)}, u32[]{:S(2)}, u32[]{:S(2)}) collective-permute-start(bf16[448,512]{1,0:T(8,128)(2,1)S(1)} %get-tuple-element.35), channel_id=1, source_target_pairs={{0,8},{1,25},{8,16},{9,1},{16,24},{17,9},{24,0},{25,17},{2,10},{3,... | collective-permute-start | bytes 1376264 | tf_op jit(solution)/shard_map/ppermute | solution.py:355
  79.6 1.7 %collective-permute-start.12 = (bf16[224,512]{1,0:T(8,128)(2,1)S(1)}, bf16[224,512]{1,0:T(8,128)(2,1)S(1)}, u32[]{:S(2)}, u32[]{:S(2)}) collective-permute-start(bf16[224,512]{1,0:T(8,128)(2,1)S(1)} %get-tuple-element.32), channel_id=1, source_target_pairs={{0,129},{1,128},{128,1},{129,0},{2,131},{3,130},{130,3},{131,2},{4... | collective-permute-start | bytes 688136 | tf_op jit(solution)/shard_map/ppermute | solution.py:369
  82.4 3.2 %collective-permute-start.17 = (bf16[224,512]{1,0:T(8,128)(2,1)S(1)}, bf16[224,512]{1,0:T(8,128)(2,1)S(1)}, u32[]{:S(2)}, u32[]{:S(2)}) collective-permute-start(bf16[224,512]{1,0:T(8,128)(2,1)S(1)} %get-tuple-element.36), channel_id=1, source_target_pairs={{0,16},{8,24},{16,0},{24,8},{1,17},{9,25},{17,1},{25,9},{2,18},{10... | collective-permute-start | bytes 688136 | tf_op jit(solution)/shard_map/ppermute | solution.py:18
  85.7 1.7 %collective-permute-done.12.z_give = bf16[224,512]{1,0:T(8,128)(2,1)S(1)} collective-permute-done((bf16[224,512]{1,0:T(8,128)(2,1)S(1)}, bf16[224,512]{1,0:T(8,128)(2,1)S(1)}, u32[]{:S(2)}, u32[]{:S(2)}) %collective-permute-start.12) | collective-permute-done | bytes 229408 | tf_op jit(solution)/shard_map/ppermute | solution.py:369
  87.4 4.5 %collective-permute-done.17.far = bf16[224,512]{1,0:T(8,128)(2,1)S(1)} collective-permute-done((bf16[224,512]{1,0:T(8,128)(2,1)S(1)}, bf16[224,512]{1,0:T(8,128)(2,1)S(1)}, u32[]{:S(2)}, u32[]{:S(2)}) %collective-permute-start.17) | collective-permute-done | bytes 229408 | tf_op jit(solution)/shard_map/ppermute | solution.py:18
  93.1 1.3 %collective-permute-start.18 = (bf16[3360,512]{1,0:T(8,128)(2,1)S(1)}, bf16[3360,512]{1,0:T(8,128)(2,1)S(1)}, u32[]{:S(2)}, u32[]{:S(2)}) collective-permute-start(bf16[3360,512]{1,0:T(8,128)(2,1)S(1)} %get-tuple-element.38), channel_id=1, source_target_pairs={{0,1},{1,0},{2,3},{3,2},{4,5},{5,4},{6,7},{7,6},{8,9},{9,8},{10,11... | collective-permute-start | bytes 10321928 | tf_op jit(solution)/shard_map/ppermute | solution.py:18
  94.6 2.4 %collective-permute-start.22 = (bf16[448,512]{1,0:T(8,128)(2,1)S(1)}, bf16[448,512]{1,0:T(8,128)(2,1)S(1)}, u32[]{:S(2)}, u32[]{:S(2)}) collective-permute-start(bf16[448,512]{1,0:T(8,128)(2,1)S(1)} %get-tuple-element.46), channel_id=1, source_target_pairs={{0,25},{1,96},{8,1},{9,104},{16,9},{17,112},{24,17},{25,120},{32,5... | collective-permute-start | bytes 1376264 | tf_op jit(solution)/shard_map/ppermute | solution.py:352
  97.8 2.3 %collective-permute-done.18.got = bf16[3360,512]{1,0:T(8,128)(2,1)S(1)} collective-permute-done((bf16[3360,512]{1,0:T(8,128)(2,1)S(1)}, bf16[3360,512]{1,0:T(8,128)(2,1)S(1)}, u32[]{:S(2)}, u32[]{:S(2)}) %collective-permute-start.18) | collective-permute-done | bytes 3440672 | tf_op jit(solution)/shard_map/ppermute | solution.py:18
  100.1 5.2 %shard_map.54 = (bf16[448,2048]{1,0:T(8,128)(2,1)S(1)}, f32[448,896]{1,0:T(8,128)S(1)}, f32[448,896]{1,0:T(8,128)S(1)}, bf16[896,2048]{1,0:T(8,128)(2,1)S(1)}) custom-call(s32[5]{0:T(128)S(1)} %stack.38.idx_ref, bf16[896,2048]{1,0:T(8,128)(2,1)S(1)} %get-tuple-element.37.mine_in, ...), custom_call_target="tpu_custom_call", output_to_operand_aliasing={{3}: (1, {})} | custom-call | flops 234881024 | bytes 2097152 | tf_op jit(solution)/shard_map/pallas_call | solution.py:384
  105.9 4.4 %shard_map.55 = f32[448,1,1792]{2,1,0:T(1,128)} custom-call(s32[5]{0:T(128)S(1)} %stack.38.idx_ref, bf16[448,2048]{1,0:T(8,128)(2,1)S(1)} %get-tuple-element.40.r_ref, f32[448,896]{1,0:T(8,128)S(1)} %get-tuple-element.41.acc_mine, f32[448,896]{1,0:T(8,128)S(1)} %get-tuple-element.42.acc_theirs, bf16[448,512]{1,0:T(8,128)(2,1)S(1)} %collective-permute-done.19.d_a, ...), custom_call_target="tpu_custom_call" | custom-call | flops 939524096 | bytes 2097152 | tf_op jit(solution)/shard_map/pallas_call | solution.py:288
  (29 shorter events, 7.0 us)
Async XLA Ops:
  4.9 17.2 %collective-permute-start.1 = (bf16[464,512]{1,0:T(8,128)(2,1)}, bf16[464,512]{1,0:T(8,128)(2,1)S(1)}, u32[]{:S(2)}, u32[]{:S(2)}) collective-permute-start(bf16[464,512]{1,0:T(8,128)(2,1)} %get-tuple-element.28), channel_id=1, source_target_pairs={{0,16},{8,24},{16,0},{24,8},{1,17},{9,25},{17,1},{25,9},{2,18},{10... | collective-permute-start | bytes 1425416 | tf_op jit(solution)/shard_map/ppermute | solution.py:18
  14.9 15.0 %collective-permute-start = (bf16[464,512]{1,0:T(8,128)(2,1)S(1)}, bf16[464,512]{1,0:T(8,128)(2,1)S(1)}, u32[]{:S(2)}, u32[]{:S(2)}) collective-permute-start(bf16[464,512]{1,0:T(8,128)(2,1)S(1)} %get-tuple-element.27), channel_id=1, source_target_pairs={{0,8},{8,16},{16,24},{24,0},{1,9},{9,17},{17,25},{25,1},{2,10},{10... | collective-permute-start | bytes 1425416 | tf_op jit(solution)/shard_map/ppermute | solution.py:18
  15.3 14.6 %collective-permute-start.2 = (bf16[464,512]{1,0:T(8,128)(2,1)S(1)}, bf16[464,512]{1,0:T(8,128)(2,1)S(1)}, u32[]{:S(2)}, u32[]{:S(2)}) collective-permute-start(bf16[464,512]{1,0:T(8,128)(2,1)S(1)} %get-tuple-element.29), channel_id=1, source_target_pairs={{0,24},{8,0},{16,8},{24,16},{1,25},{9,1},{17,9},{25,17},{2,26},{10... | collective-permute-start | bytes 1425416 | tf_op jit(solution)/shard_map/ppermute | solution.py:18
  31.1 6.7 %collective-permute-start.4 = (bf16[224,512]{1,0:T(8,128)(2,1)S(1)}, bf16[224,512]{1,0:T(8,128)(2,1)S(1)}, u32[]{:S(2)}, u32[]{:S(2)}) collective-permute-start(bf16[224,512]{1,0:T(8,128)(2,1)S(1)} %shard_map.49.k_ref), channel_id=1, source_target_pairs={{0,128},{128,0},{1,129},{129,1},{2,130},{130,2},{3,131},{131,3},{4... | collective-permute-start | bytes 688136 | tf_op jit(solution)/shard_map/ppermute | solution.py:18
  33.0 6.6 %collective-permute-start.3 = (bf16[224,512]{1,0:T(8,128)(2,1)S(1)}, bf16[224,512]{1,0:T(8,128)(2,1)S(1)}, u32[]{:S(2)}, u32[]{:S(2)}) collective-permute-start(bf16[224,512]{1,0:T(8,128)(2,1)S(1)} %shard_map.49.k_ref), channel_id=1, source_target_pairs={{0,1},{1,0},{2,3},{3,2},{4,5},{5,4},{6,7},{7,6},{8,9},{9,8},{10,11... | collective-permute-start | bytes 688136 | tf_op jit(solution)/shard_map/ppermute | solution.py:18
  37.7 2.9 %collective-permute-start.5 = (bf16[224,512]{1,0:T(8,128)(2,1)S(1)}, bf16[224,512]{1,0:T(8,128)(2,1)S(1)}, u32[]{:S(2)}, u32[]{:S(2)}) collective-permute-start(bf16[224,512]{1,0:T(8,128)(2,1)S(1)} %collective-permute-done.4.p_ref), channel_id=1, source_target_pairs={{0,1},{1,0},{2,3},{3,2},{4,5},{5,4},{6,7},{7,6},{8,9},{9,8},{10,11... | collective-permute-start | bytes 688136 | tf_op jit(solution)/shard_map/ppermute | solution.py:18
  41.2 11.9 %collective-permute-start.8 = (bf16[448,512]{1,0:T(8,128)(2,1)S(1)}, bf16[448,512]{1,0:T(8,128)(2,1)S(1)}, u32[]{:S(2)}, u32[]{:S(2)}) collective-permute-start(bf16[448,512]{1,0:T(8,128)(2,1)S(1)} %shard_map.50.base), channel_id=1, source_target_pairs={{0,64},{1,17},{8,72},{9,25},{16,80},{17,1},{24,88},{25,9},{32,96},... | collective-permute-start | bytes 1376264 | tf_op jit(solution)/shard_map/ppermute | solution.py:352
  44.5 11.1 %collective-permute-start.7 = (bf16[448,512]{1,0:T(8,128)(2,1)S(1)}, bf16[448,512]{1,0:T(8,128)(2,1)S(1)}, u32[]{:S(2)}, u32[]{:S(2)}) collective-permute-start(bf16[448,512]{1,0:T(8,128)(2,1)S(1)} %shard_map.50.base), channel_id=1, source_target_pairs={{0,32},{1,9},{8,40},{9,17},{16,48},{17,25},{24,56},{25,1},{32,64},... | collective-permute-start | bytes 1376264 | tf_op jit(solution)/shard_map/ppermute | solution.py:352
  44.5 11.1 %collective-permute-start.6 = (bf16[448,512]{1,0:T(8,128)(2,1)S(1)}, bf16[448,512]{1,0:T(8,128)(2,1)S(1)}, u32[]{:S(2)}, u32[]{:S(2)}) collective-permute-start(bf16[448,512]{1,0:T(8,128)(2,1)S(1)} %shard_map.50.base), channel_id=1, source_target_pairs={{0,96},{1,25},{8,104},{9,1},{16,112},{17,9},{24,120},{25,17},{32,0... | collective-permute-start | bytes 1376264 | tf_op jit(solution)/shard_map/ppermute | solution.py:352
  47.2 16.3 %collective-permute-start.13 = (bf16[448,512]{1,0:T(8,128)(2,1)S(1)}, bf16[448,512]{1,0:T(8,128)(2,1)S(1)}, u32[]{:S(2)}, u32[]{:S(2)}) collective-permute-start(bf16[448,512]{1,0:T(8,128)(2,1)S(1)} %pad_maximum_fusion.1), channel_id=1, source_target_pairs={{0,2},{1,7},{2,4},{3,1},{4,6},{5,3},{6,0},{7,5},{8,10},{9,15},{10,... | collective-permute-start | bytes 1376264 | tf_op jit(solution)/shard_map/ppermute | solution.py:355
  55.8 31.7 %collective-permute-start.10 = (bf16[1792,512]{1,0:T(8,128)(2,1)S(1)}, bf16[1792,512]{1,0:T(8,128)(2,1)S(1)}, u32[]{:S(2)}, u32[]{:S(2)}) collective-permute-start(bf16[1792,512]{1,0:T(8,128)(2,1)S(1)} %get-tuple-element.30.q_ref), channel_id=1, source_target_pairs={{0,8},{1,33},{8,16},{9,41},{16,24},{17,49},{24,0},{25,57},{32,40},... | collective-permute-start | bytes 5505032 | tf_op jit(solution)/shard_map/ppermute | solution.py:352
  57.1 34.8 %collective-permute-start.9 = (bf16[1792,512]{1,0:T(8,128)(2,1)S(1)}, bf16[1792,512]{1,0:T(8,128)(2,1)S(1)}, u32[]{:S(2)}, u32[]{:S(2)}) collective-permute-start(bf16[1792,512]{1,0:T(8,128)(2,1)S(1)} %get-tuple-element.30.q_ref), channel_id=1, source_target_pairs={{0,24},{1,97},{8,0},{9,105},{16,8},{17,113},{24,16},{25,121},{32,5... | collective-permute-start | bytes 5505032 | tf_op jit(solution)/shard_map/ppermute | solution.py:352
  63.5 7.9 %collective-permute-start.14 = (bf16[224,512]{1,0:T(8,128)(2,1)S(1)}, bf16[224,512]{1,0:T(8,128)(2,1)S(1)}, u32[]{:S(2)}, u32[]{:S(2)}) collective-permute-start(bf16[224,512]{1,0:T(8,128)(2,1)S(1)} %slice.4), channel_id=1, source_target_pairs={{0,2},{1,7},{2,4},{3,1},{4,6},{5,3},{6,0},{7,5},{8,10},{9,15},{10,... | collective-permute-start | bytes 688136 | tf_op jit(solution)/shard_map/ppermute | solution.py:355
  71.4 5.2 %collective-permute-start.15 = (bf16[672,512]{1,0:T(8,128)(2,1)S(1)}, bf16[672,512]{1,0:T(8,128)(2,1)S(1)}, u32[]{:S(2)}, u32[]{:S(2)}) collective-permute-start(bf16[672,512]{1,0:T(8,128)(2,1)S(1)} %pad_maximum_fusion), channel_id=1, source_target_pairs={{0,1},{1,0},{2,3},{3,2},{4,5},{5,4},{6,7},{7,6},{8,9},{9,8},{10,11... | collective-permute-start | bytes 2064392 | tf_op jit(solution)/shard_map/ppermute | solution.py:18
  73.6 8.8 %collective-permute-start.11 = (bf16[224,512]{1,0:T(8,128)(2,1)S(1)}, bf16[224,512]{1,0:T(8,128)(2,1)S(1)}, u32[]{:S(2)}, u32[]{:S(2)}) collective-permute-start(bf16[224,512]{1,0:T(8,128)(2,1)S(1)} %get-tuple-element.31), channel_id=1, source_target_pairs={{0,128},{128,0},{1,129},{129,1},{2,130},{130,2},{3,131},{131,3},{4... | collective-permute-start | bytes 688136 | tf_op jit(solution)/shard_map/ppermute | solution.py:18
  77.3 14.6 %collective-permute-start.16 = (bf16[448,512]{1,0:T(8,128)(2,1)S(1)}, bf16[448,512]{1,0:T(8,128)(2,1)S(1)}, u32[]{:S(2)}, u32[]{:S(2)}) collective-permute-start(bf16[448,512]{1,0:T(8,128)(2,1)S(1)} %get-tuple-element.35), channel_id=1, source_target_pairs={{0,8},{1,25},{8,16},{9,1},{16,24},{17,9},{24,0},{25,17},{2,10},{3,... | collective-permute-start | bytes 1376264 | tf_op jit(solution)/shard_map/ppermute | solution.py:355
  79.6 7.8 %collective-permute-start.12 = (bf16[224,512]{1,0:T(8,128)(2,1)S(1)}, bf16[224,512]{1,0:T(8,128)(2,1)S(1)}, u32[]{:S(2)}, u32[]{:S(2)}) collective-permute-start(bf16[224,512]{1,0:T(8,128)(2,1)S(1)} %get-tuple-element.32), channel_id=1, source_target_pairs={{0,129},{1,128},{128,1},{129,0},{2,131},{3,130},{130,3},{131,2},{4... | collective-permute-start | bytes 688136 | tf_op jit(solution)/shard_map/ppermute | solution.py:369
  82.4 9.5 %collective-permute-start.17 = (bf16[224,512]{1,0:T(8,128)(2,1)S(1)}, bf16[224,512]{1,0:T(8,128)(2,1)S(1)}, u32[]{:S(2)}, u32[]{:S(2)}) collective-permute-start(bf16[224,512]{1,0:T(8,128)(2,1)S(1)} %get-tuple-element.36), channel_id=1, source_target_pairs={{0,16},{8,24},{16,0},{24,8},{1,17},{9,25},{17,1},{25,9},{2,18},{10... | collective-permute-start | bytes 688136 | tf_op jit(solution)/shard_map/ppermute | solution.py:18
  93.1 7.0 %collective-permute-start.18 = (bf16[3360,512]{1,0:T(8,128)(2,1)S(1)}, bf16[3360,512]{1,0:T(8,128)(2,1)S(1)}, u32[]{:S(2)}, u32[]{:S(2)}) collective-permute-start(bf16[3360,512]{1,0:T(8,128)(2,1)S(1)} %get-tuple-element.38), channel_id=1, source_target_pairs={{0,1},{1,0},{2,3},{3,2},{4,5},{5,4},{6,7},{7,6},{8,9},{9,8},{10,11... | collective-permute-start | bytes 10321928 | tf_op jit(solution)/shard_map/ppermute | solution.py:18
  94.4 11.6 %collective-permute-start.19 = (bf16[448,512]{1,0:T(8,128)(2,1)S(1)}, bf16[448,512]{1,0:T(8,128)(2,1)S(1)}, u32[]{:S(2)}, u32[]{:S(2)}) collective-permute-start(bf16[448,512]{1,0:T(8,128)(2,1)S(1)} %get-tuple-element.43), channel_id=1, source_target_pairs={{0,8},{1,33},{8,16},{9,41},{16,24},{17,49},{24,0},{25,57},{32,40},... | collective-permute-start | bytes 1376264 | tf_op jit(solution)/shard_map/ppermute | solution.py:352
  94.6 11.4 %collective-permute-start.22 = (bf16[448,512]{1,0:T(8,128)(2,1)S(1)}, bf16[448,512]{1,0:T(8,128)(2,1)S(1)}, u32[]{:S(2)}, u32[]{:S(2)}) collective-permute-start(bf16[448,512]{1,0:T(8,128)(2,1)S(1)} %get-tuple-element.46), channel_id=1, source_target_pairs={{0,25},{1,96},{8,1},{9,104},{16,9},{17,112},{24,17},{25,120},{32,5... | collective-permute-start | bytes 1376264 | tf_op jit(solution)/shard_map/ppermute | solution.py:352
  97.0 8.3 %collective-permute-start.20 = (bf16[224,512]{1,0:T(8,128)(2,1)S(1)}, bf16[224,512]{1,0:T(8,128)(2,1)S(1)}, u32[]{:S(2)}, u32[]{:S(2)}) collective-permute-start(bf16[224,512]{1,0:T(8,128)(2,1)S(1)} %get-tuple-element.44), channel_id=1, source_target_pairs={{0,24},{1,97},{8,0},{9,105},{16,8},{17,113},{24,16},{25,121},{32,5... | collective-permute-start | bytes 688136 | tf_op jit(solution)/shard_map/ppermute | solution.py:352
  97.1 8.9 %collective-permute-start.21 = (bf16[224,512]{1,0:T(8,128)(2,1)S(1)}, bf16[224,512]{1,0:T(8,128)(2,1)S(1)}, u32[]{:S(2)}, u32[]{:S(2)}) collective-permute-start(bf16[224,512]{1,0:T(8,128)(2,1)S(1)} %get-tuple-element.45), channel_id=1, source_target_pairs={{0,9},{1,32},{8,17},{9,40},{16,25},{17,48},{24,1},{25,56},{32,41},... | collective-permute-start | bytes 688136 | tf_op jit(solution)/shard_map/ppermute | solution.py:352

commit v4 on v3

--- a/solution.py
+++ b/solution.py
@@ -147,12 +147,10 @@
             b_ref[width:, :] = second[...]
 
 
-def pack_kernel(base, p1_ref, p3_ref, p2_ref, q_ref, keep, give):
-    size = p1_ref.shape[0]
-    for i, ref in enumerate((base, p1_ref, p3_ref, p2_ref)):
-        q_ref[i * size : (i + 1) * size, :] = ref[...]
-    keep[...] = p2_ref[0 : size // 2, :]
-    give[...] = p2_ref[size // 2 :, :]
+def pack_kernel(*refs):
+    size = refs[0].shape[0]
+    for i, ref in enumerate(refs[:4]):
+        refs[4][i * size : (i + 1) * size, :] = ref[...]
 
 
 def clear(cols, idx_ref, role):
@@ -171,7 +169,7 @@
 REST = ORDER[1:]
 
 
-def mine_kernel(idx_ref, q_ref, up_ref, down_ref, near, far, cols, a_keep, a_give, b_keep, b_give, give):
+def mine_kernel(idx_ref, q_ref, up_ref, down_ref, near, far, z_ref, cols, a_keep, a_give, b_keep, b_give, give):
     width = cols.shape[0] // 4
 
     def shard(ref, i):
@@ -190,8 +188,10 @@
         for i in range(4):
             give[to : to + width, :] = shard(ref, 2 * i + 1)
             to += width
-    give[to : to + 2 * width, :] = near[...]
-    give[to + 2 * width :, :] = far[...]
+    put(cols, z_ref, idx_ref, idx_ref[4], 2, (0,), 1)
+    give[to : to + width, :] = shard(z_ref, 0)
+    give[to + width : to + 3 * width, :] = near[...]
+    give[to + 3 * width :, :] = far[...]
 
 
 def row_kernel(idx_ref, k_ref, k_other, near, far, got, out_ref, out2_ref, own_ref, buf):
@@ -210,7 +210,7 @@
     own_ref[...] = buf[x]
 
 
-def early_kernel(idx_ref, mine_in, got, z_keep, z_give, row_own, near, far, r_buf, acc_mine, acc_theirs, mine, theirs):
+def early_kernel(idx_ref, mine, got, row_own, near, far, r_buf, acc_mine, acc_theirs, theirs):
     width = mine.shape[0] // 4
     x, c = idx_ref[2], idx_ref[4]
     this, that = places(c, width), places(1 - c, width)
@@ -219,15 +219,14 @@
     r_buf[that, lanes(x, 512)] = row_own[width:, :]
     r_buf[this, before] = near[0:width, :]
     r_buf[that, before] = near[width:, :]
-    r_buf[that, behind] = got[12 * width : 13 * width, :]
-    r_buf[this, behind] = got[13 * width : 14 * width, :]
+    r_buf[that, behind] = got[13 * width : 14 * width, :]
+    r_buf[this, behind] = got[14 * width : 15 * width, :]
     r_buf[this, lanes(x + 2, 512)] = far[...]
-    r_buf[that, lanes(x + 2, 512)] = got[14 * width :, :]
+    r_buf[that, lanes(x + 2, 512)] = got[15 * width :, :]
     clear(theirs, idx_ref, 1 - c)
     for n, d in enumerate((0, 1, 3)):
         put(theirs, got.at[4 * n * width : 4 * (n + 1) * width], idx_ref, 1 - c, d, ORDER, 0, 1)
-    put(theirs, z_keep, idx_ref, 1 - c, 2, (0,), 0, 1)
-    put(mine, z_give, idx_ref, c, 2, (0,), 0, 1)
+    put(theirs, got.at[12 * width : 13 * width], idx_ref, 1 - c, 2, (0,), 0, 1)
     acc_mine[...] = lax.dot_general(r_buf[...], mine[...], NT, preferred_element_type=F32)
     acc_theirs[...] = lax.dot_general(r_buf[...], theirs[...], NT, preferred_element_type=F32)
 
@@ -364,9 +363,8 @@
     near = apart(after(join(keys, other), base), "zh")
     p1, p3, p2 = cross(base, -1, False), cross(base, 1, False), cross(base, 2, False)
     far = apart(near[0:width], "zh")
-    q, z_keep, z_give = local(pack_kernel, (base, p1, p3, p2), (block(8), block(1), block(1)), indexed=False)
-    z_keep = shift(z_keep, "zl", 2, 1)
-    z_give = lax.ppermute(z_give, ("zl", "c"), [(0, 3), (1, 2), (2, 1), (3, 0)])
+    q = local(pack_kernel, (base, p1, p3, p2), block(8), indexed=False)
+    z_pair = lax.ppermute(p2, ("zl", "c"), [(0, 3), (1, 2), (2, 1), (3, 0)])
     q1, q3 = cross(q, -1, True), cross(q, 1, True)
     row_out, row_out2, row_own = local(
         row_kernel, (keys, other, near, far, swap(join(near, far))), (block(2), block(1), block(2)),
@@ -374,23 +372,17 @@
     )
     row_near, row_far = apart(row_out, "x"), shift(row_out2, "x", 4, 2)
     mine, a_keep, a_give, b_keep, b_give, give = local(
-        mine_kernel, (q, q1, after(q3, z_keep, z_give), row_near, row_far),
-        (cols, block(2), block(1), block(1), block(2), block(15)),
+        mine_kernel, (q, q1, q3, row_near, row_far, z_pair),
+        (cols, block(2), block(1), block(1), block(2), block(16)),
     )
     d_a, d_b = cross(a_keep, 1, True), cross(b_keep, -1, True)
     e_a, e_b = cross(a_give, 1, True, 1), cross(b_give, -1, True, 1)
     got = swap(give)
     sums = jax.ShapeDtypeStruct((rows, 4 * width), F32)
-    row_keys, acc_mine, acc_theirs, _ = pl.pallas_call(
-        early_kernel,
-        in_specs=[SMEM] + [VMEM] * 7,
-        out_specs=(VMEM,) * 4,
-        out_shape=(jax.ShapeDtypeStruct((rows, 2048), BF16), sums, sums, cols),
-        scratch_shapes=[pltpu.VMEM((4 * width, 2048), BF16)],
-        input_output_aliases={1: 3},
-        compiler_params=pltpu.CompilerParams(vmem_limit_bytes=12 * MIB),
-        cost_estimate=pl.CostEstimate(flops=flops // 4, bytes_accessed=2 * MIB, transcendentals=0),
-    )(place, mine, got, z_keep, z_give, row_own, row_near, row_far)
+    row_keys, acc_mine, acc_theirs = local(
+        early_kernel, (mine, got, row_own, row_near, row_far),
+        (jax.ShapeDtypeStruct((rows, 2048), BF16), sums, sums), [pltpu.VMEM((4 * width, 2048), BF16)],
+    )
     ins = (row_keys, acc_mine, acc_theirs, d_a, d_b, e_a, e_b)
     return call(
         moment_kernel, [SMEM] + [VMEM] * len(ins), jax.ShapeDtypeStruct((rows, 1, 8 * width), F32), HBM,

time: 111 us -> 111 us (level)
  starting transfers between devices: 47.4 us -> 46.2 us
  waiting for transfers between devices: 33.7 us -> 34.9 us
    pallas_call x1 -> x0, Pallas kernels: 5.16 us -> none  [shards(): pl.pallas_call(early_kernel, in_specs=[SMEM] + [VMEM] * 7, out_specs=(VME...]
    pallas_call x9 -> x10, Pallas kernels: 23.7 us -> 28.9 us  [call(): pl.pallas_call(kernel, in_specs=in_specs, out_specs=out_specs, out_shape=...]
    ppermute x1, waiting for transfers between devices: 1.74 us -> 6.81 us  [shards(): z_pair = lax.ppermute(p2, ('zl', 'c'), [(0, 3), (1, 2), (2, 1), (3, 0)])]
    ppermute x10 -> x9, waiting for transfers between devices: 20.2 us -> 15.8 us  [shift(): return lax.ppermute(value, axis, [(i, (i + by) % n) for i in range(n)])]
    ppermute x10 -> x9, starting transfers between devices: 21.1 us -> 18.7 us  [shift(): return lax.ppermute(value, axis, [(i, (i + by) % n) for i in range(n)])]
    ppermute x1, starting transfers between devices: 1.71 us -> 2.92 us  [shards(): z_pair = lax.ppermute(p2, ('zl', 'c'), [(0, 3), (1, 2), (2, 1), (3, 0)])]
  transfers between devices with their start and end apart: 23 -> 22, of which waited for: 11 -> 11; matrix products, arithmetic and copies ran while one was open for 0% -> 0% of each run, Pallas kernels for 15% -> 15%
where the time goes in v4:
time: 111 us
  starting transfers between devices  46.2 us (42%)
  waiting for transfers between devices  34.9 us (31%)
  Pallas kernels  28.9 us (26%)
    pallas_call x10, Pallas kernels, call(): pl.pallas_call(kernel, in_specs=in_specs, out_specs=out_specs, out_shape=...  28.9 us
    ppermute x9, starting transfers between devices, shift(): return lax.ppermute(value, axis, [(i, (i + by) % n) for i in range(n)])  18.7 us
    ppermute x9, waiting for transfers between devices, shift(): return lax.ppermute(value, axis, [(i, (i + by) % n) for i in range(n)])  15.8 us
    ppermute x3, starting transfers between devices, apart(): lax.ppermute(v, (axis, 'c'), [(i * 2 + e, (i + 1 - 2 * e) % 4 * 2 + e) fo...  12.3 us
    ppermute x9, starting transfers between devices, cross(): return lax.ppermute(v, ('y', 'x', 'c'), pairs)  12.2 us
    ppermute x3, waiting for transfers between devices, apart(): lax.ppermute(v, (axis, 'c'), [(i * 2 + e, (i + 1 - 2 * e) % 4 * 2 + e) fo...  9.52 us
    ppermute x1, waiting for transfers between devices, shards(): z_pair = lax.ppermute(p2, ('zl', 'c'), [(0, 3), (1, 2), (2, 1), (3, 0)])  6.81 us
    ppermute x1, starting transfers between devices, shards(): z_pair = lax.ppermute(p2, ('zl', 'c'), [(0, 3), (1, 2), (2, 1), (3, 0)])  2.92 us
  transfers between devices with their start and end apart: 22, of which 11 were waited for; matrix products, arithmetic and copies ran while one was open for 0% of the time, Pallas kernels for 15%

profile of v4, /device:TPU:1, one launch (start us, length us, event | category | flops | bytes accessed | tf_op | source)
XLA Modules:
  0.0 110.5 jit_solution(2304808109352943818)
XLA Ops:
  0.0 4.9 %shard_map.46 = (bf16[448,2048]{1,0:T(8,128)(2,1)}, bf16[464,512]{1,0:T(8,128)(2,1)}) custom-call(s32[1]{0:T(128)} %bitcast.6.idx_ref, f32[1,2048]{1,0:T(1,128)} %bitcast.14, bf16[224,2048]{1,0:T(8,128)(2,1)} %bitcast.12, bf16[224,2048]{1,0:T(8,128)(2,1)} %bitcast.13, bf16[2048,2048]{1,0:T(8,128)(2,1)} %h_ref.5), custom_call_target="tpu_custom_call" | custom-call | flops 939524096 | bytes 2097152 | tf_op jit(solution)/shard_map/pallas_call | solution.py:287
  4.9 3.7 %collective-permute-start.1 = (bf16[464,512]{1,0:T(8,128)(2,1)}, bf16[464,512]{1,0:T(8,128)(2,1)S(1)}, u32[]{:S(2)}, u32[]{:S(2)}) collective-permute-start(bf16[464,512]{1,0:T(8,128)(2,1)} %get-tuple-element.24), channel_id=1, source_target_pairs={{0,16},{8,24},{16,0},{24,8},{1,17},{9,25},{17,1},{25,9},{2,18},{10... | collective-permute-start | bytes 1425416 | tf_op jit(solution)/shard_map/ppermute | solution.py:18
  8.7 6.2 %shard_map.48 = (bf16[464,512]{1,0:T(8,128)(2,1)S(1)}, bf16[464,512]{1,0:T(8,128)(2,1)S(1)}) custom-call(s32[2]{0:T(128)S(1)} %pad_add_fusion.idx_ref, bf16[448,2048]{1,0:T(8,128)(2,1)} %get-tuple-element.22.w_ref, bf16[2048,2048]{1,0:T(8,128)(2,1)} %h_ref.5), custom_call_target="tpu_custom_call" | custom-call | flops 1879048192 | bytes 2097152 | tf_op jit(solution)/shard_map/pallas_call | solution.py:287
  15.3 2.4 %collective-permute-start.2 = (bf16[464,512]{1,0:T(8,128)(2,1)S(1)}, bf16[464,512]{1,0:T(8,128)(2,1)S(1)}, u32[]{:S(2)}, u32[]{:S(2)}) collective-permute-start(bf16[464,512]{1,0:T(8,128)(2,1)S(1)} %get-tuple-element.25), channel_id=1, source_target_pairs={{0,24},{8,0},{16,8},{24,16},{1,25},{9,1},{17,9},{25,17},{2,26},{10... | collective-permute-start | bytes 1425416 | tf_op jit(solution)/shard_map/ppermute | solution.py:18
  17.6 4.5 %shard_map.47.own_ref = f32[456,512]{1,0:T(8,128)S(1)} custom-call(s32[1]{0:T(128)} %bitcast.5.idx_ref, bf16[448,2048]{1,0:T(8,128)(2,1)} %get-tuple-element.22.w_ref, bf16[2048,2048]{1,0:T(8,128)(2,1)} %h_ref.5), custom_call_target="tpu_custom_call" | custom-call | flops 939524096 | bytes 2097152 | tf_op jit(solution)/shard_map/pallas_call | solution.py:287
  22.1 7.8 %collective-permute-done.p_ref = bf16[464,512]{1,0:T(8,128)(2,1)S(1)} collective-permute-done((bf16[464,512]{1,0:T(8,128)(2,1)S(1)}, bf16[464,512]{1,0:T(8,128)(2,1)S(1)}, u32[]{:S(2)}, u32[]{:S(2)}) %collective-permute-start) | collective-permute-done | bytes 475168 | tf_op jit(solution)/shard_map/ppermute | solution.py:18
  29.9 1.1 %shard_map.49.k_ref = bf16[224,512]{1,0:T(8,128)(2,1)S(1)} custom-call(f32[456,512]{1,0:T(8,128)S(1)} %shard_map.47.own_ref, bf16[464,512]{1,0:T(8,128)(2,1)S(1)} %collective-permute-done.p_ref, bf16[464,512]{1,0:T(8,128)(2,1)S(1)} %collective-permute-done.1.q_ref, bf16[464,512]{1,0:T(8,128)(2,1)S(1)} %collective-permute-done.2.r_ref), custom_call_target="tpu_custom_call" | custom-call | flops 939524096 | bytes 2097152 | tf_op jit(solution)/shard_map/pallas_call | solution.py:287
  31.1 1.9 %collective-permute-start.4 = (bf16[224,512]{1,0:T(8,128)(2,1)S(1)}, bf16[224,512]{1,0:T(8,128)(2,1)S(1)}, u32[]{:S(2)}, u32[]{:S(2)}) collective-permute-start(bf16[224,512]{1,0:T(8,128)(2,1)S(1)} %shard_map.49.k_ref), channel_id=1, source_target_pairs={{0,128},{128,0},{1,129},{129,1},{2,130},{130,2},{3,131},{131,3},{4... | collective-permute-start | bytes 688136 | tf_op jit(solution)/shard_map/ppermute | solution.py:18
  32.9 1.3 %collective-permute-start.3 = (bf16[224,512]{1,0:T(8,128)(2,1)S(1)}, bf16[224,512]{1,0:T(8,128)(2,1)S(1)}, u32[]{:S(2)}, u32[]{:S(2)}) collective-permute-start(bf16[224,512]{1,0:T(8,128)(2,1)S(1)} %shard_map.49.k_ref), channel_id=1, source_target_pairs={{0,1},{1,0},{2,3},{3,2},{4,5},{5,4},{6,7},{7,6},{8,9},{9,8},{10,11... | collective-permute-start | bytes 688136 | tf_op jit(solution)/shard_map/ppermute | solution.py:18
  34.3 3.5 %collective-permute-done.4.p_ref = bf16[224,512]{1,0:T(8,128)(2,1)S(1)} collective-permute-done((bf16[224,512]{1,0:T(8,128)(2,1)S(1)}, bf16[224,512]{1,0:T(8,128)(2,1)S(1)}, u32[]{:S(2)}, u32[]{:S(2)}) %collective-permute-start.4) | collective-permute-done | bytes 229408 | tf_op jit(solution)/shard_map/ppermute | solution.py:18
  37.7 1.8 %collective-permute-start.5 = (bf16[224,512]{1,0:T(8,128)(2,1)S(1)}, bf16[224,512]{1,0:T(8,128)(2,1)S(1)}, u32[]{:S(2)}, u32[]{:S(2)}) collective-permute-start(bf16[224,512]{1,0:T(8,128)(2,1)S(1)} %collective-permute-done.4.p_ref), channel_id=1, source_target_pairs={{0,1},{1,0},{2,3},{3,2},{4,5},{5,4},{6,7},{7,6},{8,9},{9,8},{10,11... | collective-permute-start | bytes 688136 | tf_op jit(solution)/shard_map/ppermute | solution.py:18
  39.6 1.0 collective-permute-done.5.p_other
  41.2 3.3 %collective-permute-start.8 = (bf16[448,512]{1,0:T(8,128)(2,1)S(1)}, bf16[448,512]{1,0:T(8,128)(2,1)S(1)}, u32[]{:S(2)}, u32[]{:S(2)}) collective-permute-start(bf16[448,512]{1,0:T(8,128)(2,1)S(1)} %shard_map.50.refs_0_), channel_id=1, source_target_pairs={{0,64},{1,17},{8,72},{9,25},{16,80},{17,1},{24,88},{25,9},{32,96},... | collective-permute-start | bytes 1376264 | tf_op jit(solution)/shard_map/ppermute | solution.py:351
  44.5 2.7 %collective-permute-start.6 = (bf16[448,512]{1,0:T(8,128)(2,1)S(1)}, bf16[448,512]{1,0:T(8,128)(2,1)S(1)}, u32[]{:S(2)}, u32[]{:S(2)}) collective-permute-start(bf16[448,512]{1,0:T(8,128)(2,1)S(1)} %shard_map.50.refs_0_), channel_id=1, source_target_pairs={{0,96},{1,25},{8,104},{9,1},{16,112},{17,9},{24,120},{25,17},{32,0... | collective-permute-start | bytes 1376264 | tf_op jit(solution)/shard_map/ppermute | solution.py:351
  47.2 5.9 %collective-permute-start.11 = (bf16[448,512]{1,0:T(8,128)(2,1)S(1)}, bf16[448,512]{1,0:T(8,128)(2,1)S(1)}, u32[]{:S(2)}, u32[]{:S(2)}) collective-permute-start(bf16[448,512]{1,0:T(8,128)(2,1)S(1)} %pad_maximum_fusion.1), channel_id=1, source_target_pairs={{0,2},{1,7},{2,4},{3,1},{4,6},{5,3},{6,0},{7,5},{8,10},{9,15},{10,... | collective-permute-start | bytes 1376264 | tf_op jit(solution)/shard_map/ppermute | solution.py:354
  53.2 2.4 %collective-permute-done.7.refs_2_ = bf16[448,512]{1,0:T(8,128)(2,1)S(1)} collective-permute-done((bf16[448,512]{1,0:T(8,128)(2,1)S(1)}, bf16[448,512]{1,0:T(8,128)(2,1)S(1)}, u32[]{:S(2)}, u32[]{:S(2)}) %collective-permute-start.7) | collective-permute-done | bytes 458784 | tf_op jit(solution)/shard_map/ppermute | solution.py:351
  55.7 1.4 %collective-permute-start.10 = (bf16[1792,512]{1,0:T(8,128)(2,1)S(1)}, bf16[1792,512]{1,0:T(8,128)(2,1)S(1)}, u32[]{:S(2)}, u32[]{:S(2)}) collective-permute-start(bf16[1792,512]{1,0:T(8,128)(2,1)S(1)} %shard_map.51.q_ref), channel_id=1, source_target_pairs={{0,8},{1,33},{8,16},{9,41},{16,24},{17,49},{24,0},{25,57},{32,40},... | collective-permute-start | bytes 5505032 | tf_op jit(solution)/shard_map/ppermute | solution.py:351
  57.1 1.5 %collective-permute-start.9 = (bf16[1792,512]{1,0:T(8,128)(2,1)S(1)}, bf16[1792,512]{1,0:T(8,128)(2,1)S(1)}, u32[]{:S(2)}, u32[]{:S(2)}) collective-permute-start(bf16[1792,512]{1,0:T(8,128)(2,1)S(1)} %shard_map.51.q_ref), channel_id=1, source_target_pairs={{0,24},{1,97},{8,0},{9,105},{16,8},{17,113},{24,16},{25,121},{32,5... | collective-permute-start | bytes 5505032 | tf_op jit(solution)/shard_map/ppermute | solution.py:351
  58.6 4.9 %collective-permute-done.11.near = bf16[448,512]{1,0:T(8,128)(2,1)S(1)} collective-permute-done((bf16[448,512]{1,0:T(8,128)(2,1)S(1)}, bf16[448,512]{1,0:T(8,128)(2,1)S(1)}, u32[]{:S(2)}, u32[]{:S(2)}) %collective-permute-start.11) | collective-permute-done | bytes 458784 | tf_op jit(solution)/shard_map/ppermute | solution.py:354
  63.5 4.1 %collective-permute-start.12 = (bf16[224,512]{1,0:T(8,128)(2,1)S(1)}, bf16[224,512]{1,0:T(8,128)(2,1)S(1)}, u32[]{:S(2)}, u32[]{:S(2)}) collective-permute-start(bf16[224,512]{1,0:T(8,128)(2,1)S(1)} %slice.4), channel_id=1, source_target_pairs={{0,2},{1,7},{2,4},{3,1},{4,6},{5,3},{6,0},{7,5},{8,10},{9,15},{10,... | collective-permute-start | bytes 688136 | tf_op jit(solution)/shard_map/ppermute | solution.py:354
  67.6 3.8 %collective-permute-done.12.far = bf16[224,512]{1,0:T(8,128)(2,1)S(1)} collective-permute-done((bf16[224,512]{1,0:T(8,128)(2,1)S(1)}, bf16[224,512]{1,0:T(8,128)(2,1)S(1)}, u32[]{:S(2)}, u32[]{:S(2)}) %collective-permute-start.12) | collective-permute-done | bytes 229408 | tf_op jit(solution)/shard_map/ppermute | solution.py:354
  71.4 2.2 %collective-permute-start.13 = (bf16[672,512]{1,0:T(8,128)(2,1)S(1)}, bf16[672,512]{1,0:T(8,128)(2,1)S(1)}, u32[]{:S(2)}, u32[]{:S(2)}) collective-permute-start(bf16[672,512]{1,0:T(8,128)(2,1)S(1)} %pad_maximum_fusion), channel_id=1, source_target_pairs={{0,1},{1,0},{2,3},{3,2},{4,5},{5,4},{6,7},{7,6},{8,9},{9,8},{10,11... | collective-permute-start | bytes 2064392 | tf_op jit(solution)/shard_map/ppermute | solution.py:18
  73.6 2.9 %collective-permute-start.16 = (bf16[448,512]{1,0:T(8,128)(2,1)S(1)}, bf16[448,512]{1,0:T(8,128)(2,1)S(1)}, u32[]{:S(2)}, u32[]{:S(2)}) collective-permute-start(bf16[448,512]{1,0:T(8,128)(2,1)S(1)} %collective-permute-done.8.refs_3_), channel_id=1, source_target_pairs={{0,129},{1,128},{128,1},{129,0},{2,131},{3,130},{130,3},{131,2},{4... | collective-permute-start | bytes 1376264 | tf_op jit(solution)/shard_map/ppermute | solution.py:367
  77.3 2.3 %collective-permute-start.14 = (bf16[448,512]{1,0:T(8,128)(2,1)S(1)}, bf16[448,512]{1,0:T(8,128)(2,1)S(1)}, u32[]{:S(2)}, u32[]{:S(2)}) collective-permute-start(bf16[448,512]{1,0:T(8,128)(2,1)S(1)} %get-tuple-element.27), channel_id=1, source_target_pairs={{0,8},{1,25},{8,16},{9,1},{16,24},{17,9},{24,0},{25,17},{2,10},{3,... | collective-permute-start | bytes 1376264 | tf_op jit(solution)/shard_map/ppermute | solution.py:354
  79.6 1.2 %collective-permute-start.15 = (bf16[224,512]{1,0:T(8,128)(2,1)S(1)}, bf16[224,512]{1,0:T(8,128)(2,1)S(1)}, u32[]{:S(2)}, u32[]{:S(2)}) collective-permute-start(bf16[224,512]{1,0:T(8,128)(2,1)S(1)} %get-tuple-element.28), channel_id=1, source_target_pairs={{0,16},{8,24},{16,0},{24,8},{1,17},{9,25},{17,1},{25,9},{2,18},{10... | collective-permute-start | bytes 688136 | tf_op jit(solution)/shard_map/ppermute | solution.py:18
  80.8 6.8 %collective-permute-done.16.z_ref = bf16[448,512]{1,0:T(8,128)(2,1)S(1)} collective-permute-done((bf16[448,512]{1,0:T(8,128)(2,1)S(1)}, bf16[448,512]{1,0:T(8,128)(2,1)S(1)}, u32[]{:S(2)}, u32[]{:S(2)}) %collective-permute-start.16) | collective-permute-done | bytes 458784 | tf_op jit(solution)/shard_map/ppermute | solution.py:367
  89.3 1.2 %shard_map.53 = (bf16[896,2048]{1,0:T(8,128)(2,1)S(1)}, bf16[448,512]{1,0:T(8,128)(2,1)S(1)}, bf16[224,512]{1,0:T(8,128)(2,1)S(1)}, bf16[224,512]{1,0:T(8,128)(2...) custom-call(s32[5]{0:T(128)S(1)} %stack.38.idx_ref, bf16[1792,512]{1,0:T(8,128)(2,1)S(1)} %shard_map.51.q_ref, ...), custom_call_target="tpu_custom_call" | custom-call | flops 234881024 | bytes 2097152 | tf_op jit(solution)/shard_map/pallas_call | solution.py:287
  90.5 4.0 %collective-permute-start.17 = (bf16[3584,512]{1,0:T(8,128)(2,1)S(1)}, bf16[3584,512]{1,0:T(8,128)(2,1)S(1)}, u32[]{:S(2)}, u32[]{:S(2)}) collective-permute-start(bf16[3584,512]{1,0:T(8,128)(2,1)S(1)} %get-tuple-element.30), channel_id=1, source_target_pairs={{0,1},{1,0},{2,3},{3,2},{4,5},{5,4},{6,7},{7,6},{8,9},{9,8},{10,11... | collective-permute-start | bytes 11010056 | tf_op jit(solution)/shard_map/ppermute | solution.py:18
  94.6 2.4 %collective-permute-start.21 = (bf16[448,512]{1,0:T(8,128)(2,1)S(1)}, bf16[448,512]{1,0:T(8,128)(2,1)S(1)}, u32[]{:S(2)}, u32[]{:S(2)}) collective-permute-start(bf16[448,512]{1,0:T(8,128)(2,1)S(1)} %get-tuple-element.38), channel_id=1, source_target_pairs={{0,25},{1,96},{8,1},{9,104},{16,9},{17,112},{24,17},{25,120},{32,5... | collective-permute-start | bytes 1376264 | tf_op jit(solution)/shard_map/ppermute | solution.py:351
  97.8 2.7 %collective-permute-done.17.got = bf16[3584,512]{1,0:T(8,128)(2,1)S(1)} collective-permute-done((bf16[3584,512]{1,0:T(8,128)(2,1)S(1)}, bf16[3584,512]{1,0:T(8,128)(2,1)S(1)}, u32[]{:S(2)}, u32[]{:S(2)}) %collective-permute-start.17) | collective-permute-done | bytes 3670048 | tf_op jit(solution)/shard_map/ppermute | solution.py:18
  100.5 5.1 %shard_map.54 = (bf16[448,2048]{1,0:T(8,128)(2,1)S(1)}, f32[448,896]{1,0:T(8,128)S(1)}, f32[448,896]{1,0:T(8,128)S(1)}) custom-call(s32[5]{0:T(128)S(1)} %stack.38.idx_ref, bf16[896,2048]{1,0:T(8,128)(2,1)S(1)} %get-tuple-element.29.mine, bf16[3584,512]{1,0:T(8,128)(2,1)S(1)} %collective-permute-done.17.got, bf16[448,512]{1,0:T(8,128)(2,1)S(1)} %get-tuple-element.31.row_own, ...), custom_call_target="tpu_custom_call" | custom-call | flops 234881024 | bytes 2097152 | tf_op jit(solution)/shard_map/pallas_call | solution.py:287
  106.0 4.4 %shard_map.55 = f32[448,1,1792]{2,1,0:T(1,128)} custom-call(s32[5]{0:T(128)S(1)} %stack.38.idx_ref, bf16[448,2048]{1,0:T(8,128)(2,1)S(1)} %get-tuple-element.32.r_ref, f32[448,896]{1,0:T(8,128)S(1)} %get-tuple-element.33.acc_mine, f32[448,896]{1,0:T(8,128)S(1)} %get-tuple-element.34.acc_theirs, bf16[448,512]{1,0:T(8,128)(2,1)S(1)} %collective-permute-done.18.d_a, ...), custom_call_target="tpu_custom_call" | custom-call | flops 939524096 | bytes 2097152 | tf_op jit(solution)/shard_map/pallas_call | solution.py:287
  (27 shorter events, 5.0 us)
Async XLA Ops:
  4.9 17.2 %collective-permute-start.1 = (bf16[464,512]{1,0:T(8,128)(2,1)}, bf16[464,512]{1,0:T(8,128)(2,1)S(1)}, u32[]{:S(2)}, u32[]{:S(2)}) collective-permute-start(bf16[464,512]{1,0:T(8,128)(2,1)} %get-tuple-element.24), channel_id=1, source_target_pairs={{0,16},{8,24},{16,0},{24,8},{1,17},{9,25},{17,1},{25,9},{2,18},{10... | collective-permute-start | bytes 1425416 | tf_op jit(solution)/shard_map/ppermute | solution.py:18
  14.9 15.0 %collective-permute-start = (bf16[464,512]{1,0:T(8,128)(2,1)S(1)}, bf16[464,512]{1,0:T(8,128)(2,1)S(1)}, u32[]{:S(2)}, u32[]{:S(2)}) collective-permute-start(bf16[464,512]{1,0:T(8,128)(2,1)S(1)} %get-tuple-element.23), channel_id=1, source_target_pairs={{0,8},{8,16},{16,24},{24,0},{1,9},{9,17},{17,25},{25,1},{2,10},{10... | collective-permute-start | bytes 1425416 | tf_op jit(solution)/shard_map/ppermute | solution.py:18
  15.3 14.7 %collective-permute-start.2 = (bf16[464,512]{1,0:T(8,128)(2,1)S(1)}, bf16[464,512]{1,0:T(8,128)(2,1)S(1)}, u32[]{:S(2)}, u32[]{:S(2)}) collective-permute-start(bf16[464,512]{1,0:T(8,128)(2,1)S(1)} %get-tuple-element.25), channel_id=1, source_target_pairs={{0,24},{8,0},{16,8},{24,16},{1,25},{9,1},{17,9},{25,17},{2,26},{10... | collective-permute-start | bytes 1425416 | tf_op jit(solution)/shard_map/ppermute | solution.py:18
  31.1 6.7 %collective-permute-start.4 = (bf16[224,512]{1,0:T(8,128)(2,1)S(1)}, bf16[224,512]{1,0:T(8,128)(2,1)S(1)}, u32[]{:S(2)}, u32[]{:S(2)}) collective-permute-start(bf16[224,512]{1,0:T(8,128)(2,1)S(1)} %shard_map.49.k_ref), channel_id=1, source_target_pairs={{0,128},{128,0},{1,129},{129,1},{2,130},{130,2},{3,131},{131,3},{4... | collective-permute-start | bytes 688136 | tf_op jit(solution)/shard_map/ppermute | solution.py:18
  32.9 6.6 %collective-permute-start.3 = (bf16[224,512]{1,0:T(8,128)(2,1)S(1)}, bf16[224,512]{1,0:T(8,128)(2,1)S(1)}, u32[]{:S(2)}, u32[]{:S(2)}) collective-permute-start(bf16[224,512]{1,0:T(8,128)(2,1)S(1)} %shard_map.49.k_ref), channel_id=1, source_target_pairs={{0,1},{1,0},{2,3},{3,2},{4,5},{5,4},{6,7},{7,6},{8,9},{9,8},{10,11... | collective-permute-start | bytes 688136 | tf_op jit(solution)/shard_map/ppermute | solution.py:18
  37.7 2.9 %collective-permute-start.5 = (bf16[224,512]{1,0:T(8,128)(2,1)S(1)}, bf16[224,512]{1,0:T(8,128)(2,1)S(1)}, u32[]{:S(2)}, u32[]{:S(2)}) collective-permute-start(bf16[224,512]{1,0:T(8,128)(2,1)S(1)} %collective-permute-done.4.p_ref), channel_id=1, source_target_pairs={{0,1},{1,0},{2,3},{3,2},{4,5},{5,4},{6,7},{7,6},{8,9},{9,8},{10,11... | collective-permute-start | bytes 688136 | tf_op jit(solution)/shard_map/ppermute | solution.py:18
  41.2 11.9 %collective-permute-start.8 = (bf16[448,512]{1,0:T(8,128)(2,1)S(1)}, bf16[448,512]{1,0:T(8,128)(2,1)S(1)}, u32[]{:S(2)}, u32[]{:S(2)}) collective-permute-start(bf16[448,512]{1,0:T(8,128)(2,1)S(1)} %shard_map.50.refs_0_), channel_id=1, source_target_pairs={{0,64},{1,17},{8,72},{9,25},{16,80},{17,1},{24,88},{25,9},{32,96},... | collective-permute-start | bytes 1376264 | tf_op jit(solution)/shard_map/ppermute | solution.py:351
  44.5 11.1 %collective-permute-start.7 = (bf16[448,512]{1,0:T(8,128)(2,1)S(1)}, bf16[448,512]{1,0:T(8,128)(2,1)S(1)}, u32[]{:S(2)}, u32[]{:S(2)}) collective-permute-start(bf16[448,512]{1,0:T(8,128)(2,1)S(1)} %shard_map.50.refs_0_), channel_id=1, source_target_pairs={{0,32},{1,9},{8,40},{9,17},{16,48},{17,25},{24,56},{25,1},{32,64},... | collective-permute-start | bytes 1376264 | tf_op jit(solution)/shard_map/ppermute | solution.py:351
  44.5 11.1 %collective-permute-start.6 = (bf16[448,512]{1,0:T(8,128)(2,1)S(1)}, bf16[448,512]{1,0:T(8,128)(2,1)S(1)}, u32[]{:S(2)}, u32[]{:S(2)}) collective-permute-start(bf16[448,512]{1,0:T(8,128)(2,1)S(1)} %shard_map.50.refs_0_), channel_id=1, source_target_pairs={{0,96},{1,25},{8,104},{9,1},{16,112},{17,9},{24,120},{25,17},{32,0... | collective-permute-start | bytes 1376264 | tf_op jit(solution)/shard_map/ppermute | solution.py:351
  47.2 16.3 %collective-permute-start.11 = (bf16[448,512]{1,0:T(8,128)(2,1)S(1)}, bf16[448,512]{1,0:T(8,128)(2,1)S(1)}, u32[]{:S(2)}, u32[]{:S(2)}) collective-permute-start(bf16[448,512]{1,0:T(8,128)(2,1)S(1)} %pad_maximum_fusion.1), channel_id=1, source_target_pairs={{0,2},{1,7},{2,4},{3,1},{4,6},{5,3},{6,0},{7,5},{8,10},{9,15},{10,... | collective-permute-start | bytes 1376264 | tf_op jit(solution)/shard_map/ppermute | solution.py:354
  55.7 33.6 %collective-permute-start.10 = (bf16[1792,512]{1,0:T(8,128)(2,1)S(1)}, bf16[1792,512]{1,0:T(8,128)(2,1)S(1)}, u32[]{:S(2)}, u32[]{:S(2)}) collective-permute-start(bf16[1792,512]{1,0:T(8,128)(2,1)S(1)} %shard_map.51.q_ref), channel_id=1, source_target_pairs={{0,8},{1,33},{8,16},{9,41},{16,24},{17,49},{24,0},{25,57},{32,40},... | collective-permute-start | bytes 5505032 | tf_op jit(solution)/shard_map/ppermute | solution.py:351
  57.1 32.2 %collective-permute-start.9 = (bf16[1792,512]{1,0:T(8,128)(2,1)S(1)}, bf16[1792,512]{1,0:T(8,128)(2,1)S(1)}, u32[]{:S(2)}, u32[]{:S(2)}) collective-permute-start(bf16[1792,512]{1,0:T(8,128)(2,1)S(1)} %shard_map.51.q_ref), channel_id=1, source_target_pairs={{0,24},{1,97},{8,0},{9,105},{16,8},{17,113},{24,16},{25,121},{32,5... | collective-permute-start | bytes 5505032 | tf_op jit(solution)/shard_map/ppermute | solution.py:351
  63.5 7.9 %collective-permute-start.12 = (bf16[224,512]{1,0:T(8,128)(2,1)S(1)}, bf16[224,512]{1,0:T(8,128)(2,1)S(1)}, u32[]{:S(2)}, u32[]{:S(2)}) collective-permute-start(bf16[224,512]{1,0:T(8,128)(2,1)S(1)} %slice.4), channel_id=1, source_target_pairs={{0,2},{1,7},{2,4},{3,1},{4,6},{5,3},{6,0},{7,5},{8,10},{9,15},{10,... | collective-permute-start | bytes 688136 | tf_op jit(solution)/shard_map/ppermute | solution.py:354
  71.4 5.1 %collective-permute-start.13 = (bf16[672,512]{1,0:T(8,128)(2,1)S(1)}, bf16[672,512]{1,0:T(8,128)(2,1)S(1)}, u32[]{:S(2)}, u32[]{:S(2)}) collective-permute-start(bf16[672,512]{1,0:T(8,128)(2,1)S(1)} %pad_maximum_fusion), channel_id=1, source_target_pairs={{0,1},{1,0},{2,3},{3,2},{4,5},{5,4},{6,7},{7,6},{8,9},{9,8},{10,11... | collective-permute-start | bytes 2064392 | tf_op jit(solution)/shard_map/ppermute | solution.py:18
  73.6 14.0 %collective-permute-start.16 = (bf16[448,512]{1,0:T(8,128)(2,1)S(1)}, bf16[448,512]{1,0:T(8,128)(2,1)S(1)}, u32[]{:S(2)}, u32[]{:S(2)}) collective-permute-start(bf16[448,512]{1,0:T(8,128)(2,1)S(1)} %collective-permute-done.8.refs_3_), channel_id=1, source_target_pairs={{0,129},{1,128},{128,1},{129,0},{2,131},{3,130},{130,3},{131,2},{4... | collective-permute-start | bytes 1376264 | tf_op jit(solution)/shard_map/ppermute | solution.py:367
  77.3 12.0 %collective-permute-start.14 = (bf16[448,512]{1,0:T(8,128)(2,1)S(1)}, bf16[448,512]{1,0:T(8,128)(2,1)S(1)}, u32[]{:S(2)}, u32[]{:S(2)}) collective-permute-start(bf16[448,512]{1,0:T(8,128)(2,1)S(1)} %get-tuple-element.27), channel_id=1, source_target_pairs={{0,8},{1,25},{8,16},{9,1},{16,24},{17,9},{24,0},{25,17},{2,10},{3,... | collective-permute-start | bytes 1376264 | tf_op jit(solution)/shard_map/ppermute | solution.py:354
  79.6 8.8 %collective-permute-start.15 = (bf16[224,512]{1,0:T(8,128)(2,1)S(1)}, bf16[224,512]{1,0:T(8,128)(2,1)S(1)}, u32[]{:S(2)}, u32[]{:S(2)}) collective-permute-start(bf16[224,512]{1,0:T(8,128)(2,1)S(1)} %get-tuple-element.28), channel_id=1, source_target_pairs={{0,16},{8,24},{16,0},{24,8},{1,17},{9,25},{17,1},{25,9},{2,18},{10... | collective-permute-start | bytes 688136 | tf_op jit(solution)/shard_map/ppermute | solution.py:18
  90.5 10.0 %collective-permute-start.17 = (bf16[3584,512]{1,0:T(8,128)(2,1)S(1)}, bf16[3584,512]{1,0:T(8,128)(2,1)S(1)}, u32[]{:S(2)}, u32[]{:S(2)}) collective-permute-start(bf16[3584,512]{1,0:T(8,128)(2,1)S(1)} %get-tuple-element.30), channel_id=1, source_target_pairs={{0,1},{1,0},{2,3},{3,2},{4,5},{5,4},{6,7},{7,6},{8,9},{9,8},{10,11... | collective-permute-start | bytes 11010056 | tf_op jit(solution)/shard_map/ppermute | solution.py:18
  94.4 11.6 %collective-permute-start.18 = (bf16[448,512]{1,0:T(8,128)(2,1)S(1)}, bf16[448,512]{1,0:T(8,128)(2,1)S(1)}, u32[]{:S(2)}, u32[]{:S(2)}) collective-permute-start(bf16[448,512]{1,0:T(8,128)(2,1)S(1)} %get-tuple-element.35), channel_id=1, source_target_pairs={{0,8},{1,33},{8,16},{9,41},{16,24},{17,49},{24,0},{25,57},{32,40},... | collective-permute-start | bytes 1376264 | tf_op jit(solution)/shard_map/ppermute | solution.py:351
  94.6 11.4 %collective-permute-start.21 = (bf16[448,512]{1,0:T(8,128)(2,1)S(1)}, bf16[448,512]{1,0:T(8,128)(2,1)S(1)}, u32[]{:S(2)}, u32[]{:S(2)}) collective-permute-start(bf16[448,512]{1,0:T(8,128)(2,1)S(1)} %get-tuple-element.38), channel_id=1, source_target_pairs={{0,25},{1,96},{8,1},{9,104},{16,9},{17,112},{24,17},{25,120},{32,5... | collective-permute-start | bytes 1376264 | tf_op jit(solution)/shard_map/ppermute | solution.py:351
  97.0 8.6 %collective-permute-start.19 = (bf16[224,512]{1,0:T(8,128)(2,1)S(1)}, bf16[224,512]{1,0:T(8,128)(2,1)S(1)}, u32[]{:S(2)}, u32[]{:S(2)}) collective-permute-start(bf16[224,512]{1,0:T(8,128)(2,1)S(1)} %get-tuple-element.36), channel_id=1, source_target_pairs={{0,24},{1,97},{8,0},{9,105},{16,8},{17,113},{24,16},{25,121},{32,5... | collective-permute-start | bytes 688136 | tf_op jit(solution)/shard_map/ppermute | solution.py:351
  97.1 8.9 %collective-permute-start.20 = (bf16[224,512]{1,0:T(8,128)(2,1)S(1)}, bf16[224,512]{1,0:T(8,128)(2,1)S(1)}, u32[]{:S(2)}, u32[]{:S(2)}) collective-permute-start(bf16[224,512]{1,0:T(8,128)(2,1)S(1)} %get-tuple-element.37), channel_id=1, source_target_pairs={{0,9},{1,32},{8,17},{9,40},{16,25},{17,48},{24,1},{25,56},{32,41},... | collective-permute-start | bytes 688136 | tf_op jit(solution)/shard_map/ppermute | solution.py:351
